TPU v7x, 128 devices: a whole 4x4x4 slice. The times are simulated.
128 devices in a mesh: sec: 2 (over core), dev: 64 (over x, y, z).
Axes of the slice: x: 4, y: 4, z: 4, core: 2. Of those that a mesh axis runs over, the one named last changes fastest.
Arguments:
- resid: bfloat16 [1024, 7168], P(('sec', 'dev')), may hold values from -6 to 6
- ffn_gain: float32 [7168], replicated, may hold values from 0.25 to 1.75
- expert_ids: int32 [1024, 8], P(('sec', 'dev')), may hold values from 0 to 15, all different within a row; in each aligned block of 8 rows (0 to 7, 8 to 15, ...) at most 6 rows name the same one
- gate_weights: float32 [1024, 8], P(('sec', 'dev')), may hold values from 0.1 to 0.6
- w_gate: bfloat16 [7168, 32768], P(None, ('sec', 'dev')), may hold values from -0.0625 to 0.0625
- w_up: bfloat16 [7168, 32768], P(None, ('sec', 'dev')), may hold values from -0.0625 to 0.0625
- w_down: bfloat16 [32768, 7168], P(('sec', 'dev')), may hold values from -0.125 to 0.125
- attn_gain: float32 [7168], replicated, may hold values from 0.25 to 1.75
- w_kv: bfloat16 [7168, 576], replicated, may hold values from -0.0625 to 0.0625
- kv_gain: float32 [512], replicated, may hold values from 0.25 to 1.75
- cache: bfloat16 [1024, 256, 576], P(('sec', 'dev')), may hold values from -6 to 6
- lengths: int32 [1024], P(('sec', 'dev')), may hold values from 1 to 256, as said below
- queries: bfloat16 [1024, 128, 576], P(('sec', 'dev')), may hold values from -150 to 150
Outputs:
- hidden: bfloat16 [1024, 7168], P(('sec', 'dev'))
- new_entry: bfloat16 [1024, 576], P(('sec', 'dev'))
- attn_out: bfloat16 [1024, 128, 512], P(('sec', 'dev'))
Inputs may be any that keep to these rules, and one draw needn't show every extreme that they name: `expert_ids`: the 8 ids of a token differ; among the 8 tokens of one device at most 6 name the same expert, and in every draw some expert is named by exactly 6 of them. `lengths`: some request in every draw has all 256 positions cached.
All inputs are finite; a program needn't handle non-finite values.
Results may differ from a plain program's by a relative error of at most 0.011.
Values may be sent and summed in bfloat16 or wider, within the bound.
No kernel may reach another device: no remote copies, remote signals or barrier semaphores. Data moves between devices by JAX's collectives and lax.ppermute only.
A program may use at most 192 MiB of HBM per device.

v0:
```python
import functools

import jax
import jax.numpy as jnp
from jax import lax
from jax.experimental import pallas as pl
from jax.experimental.pallas import tpu as pltpu
from jax.sharding import PartitionSpec as P

KVL = 512
EXPERTS = 16
AXES = ("sec", "dev")
SIDE = 4
STRIDE = {"x": 16, "y": 4, "z": 1}
ORDER = (("x", "y", "z"), ("y", "z", "x"))
LANES = 128


norm_eps = 1e-06
SCORE_SCALE = 0.0721687836


def rms_scale(values, gain_vec):
    values = values.astype(jnp.float32)
    return (
        values * lax.rsqrt(jnp.mean(values * values, axis=-1, keepdims=True) + norm_eps) * gain_vec
    )


def rotate_half(rotary, positions):
    half_dim = rotary.shape[-1] // 2
    inv_freq = jnp.exp(
        -jnp.log(10000.0) * jnp.arange(half_dim).astype(jnp.float32) * 2.0 / rotary.shape[-1]
    )
    angles = positions.astype(jnp.float32)[:, None] * inv_freq[None, :]
    lower_half = rotary[:, :half_dim]
    upper_half = rotary[:, half_dim:]
    cosine = jnp.cos(angles)
    sine_val = jnp.sin(angles)
    return jnp.concatenate(
        [lower_half * cosine - upper_half * sine_val, upper_half * cosine + lower_half * sine_val],
        axis=-1,
    )


def shift(values, phase, amount):
    pairs = []
    for sec in range(2):
        stride = STRIDE[ORDER[sec][phase]]
        for dev in range(SIDE**3):
            place = dev // stride % SIDE
            there = dev + ((place + amount) % SIDE - place) * stride
            pairs.append((sec * SIDE**3 + dev, sec * SIDE**3 + there))
    return lax.ppermute(values, AXES, pairs)


def swap_cores(values):
    return lax.ppermute(values, AXES, [(i, (i + SIDE**3) % (2 * SIDE**3)) for i in range(2 * SIDE**3)])


def after(values, *earlier):
    return lax.optimization_barrier((values, *earlier))[0]


def join_body(count, *refs):
    ins, outs, sems = refs[:SIDE], refs[SIDE : SIDE + count], refs[-1]
    each = SIDE // count
    copies = []
    for back in range(SIDE):
        rows = ins[back].shape[0]
        copies.append(
            pltpu.make_async_copy(
                ins[back],
                outs[back // each].at[pl.ds(back % each * rows, rows)],
                sems.at[back],
            )
        )
    for copy in copies:
        copy.start()
    for copy in copies:
        copy.wait()


def join(blocks, count):
    rows, *rest = blocks[0].shape
    hbm = pl.BlockSpec(memory_space=pl.ANY)
    return pl.pallas_call(
        functools.partial(join_body, count),
        out_shape=[jax.ShapeDtypeStruct((SIDE // count * rows, *rest), blocks[0].dtype)] * count,
        in_specs=[hbm] * SIDE,
        out_specs=[hbm] * count,
        scratch_shapes=[pltpu.SemaphoreType.DMA((SIDE,))],
        compiler_params=pltpu.CompilerParams(vmem_limit_bytes=1 << 20),
        name="join",
    )(*blocks)


def act_body(info_ref, *refs):
    rows, weights, out_ref = refs[:SIDE], refs[SIDE : 2 * SIDE], refs[2 * SIDE]
    depth, wide = weights[0].shape
    held = jnp.concatenate([part[:, depth:] for part in rows], axis=0).astype(jnp.float32)
    lane = lax.broadcasted_iota(jnp.int32, (1, LANES), 1)

    def product(which):
        left = jnp.concatenate([part[:, :depth] for part in rows], axis=0)
        return jnp.dot(left, weights[which][...], preferred_element_type=jnp.float32)

    for which in range(2):
        expert = info_ref[which]
        hit = (lane == expert) | (lane == expert + EXPERTS) | (lane == expert + 2 * EXPERTS)
        weight = jnp.sum(jnp.where(hit, held, 0.0), axis=1, keepdims=True)
        gate = product(which)
        up = product(2 + which)
        act = gate / (1.0 + jnp.exp(-gate)) * up * weight
        out_ref[:, which * wide : (which + 1) * wide] = act.astype(jnp.bfloat16)


def expert_acts(info, rows, weights):
    tokens = SIDE * rows[0].shape[0]
    depth, wide = weights[0].shape
    vmem = pl.BlockSpec(memory_space=pltpu.VMEM)
    return pl.pallas_call(
        act_body,
        out_shape=jax.ShapeDtypeStruct((tokens, 2 * wide), jnp.bfloat16),
        in_specs=[pl.BlockSpec(memory_space=pltpu.SMEM)] + [vmem] * (2 * SIDE),
        out_specs=vmem,
        compiler_params=pltpu.CompilerParams(vmem_limit_bytes=30 << 20),
        cost_estimate=pl.CostEstimate(
            flops=8 * tokens * depth * wide, bytes_accessed=1 << 20, transcendentals=0
        ),
        name="expert_acts",
    )(info, *rows, *weights)


def down_body(acts_ref, mine_ref, other_ref, *outs):
    wide = mine_ref.shape[0]
    group = acts_ref.shape[0] // SIDE
    step = 2 * LANES
    for low in range(0, mine_ref.shape[1], step):
        high = low + step
        part = jnp.dot(
            acts_ref[:, :wide], mine_ref[:, low:high], preferred_element_type=jnp.float32
        ) + jnp.dot(acts_ref[:, wide:], other_ref[:, low:high], preferred_element_type=jnp.float32)
        part = part.astype(jnp.bfloat16)
        for back in range(SIDE):
            outs[back][:, low:high] = part[back * group : (back + 1) * group]


def expert_outs(acts, mine, other):
    tokens, both = acts.shape
    group, width, steps = tokens // SIDE, mine.shape[1], 4
    block = width // steps
    spec = pl.BlockSpec((both // 2, block), lambda i: (0, i))
    return pl.pallas_call(
        down_body,
        grid=(steps,),
        out_shape=[jax.ShapeDtypeStruct((group, width), jnp.bfloat16)] * SIDE,
        in_specs=[pl.BlockSpec((tokens, both), lambda i: (0, 0)), spec, spec],
        out_specs=[pl.BlockSpec((group, block), lambda i: (0, i))] * SIDE,
        compiler_params=pltpu.CompilerParams(vmem_limit_bytes=12 << 20),
        cost_estimate=pl.CostEstimate(
            flops=2 * tokens * both * width, bytes_accessed=1 << 20, transcendentals=0
        ),
        name="expert_outs",
    )(acts, mine, other)


def plus(first, *others):
    total = first.astype(jnp.float32)
    for other in others:
        total = total + other.astype(jnp.float32)
    return total


def on_device(
    resid,
    ffn_gain,
    expert_ids,
    gate_weights,
    w_gate,
    w_up,
    w_down,
    attn_gain,
    w_kv,
    kv_gain,
    cache,
    lengths,
    queries,
):
    tok_count = resid.shape[0]
    model_width = resid.shape[1]
    sec = lax.axis_index("sec")
    chip_expert = lax.axis_index("dev") // (SIDE**3 // (EXPERTS // 2))
    gate_other = swap_cores(w_gate)
    normed = rms_scale(resid, ffn_gain).astype(jnp.bfloat16)
    dense_weights = jnp.sum(
        jnp.where(
            expert_ids[:, :, None] == jnp.arange(EXPERTS, dtype=jnp.int32)[None, None, :],
            gate_weights[:, :, None],
            0.0,
        ),
        axis=1,
    )
    high = dense_weights.astype(jnp.bfloat16)
    rest = dense_weights - high.astype(jnp.float32)
    middle = rest.astype(jnp.bfloat16)
    low = (rest - middle.astype(jnp.float32)).astype(jnp.bfloat16)
    weight_cols = jnp.concatenate(
        [high, middle, low, jnp.zeros((tok_count, LANES - 3 * EXPERTS), jnp.bfloat16)], axis=1
    )
    rows = jnp.concatenate([normed, weight_cols], axis=1)[None]
    got = [rows] + [shift(rows, 0, back) for back in range(1, SIDE)]
    (rows,) = join(lax.optimization_barrier((got, gate_other))[0], 1)
    up_other = swap_cores(after(w_up, rows))
    got = [rows] + [shift(rows, 1, back) for back in range(1, SIDE)]
    low, high = join(lax.optimization_barrier((got, up_other))[0], 2)
    down_other = swap_cores(after(w_down, low))
    low_back, high_ahead = shift(low, 2, 1), shift(high, 2, -1)
    high_back, low_ahead = shift(high, 2, 1), shift(low, 2, -1)
    low_far, high_far = shift(low_back, 2, 1), shift(high_ahead, 2, -1)

    half = EXPERTS // 2
    info = jnp.stack([chip_expert + sec * half, chip_expert + (1 - sec) * half]).astype(jnp.int32)
    weights = (w_gate, gate_other, w_up, up_other)

    def flat(*parts):
        return [part.reshape(-1, part.shape[-1]) for part in parts]

    acts = expert_acts(info, flat(low, high, low_back, high_ahead), weights)
    low_mine, high_mine, low_back, high_ahead = expert_outs(acts, w_down, down_other)
    info = after(info, low_mine)
    acts = expert_acts(info, flat(high_back, low_ahead, low_far, high_far), weights)
    high_back, low_ahead, low_far, high_far = expert_outs(acts, w_down, down_other)

    low_far, high_far = shift(low_far, 2, -1), shift(high_far, 2, 1)
    high_back, low_ahead = shift(high_back, 2, -1), shift(low_ahead, 2, 1)
    low_back = shift(plus(low_back, low_far).astype(jnp.bfloat16), 2, -1)
    high_ahead = shift(plus(high_ahead, high_far).astype(jnp.bfloat16), 2, 1)
    low = plus(low_mine, low_back, low_ahead).astype(jnp.bfloat16)
    high = plus(high_mine, high_back, high_ahead).astype(jnp.bfloat16)
    parts = [*jnp.split(low, 2, axis=0), *jnp.split(high, 2, axis=0)]
    for phase in (1, 0):
        moe = plus(parts[0], *(shift(parts[back], phase, -back) for back in range(1, SIDE)))
        if phase > 0:
            parts = jnp.split(moe.astype(jnp.bfloat16), SIDE, axis=0)
    hidden = (resid.astype(jnp.float32) + moe).astype(jnp.bfloat16)
    attn_in = rms_scale(hidden, attn_gain).astype(jnp.bfloat16)
    kv_raw = jnp.dot(attn_in, w_kv, preferred_element_type=jnp.float32)
    latent = rms_scale(kv_raw[:, :KVL], kv_gain)
    rotated = rotate_half(kv_raw[:, KVL:], lengths)
    new_entry = jnp.concatenate([latent, rotated], axis=-1).astype(jnp.bfloat16)
    scores_old = (
        jnp.einsum("thc,tpc->thp", queries, cache, preferred_element_type=jnp.float32) * SCORE_SCALE
    )
    scores_new = (
        jnp.einsum("thc,tc->th", queries, new_entry, preferred_element_type=jnp.float32)
        * SCORE_SCALE
    )
    live_mask = jnp.arange(cache.shape[1], dtype=jnp.int32)[None, None, :] < lengths[:, None, None]
    scores_old = jnp.where(live_mask, scores_old, -jnp.inf)
    peak = jnp.maximum(jnp.max(scores_old, axis=2), scores_new)
    exp_old = jnp.exp(scores_old - peak[:, :, None])
    exp_new = jnp.exp(scores_new - peak)
    denom = jnp.sum(exp_old, axis=2) + exp_new
    probs_old = (exp_old / denom[:, :, None]).astype(jnp.bfloat16)
    probs_new = (exp_new / denom).astype(jnp.bfloat16)
    mixed = jnp.einsum(
        "thp,tpc->thc", probs_old, cache[:, :, :KVL], preferred_element_type=jnp.float32
    )
    mixed = mixed + probs_new.astype(jnp.float32)[:, :, None] * new_entry[:, None, :KVL].astype(
        jnp.float32
    )
    attn_out = mixed.astype(jnp.bfloat16)
    return (hidden, new_entry, attn_out)


def solution(mesh):
    placed = (
        P(("sec", "dev"), None),
        P(),
        P(("sec", "dev"), None),
        P(("sec", "dev"), None),
        P(None, ("sec", "dev")),
        P(None, ("sec", "dev")),
        P(("sec", "dev"), None),
        P(),
        P(),
        P(),
        P(("sec", "dev"), None, None),
        P(("sec", "dev")),
        P(("sec", "dev"), None, None),
    )
    return jax.shard_map(
        on_device,
        mesh=mesh,
        in_specs=placed,
        out_specs=(P(("sec", "dev"), None), P(("sec", "dev"), None), P(("sec", "dev"), None, None)),
        check_vma=False,
    )
```

profile of v0, /device:TPU:2, one launch (start us, length us, event | category | flops | bytes accessed | tf_op | source)
XLA Modules:
  0.0 163.3 jit_solution(15202633266811590068)
XLA Ops:
  8.6 3.1 %collective-permute-done.1.refs_2_ = bf16[1,8,7296]{2,1,0:T(8,128)(2,1)S(1)} collective-permute-done((bf16[1,8,7296]{2,1,0:T(8,128)(2,1)S(1)}, bf16[1,8,7296]{2,1,0:T(8,128)(2,1)S(1)}, u32[]{:S(2)}, u32[]{:S(2)}) %collective-permute-start.1) | collective-permute-done | bytes 116768 | tf_op jit(solution)/shard_map/ppermute | solution.py:54
  14.9 2.9 %collective-permute-start.5 = (bf16[4,8,7296]{2,1,0:T(8,128)(2,1)S(1)}, bf16[4,8,7296]{2,1,0:T(8,128)(2,1)S(1)}, u32[]{:S(2)}, u32[]{:S(2)}) collective-permute-start(bf16[4,8,7296]{2,1,0:T(8,128)(2,1)S(1)} %join.2.refs_0_), channel_id=1, source_target_pairs={{0,8},{1,9},{2,10},{3,11},{4,12},{5,13},{6,14},{7,15},{8,0},{9,1},... | collective-permute-start | bytes 1400840 | tf_op jit(solution)/shard_map/ppermute | solution.py:54
  19.1 3.9 %collective-permute-done.4.refs_1_ = bf16[4,8,7296]{2,1,0:T(8,128)(2,1)S(1)} collective-permute-done((bf16[4,8,7296]{2,1,0:T(8,128)(2,1)S(1)}, bf16[4,8,7296]{2,1,0:T(8,128)(2,1)S(1)}, u32[]{:S(2)}, u32[]{:S(2)}) %collective-permute-start.4) | collective-permute-done | bytes 466976 | tf_op jit(solution)/shard_map/ppermute | solution.py:54
  23.0 6.3 %collective-permute-done.5.refs_2_ = bf16[4,8,7296]{2,1,0:T(8,128)(2,1)S(1)} collective-permute-done((bf16[4,8,7296]{2,1,0:T(8,128)(2,1)S(1)}, bf16[4,8,7296]{2,1,0:T(8,128)(2,1)S(1)}, u32[]{:S(2)}, u32[]{:S(2)}) %collective-permute-start.5) | collective-permute-done | bytes 466976 | tf_op jit(solution)/shard_map/ppermute | solution.py:54
  32.8 3.8 %collective-permute-start.9 = (bf16[8,8,7296]{2,1,0:T(8,128)(2,1)S(1)}, bf16[8,8,7296]{2,1,0:T(8,128)(2,1)}, u32[]{:S(2)}, u32[]{:S(2)}) collective-permute-start(bf16[8,8,7296]{2,1,0:T(8,128)(2,1)S(1)} %get-tuple-element.34), channel_id=1, source_target_pairs={{0,3},{1,0},{2,1},{3,2},{4,7},{5,4},{6,5},{7,6},{8,11},{9,8},{10,9... | collective-permute-start | bytes 2801672 | tf_op jit(solution)/shard_map/ppermute | solution.py:54
  36.6 3.3 %collective-permute-start.12 = (bf16[8,8,7296]{2,1,0:T(8,128)(2,1)S(1)}, bf16[8,8,7296]{2,1,0:T(8,128)(2,1)}, u32[]{:S(2)}, u32[]{:S(2)}) collective-permute-start(bf16[8,8,7296]{2,1,0:T(8,128)(2,1)S(1)} %get-tuple-element.33), channel_id=1, source_target_pairs={{0,3},{1,0},{2,1},{3,2},{4,7},{5,4},{6,5},{7,6},{8,11},{9,8},{10,9... | collective-permute-start | bytes 2801672 | tf_op jit(solution)/shard_map/ppermute | solution.py:54
  39.9 7.8 %collective-permute-done.9 = bf16[8,8,7296]{2,1,0:T(8,128)(2,1)} collective-permute-done((bf16[8,8,7296]{2,1,0:T(8,128)(2,1)S(1)}, bf16[8,8,7296]{2,1,0:T(8,128)(2,1)}, u32[]{:S(2)}, u32[]{:S(2)}) %collective-permute-start.9) | collective-permute-done | bytes 933920 | tf_op jit(solution)/shard_map/ppermute | solution.py:54
  47.7 3.8 %collective-permute-start.14 = (bf16[8,8,7296]{2,1,0:T(8,128)(2,1)}, bf16[8,8,7296]{2,1,0:T(8,128)(2,1)}, u32[]{:S(2)}, u32[]{:S(2)}) collective-permute-start(bf16[8,8,7296]{2,1,0:T(8,128)(2,1)} %collective-permute-done.9), channel_id=1, source_target_pairs={{0,3},{1,0},{2,1},{3,2},{4,7},{5,4},{6,5},{7,6},{8,11},{9,8},{10,9... | collective-permute-start | bytes 2801672 | tf_op jit(solution)/shard_map/ppermute | solution.py:54
  57.7 6.7 %expert_acts.2.acts_ref = bf16[256,512]{1,0:T(8,128)(2,1)S(1)} custom-call(s32[2]{0:T(128)S(1)} %pad_add_fusion.info_ref, bf16[64,7296]{1,0:T(8,128)(2,1)S(1)} %bitcast.19, bf16[64,7296]{1,0:T(8,128)(2,1)S(1)} %bitcast.20, bf16[64,7296]{1,0:T(8,128)(2,1)} %bitcast.5.refs_2_, bf16[64,7296]{1,0:T(8,128)(2,1)} %bitcast.6.refs_3_, ...), custom_call_target="tpu_custom_call" | custom-call | flops 3758096384 | bytes 1048576 | tf_op jit(solution)/shard_map/expert_acts/pallas_call | solution.py:122
  64.5 5.3 %expert_outs.2 = (bf16[64,7168]{1,0:T(8,128)(2,1)S(1)}, bf16[64,7168]{1,0:T(8,128)(2,1)S(1)}, bf16[64,7168]{1,0:T(8,128)(2,1)S(1)}, bf16[64,7168]{1,0:T(8,128)(2,1)S(1)}) custom-call(bf16[256,512]{1,0:T(8,128)(2,1)S(1)} %expert_acts.2.acts_ref, bf16[256,7168]{1,0:T(8,128)(2,1)S(1)} %copy-done.1, bf16[256,7168]{1,0:T(8,128)(2,1)} %collective-permute-done.10.other_ref), custom_call_target="tpu_custom_call" | custom-call | flops 1879048192 | bytes 1048576 | tf_op jit(solution)/shard_map/expert_outs/pallas_call | solution.py:154
  71.5 7.2 %expert_acts.3.acts_ref = bf16[256,512]{1,0:T(8,128)(2,1)S(1)} custom-call(s32[2]{0:T(128)S(1)} %pad_add_fusion.info_ref, bf16[64,7296]{1,0:T(8,128)(2,1)} %bitcast.7.refs_0_, bf16[64,7296]{1,0:T(8,128)(2,1)} %bitcast.8.refs_1_, bf16[64,7296]{1,0:T(8,128)(2,1)} %bitcast.9.refs_2_, bf16[64,7296]{1,0:T(8,128)(2,1)} %bitcast.10.refs_3_, ...), custom_call_target="tpu_custom_call" | custom-call | flops 3758096384 | bytes 1048576 | tf_op jit(solution)/shard_map/expert_acts/pallas_call | solution.py:122
  78.7 4.8 %expert_outs.3 = (bf16[64,7168]{1,0:T(8,128)(2,1)S(1)}, bf16[64,7168]{1,0:T(8,128)(2,1)S(1)}, bf16[64,7168]{1,0:T(8,128)(2,1)S(1)}, bf16[64,7168]{1,0:T(8,128)(2,1)S(1)}) custom-call(bf16[256,512]{1,0:T(8,128)(2,1)S(1)} %expert_acts.3.acts_ref, bf16[256,7168]{1,0:T(8,128)(2,1)S(1)} %copy-done.1, bf16[256,7168]{1,0:T(8,128)(2,1)} %collective-permute-done.10.other_ref), custom_call_target="tpu_custom_call" | custom-call | flops 1879048192 | bytes 1048576 | tf_op jit(solution)/shard_map/expert_outs/pallas_call | solution.py:154
  85.6 3.2 %collective-permute-start.19 = (bf16[64,7168]{1,0:T(8,128)(2,1)S(1)}, bf16[64,7168]{1,0:T(8,128)(2,1)S(1)}, u32[]{:S(2)}, u32[]{:S(2)}) collective-permute-start(bf16[64,7168]{1,0:T(8,128)(2,1)S(1)} %get-tuple-element.42), channel_id=1, source_target_pairs={{0,3},{1,0},{2,1},{3,2},{4,7},{5,4},{6,5},{7,6},{8,11},{9,8},{10,9... | collective-permute-start | bytes 2752520 | tf_op jit(solution)/shard_map/ppermute | solution.py:54
  88.8 8.1 %collective-permute-done.15 = bf16[64,7168]{1,0:T(8,128)(2,1)S(1)} collective-permute-done((bf16[64,7168]{1,0:T(8,128)(2,1)S(1)}, bf16[64,7168]{1,0:T(8,128)(2,1)S(1)}, u32[]{:S(2)}, u32[]{:S(2)}) %collective-permute-start.15) | collective-permute-done | bytes 917536 | tf_op jit(solution)/shard_map/ppermute | solution.py:54
  97.1 2.8 %collective-permute-start.16 = (bf16[64,7168]{1,0:T(8,128)(2,1)S(1)}, bf16[64,7168]{1,0:T(8,128)(2,1)S(1)}, u32[]{:S(2)}, u32[]{:S(2)}) collective-permute-start(bf16[64,7168]{1,0:T(8,128)(2,1)S(1)} %add_convert_fusion.4), channel_id=1, source_target_pairs={{0,3},{1,0},{2,1},{3,2},{4,7},{5,4},{6,5},{7,6},{8,11},{9,8},{10,9... | collective-permute-start | bytes 2752520 | tf_op jit(solution)/shard_map/ppermute | solution.py:54
  99.9 9.5 %collective-permute-done.20 = bf16[64,7168]{1,0:T(8,128)(2,1)S(1)} collective-permute-done((bf16[64,7168]{1,0:T(8,128)(2,1)S(1)}, bf16[64,7168]{1,0:T(8,128)(2,1)S(1)}, u32[]{:S(2)}, u32[]{:S(2)}) %collective-permute-start.20) | collective-permute-done | bytes 917536 | tf_op jit(solution)/shard_map/ppermute | solution.py:54
  109.8 8.2 %collective-permute-done.16 = bf16[64,7168]{1,0:T(8,128)(2,1)S(1)} collective-permute-done((bf16[64,7168]{1,0:T(8,128)(2,1)S(1)}, bf16[64,7168]{1,0:T(8,128)(2,1)S(1)}, u32[]{:S(2)}, u32[]{:S(2)}) %collective-permute-start.16) | collective-permute-done | bytes 917536 | tf_op jit(solution)/shard_map/ppermute | solution.py:54
  120.1 10.8 %collective-permute-done.21 = bf16[64,7168]{1,0:T(8,128)(2,1)S(1)} collective-permute-done((bf16[64,7168]{1,0:T(8,128)(2,1)S(1)}, bf16[64,7168]{1,0:T(8,128)(2,1)S(1)}, u32[]{:S(2)}, u32[]{:S(2)}) %collective-permute-start.21) | collective-permute-done | bytes 917536 | tf_op jit(solution)/shard_map/ppermute | solution.py:54
  131.3 2.8 %collective-permute-start.22 = (bf16[32,7168]{1,0:T(8,128)(2,1)S(1)}, bf16[32,7168]{1,0:T(8,128)(2,1)S(1)}, u32[]{:S(2)}, u32[]{:S(2)}) collective-permute-start(bf16[32,7168]{1,0:T(8,128)(2,1)S(1)} %get-tuple-element.49), channel_id=1, source_target_pairs={{0,8},{1,9},{2,10},{3,11},{4,12},{5,13},{6,14},{7,15},{8,0},{9,1},... | collective-permute-start | bytes 1376264 | tf_op jit(solution)/shard_map/ppermute | solution.py:54
  134.2 8.2 %collective-permute-done.22 = bf16[32,7168]{1,0:T(8,128)(2,1)S(1)} collective-permute-done((bf16[32,7168]{1,0:T(8,128)(2,1)S(1)}, bf16[32,7168]{1,0:T(8,128)(2,1)S(1)}, u32[]{:S(2)}, u32[]{:S(2)}) %collective-permute-start.22) | collective-permute-done | bytes 458784 | tf_op jit(solution)/shard_map/ppermute | solution.py:54
  142.3 6.4 %collective-permute-done.23 = bf16[32,7168]{1,0:T(8,128)(2,1)S(1)} collective-permute-done((bf16[32,7168]{1,0:T(8,128)(2,1)S(1)}, bf16[32,7168]{1,0:T(8,128)(2,1)S(1)}, u32[]{:S(2)}, u32[]{:S(2)}) %collective-permute-start.23) | collective-permute-done | bytes 458784 | tf_op jit(solution)/shard_map/ppermute | solution.py:54
  149.1 3.0 %collective-permute-start.25 = (bf16[8,7168]{1,0:T(8,128)(2,1)S(1)}, bf16[8,7168]{1,0:T(8,128)(2,1)S(1)}, u32[]{:S(2)}, u32[]{:S(2)}) collective-permute-start(bf16[8,7168]{1,0:T(8,128)(2,1)S(1)} %get-tuple-element.53), channel_id=1, source_target_pairs={{0,32},{1,33},{2,34},{3,35},{4,36},{5,37},{6,38},{7,39},{8,40},{9,... | collective-permute-start | bytes 344072 | tf_op jit(solution)/shard_map/ppermute | solution.py:54
  152.1 2.3 %collective-permute-start.26 = (bf16[8,7168]{1,0:T(8,128)(2,1)S(1)}, bf16[8,7168]{1,0:T(8,128)(2,1)S(1)}, u32[]{:S(2)}, u32[]{:S(2)}) collective-permute-start(bf16[8,7168]{1,0:T(8,128)(2,1)S(1)} %get-tuple-element.52), channel_id=1, source_target_pairs={{0,16},{1,17},{2,18},{3,19},{4,20},{5,21},{6,22},{7,23},{8,24},{9,... | collective-permute-start | bytes 344072 | tf_op jit(solution)/shard_map/ppermute | solution.py:54
  157.4 2.2 %fusion.15 = f32[8,576]{1,0:T(8,128)S(1)} fusion(bf16[7168,576]{0,1:T(8,128)(2,1)S(1)} %bitcast.26, bf16[8,7168]{1,0:T(8,128)(2,1)S(1)} %get-tuple-element.48, f32[7168]{0:T(1024)S(1)} %copy-done.11, f32[8]{0:T(128)S(1)} %add_rsqrt_fusion.1), kind=kOutput, calls=%fused_computation.27 | convolution fusion | flops 66289664 | bytes 8419360 | tf_op jit(solution)/shard_map/dot_general | solution.py:248
  (103 shorter events, 35.9 us)
Async XLA Ops:
  0.6 11.8 %collective-permute-start.3 = (bf16[7168,256]{1,0:T(8,128)(2,1)}, bf16[7168,256]{1,0:T(8,128)(2,1)}, u32[]{:S(2)}, u32[]{:S(2)}) collective-permute-start(bf16[7168,256]{1,0:T(8,128)(2,1)} %refs_4_.3), channel_id=1, source_target_pairs={{0,64},{1,65},{2,66},{3,67},{4,68},{5,69},{6,70},{7,71},{8,72},{9,... | collective-permute-start | bytes 11010056 | tf_op jit(solution)/shard_map/ppermute | solution.py:58
  5.3 6.4 %collective-permute-start.1 = (bf16[1,8,7296]{2,1,0:T(8,128)(2,1)S(1)}, bf16[1,8,7296]{2,1,0:T(8,128)(2,1)S(1)}, u32[]{:S(2)}, u32[]{:S(2)}) collective-permute-start(bf16[1,8,7296]{2,1,0:T(8,128)(2,1)S(1)} %bitcast.22), channel_id=1, source_target_pairs={{0,32},{1,33},{2,34},{3,35},{4,36},{5,37},{6,38},{7,39},{8,40},{9,... | collective-permute-start | bytes 350216 | tf_op jit(solution)/shard_map/ppermute | solution.py:54
  13.0 16.3 %collective-permute-start.7 = (bf16[7168,256]{1,0:T(8,128)(2,1)}, bf16[7168,256]{1,0:T(8,128)(2,1)S(1)}, u32[]{:S(2)}, u32[]{:S(2)}) collective-permute-start(bf16[7168,256]{1,0:T(8,128)(2,1)} %refs_6_.3), channel_id=1, source_target_pairs={{0,64},{1,65},{2,66},{3,67},{4,68},{5,69},{6,70},{7,71},{8,72},{9,... | collective-permute-start | bytes 11010056 | tf_op jit(solution)/shard_map/ppermute | solution.py:58
  13.1 9.8 %collective-permute-start.4 = (bf16[4,8,7296]{2,1,0:T(8,128)(2,1)S(1)}, bf16[4,8,7296]{2,1,0:T(8,128)(2,1)S(1)}, u32[]{:S(2)}, u32[]{:S(2)}) collective-permute-start(bf16[4,8,7296]{2,1,0:T(8,128)(2,1)S(1)} %join.2.refs_0_), channel_id=1, source_target_pairs={{0,4},{1,5},{2,6},{3,7},{4,8},{5,9},{6,10},{7,11},{8,12},{9,13},{1... | collective-permute-start | bytes 1400840 | tf_op jit(solution)/shard_map/ppermute | solution.py:54
  14.9 14.4 %collective-permute-start.5 = (bf16[4,8,7296]{2,1,0:T(8,128)(2,1)S(1)}, bf16[4,8,7296]{2,1,0:T(8,128)(2,1)S(1)}, u32[]{:S(2)}, u32[]{:S(2)}) collective-permute-start(bf16[4,8,7296]{2,1,0:T(8,128)(2,1)S(1)} %join.2.refs_0_), channel_id=1, source_target_pairs={{0,8},{1,9},{2,10},{3,11},{4,12},{5,13},{6,14},{7,15},{8,0},{9,1},... | collective-permute-start | bytes 1400840 | tf_op jit(solution)/shard_map/ppermute | solution.py:54
  17.8 11.5 %collective-permute-start.6 = (bf16[4,8,7296]{2,1,0:T(8,128)(2,1)S(1)}, bf16[4,8,7296]{2,1,0:T(8,128)(2,1)S(1)}, u32[]{:S(2)}, u32[]{:S(2)}) collective-permute-start(bf16[4,8,7296]{2,1,0:T(8,128)(2,1)S(1)} %join.2.refs_0_), channel_id=1, source_target_pairs={{0,12},{1,13},{2,14},{3,15},{4,0},{5,1},{6,2},{7,3},{8,4},{9,5},{1... | collective-permute-start | bytes 1400840 | tf_op jit(solution)/shard_map/ppermute | solution.py:54
  32.4 32.0 %collective-permute-start.10 = (bf16[256,7168]{1,0:T(8,128)(2,1)}, bf16[256,7168]{1,0:T(8,128)(2,1)}, u32[]{:S(2)}, u32[]{:S(2)}) collective-permute-start(bf16[256,7168]{1,0:T(8,128)(2,1)} %mine_ref.3), channel_id=1, source_target_pairs={{0,64},{1,65},{2,66},{3,67},{4,68},{5,69},{6,70},{7,71},{8,72},{9,... | collective-permute-start | bytes 11010056 | tf_op jit(solution)/shard_map/ppermute | solution.py:58
  32.8 14.9 %collective-permute-start.9 = (bf16[8,8,7296]{2,1,0:T(8,128)(2,1)S(1)}, bf16[8,8,7296]{2,1,0:T(8,128)(2,1)}, u32[]{:S(2)}, u32[]{:S(2)}) collective-permute-start(bf16[8,8,7296]{2,1,0:T(8,128)(2,1)S(1)} %get-tuple-element.34), channel_id=1, source_target_pairs={{0,3},{1,0},{2,1},{3,2},{4,7},{5,4},{6,5},{7,6},{8,11},{9,8},{10,9... | collective-permute-start | bytes 2801672 | tf_op jit(solution)/shard_map/ppermute | solution.py:54
  36.6 14.9 %collective-permute-start.8 = (bf16[8,8,7296]{2,1,0:T(8,128)(2,1)S(1)}, bf16[8,8,7296]{2,1,0:T(8,128)(2,1)}, u32[]{:S(2)}, u32[]{:S(2)}) collective-permute-start(bf16[8,8,7296]{2,1,0:T(8,128)(2,1)S(1)} %get-tuple-element.33), channel_id=1, source_target_pairs={{0,1},{1,2},{2,3},{3,0},{4,5},{5,6},{6,7},{7,4},{8,9},{9,10},{10,1... | collective-permute-start | bytes 2801672 | tf_op jit(solution)/shard_map/ppermute | solution.py:54
  36.6 33.1 %collective-permute-start.11 = (bf16[8,8,7296]{2,1,0:T(8,128)(2,1)S(1)}, bf16[8,8,7296]{2,1,0:T(8,128)(2,1)}, u32[]{:S(2)}, u32[]{:S(2)}) collective-permute-start(bf16[8,8,7296]{2,1,0:T(8,128)(2,1)S(1)} %get-tuple-element.34), channel_id=1, source_target_pairs={{0,1},{1,2},{2,3},{3,0},{4,5},{5,6},{6,7},{7,4},{8,9},{9,10},{10,1... | collective-permute-start | bytes 2801672 | tf_op jit(solution)/shard_map/ppermute | solution.py:54
  36.6 33.1 %collective-permute-start.12 = (bf16[8,8,7296]{2,1,0:T(8,128)(2,1)S(1)}, bf16[8,8,7296]{2,1,0:T(8,128)(2,1)}, u32[]{:S(2)}, u32[]{:S(2)}) collective-permute-start(bf16[8,8,7296]{2,1,0:T(8,128)(2,1)S(1)} %get-tuple-element.33), channel_id=1, source_target_pairs={{0,3},{1,0},{2,1},{3,2},{4,7},{5,4},{6,5},{7,6},{8,11},{9,8},{10,9... | collective-permute-start | bytes 2801672 | tf_op jit(solution)/shard_map/ppermute | solution.py:54
  47.7 22.1 %collective-permute-start.14 = (bf16[8,8,7296]{2,1,0:T(8,128)(2,1)}, bf16[8,8,7296]{2,1,0:T(8,128)(2,1)}, u32[]{:S(2)}, u32[]{:S(2)}) collective-permute-start(bf16[8,8,7296]{2,1,0:T(8,128)(2,1)} %collective-permute-done.9), channel_id=1, source_target_pairs={{0,3},{1,0},{2,1},{3,2},{4,7},{5,4},{6,5},{7,6},{8,11},{9,8},{10,9... | collective-permute-start | bytes 2801672 | tf_op jit(solution)/shard_map/ppermute | solution.py:54
  51.5 20.0 %collective-permute-start.13 = (bf16[8,8,7296]{2,1,0:T(8,128)(2,1)}, bf16[8,8,7296]{2,1,0:T(8,128)(2,1)}, u32[]{:S(2)}, u32[]{:S(2)}) collective-permute-start(bf16[8,8,7296]{2,1,0:T(8,128)(2,1)} %collective-permute-done.8), channel_id=1, source_target_pairs={{0,1},{1,2},{2,3},{3,0},{4,5},{5,6},{6,7},{7,4},{8,9},{9,10},{10,1... | collective-permute-start | bytes 2801672 | tf_op jit(solution)/shard_map/ppermute | solution.py:54
  83.4 13.5 %collective-permute-start.15 = (bf16[64,7168]{1,0:T(8,128)(2,1)S(1)}, bf16[64,7168]{1,0:T(8,128)(2,1)S(1)}, u32[]{:S(2)}, u32[]{:S(2)}) collective-permute-start(bf16[64,7168]{1,0:T(8,128)(2,1)S(1)} %get-tuple-element.39), channel_id=1, source_target_pairs={{0,3},{1,0},{2,1},{3,2},{4,7},{5,4},{6,5},{7,6},{8,11},{9,8},{10,9... | collective-permute-start | bytes 2752520 | tf_op jit(solution)/shard_map/ppermute | solution.py:54
  85.0 24.7 %collective-permute-start.17 = (bf16[64,7168]{1,0:T(8,128)(2,1)S(1)}, bf16[64,7168]{1,0:T(8,128)(2,1)S(1)}, u32[]{:S(2)}, u32[]{:S(2)}) collective-permute-start(bf16[64,7168]{1,0:T(8,128)(2,1)S(1)} %get-tuple-element.40), channel_id=1, source_target_pairs={{0,1},{1,2},{2,3},{3,0},{4,5},{5,6},{6,7},{7,4},{8,9},{9,10},{10,1... | collective-permute-start | bytes 2752520 | tf_op jit(solution)/shard_map/ppermute | solution.py:54
  85.5 23.9 %collective-permute-start.20 = (bf16[64,7168]{1,0:T(8,128)(2,1)S(1)}, bf16[64,7168]{1,0:T(8,128)(2,1)S(1)}, u32[]{:S(2)}, u32[]{:S(2)}) collective-permute-start(bf16[64,7168]{1,0:T(8,128)(2,1)S(1)} %get-tuple-element.44), channel_id=1, source_target_pairs={{0,1},{1,2},{2,3},{3,0},{4,5},{5,6},{6,7},{7,4},{8,9},{9,10},{10,1... | collective-permute-start | bytes 2752520 | tf_op jit(solution)/shard_map/ppermute | solution.py:54
  85.6 34.6 %collective-permute-start.19 = (bf16[64,7168]{1,0:T(8,128)(2,1)S(1)}, bf16[64,7168]{1,0:T(8,128)(2,1)S(1)}, u32[]{:S(2)}, u32[]{:S(2)}) collective-permute-start(bf16[64,7168]{1,0:T(8,128)(2,1)S(1)} %get-tuple-element.42), channel_id=1, source_target_pairs={{0,3},{1,0},{2,1},{3,2},{4,7},{5,4},{6,5},{7,6},{8,11},{9,8},{10,9... | collective-permute-start | bytes 2752520 | tf_op jit(solution)/shard_map/ppermute | solution.py:54
  97.1 20.9 %collective-permute-start.16 = (bf16[64,7168]{1,0:T(8,128)(2,1)S(1)}, bf16[64,7168]{1,0:T(8,128)(2,1)S(1)}, u32[]{:S(2)}, u32[]{:S(2)}) collective-permute-start(bf16[64,7168]{1,0:T(8,128)(2,1)S(1)} %add_convert_fusion.4), channel_id=1, source_target_pairs={{0,3},{1,0},{2,1},{3,2},{4,7},{5,4},{6,5},{7,6},{8,11},{9,8},{10,9... | collective-permute-start | bytes 2752520 | tf_op jit(solution)/shard_map/ppermute | solution.py:54
  109.7 21.2 %collective-permute-start.21 = (bf16[64,7168]{1,0:T(8,128)(2,1)S(1)}, bf16[64,7168]{1,0:T(8,128)(2,1)S(1)}, u32[]{:S(2)}, u32[]{:S(2)}) collective-permute-start(bf16[64,7168]{1,0:T(8,128)(2,1)S(1)} %add_convert_fusion.2), channel_id=1, source_target_pairs={{0,1},{1,2},{2,3},{3,0},{4,5},{5,6},{6,7},{7,4},{8,9},{9,10},{10,1... | collective-permute-start | bytes 2752520 | tf_op jit(solution)/shard_map/ppermute | solution.py:54
  118.4 15.8 %collective-permute-start.18 = (bf16[32,7168]{1,0:T(8,128)(2,1)S(1)}, bf16[32,7168]{1,0:T(8,128)(2,1)S(1)}, u32[]{:S(2)}, u32[]{:S(2)}) collective-permute-start(bf16[32,7168]{1,0:T(8,128)(2,1)S(1)} %split.33), channel_id=1, source_target_pairs={{0,12},{1,13},{2,14},{3,15},{4,0},{5,1},{6,2},{7,3},{8,4},{9,5},{1... | collective-permute-start | bytes 1376264 | tf_op jit(solution)/shard_map/ppermute | solution.py:54
  131.3 11.0 %collective-permute-start.22 = (bf16[32,7168]{1,0:T(8,128)(2,1)S(1)}, bf16[32,7168]{1,0:T(8,128)(2,1)S(1)}, u32[]{:S(2)}, u32[]{:S(2)}) collective-permute-start(bf16[32,7168]{1,0:T(8,128)(2,1)S(1)} %get-tuple-element.49), channel_id=1, source_target_pairs={{0,8},{1,9},{2,10},{3,11},{4,12},{5,13},{6,14},{7,15},{8,0},{9,1},... | collective-permute-start | bytes 1376264 | tf_op jit(solution)/shard_map/ppermute | solution.py:54
  134.1 14.7 %collective-permute-start.23 = (bf16[32,7168]{1,0:T(8,128)(2,1)S(1)}, bf16[32,7168]{1,0:T(8,128)(2,1)S(1)}, u32[]{:S(2)}, u32[]{:S(2)}) collective-permute-start(bf16[32,7168]{1,0:T(8,128)(2,1)S(1)} %get-tuple-element.50), channel_id=1, source_target_pairs={{0,4},{1,5},{2,6},{3,7},{4,8},{5,9},{6,10},{7,11},{8,12},{9,13},{1... | collective-permute-start | bytes 1376264 | tf_op jit(solution)/shard_map/ppermute | solution.py:54
  149.0 6.2 %collective-permute-start.24 = (bf16[8,7168]{1,0:T(8,128)(2,1)S(1)}, bf16[8,7168]{1,0:T(8,128)(2,1)S(1)}, u32[]{:S(2)}, u32[]{:S(2)}) collective-permute-start(bf16[8,7168]{1,0:T(8,128)(2,1)S(1)} %get-tuple-element.51), channel_id=1, source_target_pairs={{0,48},{1,49},{2,50},{3,51},{4,52},{5,53},{6,54},{7,55},{8,56},{9,... | collective-permute-start | bytes 344072 | tf_op jit(solution)/shard_map/ppermute | solution.py:54
  149.1 6.9 %collective-permute-start.25 = (bf16[8,7168]{1,0:T(8,128)(2,1)S(1)}, bf16[8,7168]{1,0:T(8,128)(2,1)S(1)}, u32[]{:S(2)}, u32[]{:S(2)}) collective-permute-start(bf16[8,7168]{1,0:T(8,128)(2,1)S(1)} %get-tuple-element.53), channel_id=1, source_target_pairs={{0,32},{1,33},{2,34},{3,35},{4,36},{5,37},{6,38},{7,39},{8,40},{9,... | collective-permute-start | bytes 344072 | tf_op jit(solution)/shard_map/ppermute | solution.py:54
  (19 other events, 306.1 us)
where the time goes:
time: 166 us; the launch traced here: 163 us
  waiting for transfers between devices  76.8 us (46%)
  starting transfers between devices  40.3 us (24%)
  Pallas kernels  25.7 us (15%)
  local copies, waits for them, and re-layouts  8.32 us (5%)
  other arithmetic  6.12 us (4%)
  matrix products  5.13 us (3%)
    ppermute x24, waiting for transfers between devices, shift(): return lax.ppermute(values, AXES, pairs)  76.8 us
    ppermute x24, starting transfers between devices, shift(): return lax.ppermute(values, AXES, pairs)  39.8 us
    pallas_call x2, Pallas kernels, expert_acts(): pl.pallas_call(act_body, out_shape=jax.ShapeDtypeStruct((tokens, 2 * wide...  13.9 us
    pallas_call x2, Pallas kernels, expert_outs(): pl.pallas_call(down_body, grid=(steps,), out_shape=[jax.ShapeDtypeStruct(...  10 us
    unnamed x32, local copies, waits for them, and re-layouts  8.11 us
  transfers between devices with their start and end apart: 27, of which 15 were waited for; matrix products, arithmetic and copies ran while one was open for 3% of the time, Pallas kernels for 7%

commit v1 on v0

--- a/solution.py
+++ b/solution.py
@@ -12,7 +12,8 @@
 AXES = ("sec", "dev")
 SIDE = 4
 STRIDE = {"x": 16, "y": 4, "z": 1}
-ORDER = (("x", "y", "z"), ("y", "z", "x"))
+PLANE = (("x", "y"), ("y", "z"))
+LINE = ("z", "x")
 LANES = 128
 
 
@@ -43,10 +44,10 @@
     )
 
 
-def shift(values, phase, amount):
+def shift(values, amount):
     pairs = []
     for sec in range(2):
-        stride = STRIDE[ORDER[sec][phase]]
+        stride = STRIDE[LINE[sec]]
         for dev in range(SIDE**3):
             place = dev // stride % SIDE
             there = dev + ((place + amount) % SIDE - place) * stride
@@ -54,6 +55,18 @@
     return lax.ppermute(values, AXES, pairs)
 
 
+def plane_exchange(blocks):
+    groups = []
+    for sec in range(2):
+        one, two = (STRIDE[axis] for axis in PLANE[sec])
+        for line in range(SIDE):
+            base = sec * SIDE**3 + line * STRIDE[LINE[sec]]
+            groups.append([base + i * one + j * two for i in range(SIDE) for j in range(SIDE)])
+    return lax.all_to_all(
+        blocks, AXES, split_axis=0, concat_axis=0, axis_index_groups=groups, tiled=True
+    )
+
+
 def swap_cores(values):
     return lax.ppermute(values, AXES, [(i, (i + SIDE**3) % (2 * SIDE**3)) for i in range(2 * SIDE**3)])
 
@@ -62,41 +75,8 @@
     return lax.optimization_barrier((values, *earlier))[0]
 
 
-def join_body(count, *refs):
-    ins, outs, sems = refs[:SIDE], refs[SIDE : SIDE + count], refs[-1]
-    each = SIDE // count
-    copies = []
-    for back in range(SIDE):
-        rows = ins[back].shape[0]
-        copies.append(
-            pltpu.make_async_copy(
-                ins[back],
-                outs[back // each].at[pl.ds(back % each * rows, rows)],
-                sems.at[back],
-            )
-        )
-    for copy in copies:
-        copy.start()
-    for copy in copies:
-        copy.wait()
-
-
-def join(blocks, count):
-    rows, *rest = blocks[0].shape
-    hbm = pl.BlockSpec(memory_space=pl.ANY)
-    return pl.pallas_call(
-        functools.partial(join_body, count),
-        out_shape=[jax.ShapeDtypeStruct((SIDE // count * rows, *rest), blocks[0].dtype)] * count,
-        in_specs=[hbm] * SIDE,
-        out_specs=[hbm] * count,
-        scratch_shapes=[pltpu.SemaphoreType.DMA((SIDE,))],
-        compiler_params=pltpu.CompilerParams(vmem_limit_bytes=1 << 20),
-        name="join",
-    )(*blocks)
-
-
 def act_body(info_ref, *refs):
-    rows, weights, out_ref = refs[:SIDE], refs[SIDE : 2 * SIDE], refs[2 * SIDE]
+    rows, weights, out_ref = refs[:-5], refs[-5:-1], refs[-1]
     depth, wide = weights[0].shape
     held = jnp.concatenate([part[:, depth:] for part in rows], axis=0).astype(jnp.float32)
     lane = lax.broadcasted_iota(jnp.int32, (1, LANES), 1)
@@ -116,15 +96,15 @@
 
 
 def expert_acts(info, rows, weights):
-    tokens = SIDE * rows[0].shape[0]
+    tokens = sum(part.shape[0] for part in rows)
     depth, wide = weights[0].shape
     vmem = pl.BlockSpec(memory_space=pltpu.VMEM)
     return pl.pallas_call(
         act_body,
         out_shape=jax.ShapeDtypeStruct((tokens, 2 * wide), jnp.bfloat16),
-        in_specs=[pl.BlockSpec(memory_space=pltpu.SMEM)] + [vmem] * (2 * SIDE),
+        in_specs=[pl.BlockSpec(memory_space=pltpu.SMEM)] + [vmem] * (len(rows) + 4),
         out_specs=vmem,
-        compiler_params=pltpu.CompilerParams(vmem_limit_bytes=30 << 20),
+        compiler_params=pltpu.CompilerParams(vmem_limit_bytes=23 << 20),
         cost_estimate=pl.CostEstimate(
             flops=8 * tokens * depth * wide, bytes_accessed=1 << 20, transcendentals=0
         ),
@@ -134,30 +114,28 @@
 
 def down_body(acts_ref, mine_ref, other_ref, *outs):
     wide = mine_ref.shape[0]
-    group = acts_ref.shape[0] // SIDE
-    step = 2 * LANES
+    group = outs[0].shape[0]
+    step = 4 * LANES
     for low in range(0, mine_ref.shape[1], step):
         high = low + step
         part = jnp.dot(
             acts_ref[:, :wide], mine_ref[:, low:high], preferred_element_type=jnp.float32
         ) + jnp.dot(acts_ref[:, wide:], other_ref[:, low:high], preferred_element_type=jnp.float32)
         part = part.astype(jnp.bfloat16)
-        for back in range(SIDE):
-            outs[back][:, low:high] = part[back * group : (back + 1) * group]
-
-
-def expert_outs(acts, mine, other):
+        for number, out in enumerate(outs):
+            out[:, low:high] = part[number * group : (number + 1) * group]
+
+
+def expert_outs(acts, mine, other, count):
     tokens, both = acts.shape
-    group, width, steps = tokens // SIDE, mine.shape[1], 4
-    block = width // steps
-    spec = pl.BlockSpec((both // 2, block), lambda i: (0, i))
+    width = mine.shape[1]
+    vmem = pl.BlockSpec(memory_space=pltpu.VMEM)
     return pl.pallas_call(
         down_body,
-        grid=(steps,),
-        out_shape=[jax.ShapeDtypeStruct((group, width), jnp.bfloat16)] * SIDE,
-        in_specs=[pl.BlockSpec((tokens, both), lambda i: (0, 0)), spec, spec],
-        out_specs=[pl.BlockSpec((group, block), lambda i: (0, i))] * SIDE,
-        compiler_params=pltpu.CompilerParams(vmem_limit_bytes=12 << 20),
+        out_shape=[jax.ShapeDtypeStruct((tokens // count, width), jnp.bfloat16)] * count,
+        in_specs=[vmem] * 3,
+        out_specs=[vmem] * count,
+        compiler_params=pltpu.CompilerParams(vmem_limit_bytes=16 << 20),
         cost_estimate=pl.CostEstimate(
             flops=2 * tokens * both * width, bytes_accessed=1 << 20, transcendentals=0
         ),
@@ -208,16 +186,14 @@
     weight_cols = jnp.concatenate(
         [high, middle, low, jnp.zeros((tok_count, LANES - 3 * EXPERTS), jnp.bfloat16)], axis=1
     )
-    rows = jnp.concatenate([normed, weight_cols], axis=1)[None]
-    got = [rows] + [shift(rows, 0, back) for back in range(1, SIDE)]
-    (rows,) = join(lax.optimization_barrier((got, gate_other))[0], 1)
-    up_other = swap_cores(after(w_up, rows))
-    got = [rows] + [shift(rows, 1, back) for back in range(1, SIDE)]
-    low, high = join(lax.optimization_barrier((got, up_other))[0], 2)
-    down_other = swap_cores(after(w_down, low))
-    low_back, high_ahead = shift(low, 2, 1), shift(high, 2, -1)
-    high_back, low_ahead = shift(high, 2, 1), shift(low, 2, -1)
-    low_far, high_far = shift(low_back, 2, 1), shift(high_ahead, 2, -1)
+    rows = jnp.concatenate([normed, weight_cols], axis=1)
+    up_other = swap_cores(w_up)
+    rows = plane_exchange(jnp.broadcast_to(rows[None], (SIDE * SIDE, *rows.shape)))
+    rows, gate_other, up_other = lax.optimization_barrier((rows, gate_other, up_other))
+    down_other = swap_cores(after(w_down, rows))
+    low, high = jnp.split(rows, 2, axis=0)
+    low_back, high_ahead = shift(low, 1), shift(high, -1)
+    high_back, low_ahead = shift(high, 1), shift(low, -1)
 
     half = EXPERTS // 2
     info = jnp.stack([chip_expert + sec * half, chip_expert + (1 - sec) * half]).astype(jnp.int32)
@@ -226,23 +202,31 @@
     def flat(*parts):
         return [part.reshape(-1, part.shape[-1]) for part in parts]
 
-    acts = expert_acts(info, flat(low, high, low_back, high_ahead), weights)
-    low_mine, high_mine, low_back, high_ahead = expert_outs(acts, w_down, down_other)
-    info = after(info, low_mine)
-    acts = expert_acts(info, flat(high_back, low_ahead, low_far, high_far), weights)
-    high_back, low_ahead, low_far, high_far = expert_outs(acts, w_down, down_other)
-
-    low_far, high_far = shift(low_far, 2, -1), shift(high_far, 2, 1)
-    high_back, low_ahead = shift(high_back, 2, -1), shift(low_ahead, 2, 1)
-    low_back = shift(plus(low_back, low_far).astype(jnp.bfloat16), 2, -1)
-    high_ahead = shift(plus(high_ahead, high_far).astype(jnp.bfloat16), 2, 1)
+    mine_acts = expert_acts(info, flat(rows), weights)
+    low_back, high_ahead = lax.optimization_barrier((low_back, high_ahead, mine_acts))[:2]
+    low_far, high_far = shift(low_back, 1), shift(high_ahead, -1)
+    near_acts = expert_acts(info, flat(low_back, high_ahead), weights)
+    acts = expert_acts(after(info, near_acts), flat(high_back, low_ahead), weights)
+    high_back, low_ahead = expert_outs(acts, w_down, down_other, 2)
+    high_back, low_ahead, low_far, high_far = lax.optimization_barrier(
+        (high_back, low_ahead, low_far, high_far)
+    )
+    high_back, low_ahead = shift(high_back, -1), shift(low_ahead, 1)
+    acts = expert_acts(info, flat(low_far, high_far), weights)
+    low_far, high_far = expert_outs(acts, w_down, down_other, 2)
+    low_far, high_far, high_back, low_ahead = lax.optimization_barrier(
+        (low_far, high_far, high_back, low_ahead)
+    )
+    near_acts, mine_acts = lax.optimization_barrier((near_acts, mine_acts, low_far))[:2]
+    low_far, high_far = shift(low_far, -1), shift(high_far, 1)
+    low_back, high_ahead = expert_outs(near_acts, w_down, down_other, 2)
+    low_mine, high_mine = expert_outs(mine_acts, w_down, down_other, 2)
+    low_back = shift(plus(low_back, low_far).astype(jnp.bfloat16), -1)
+    high_ahead = shift(plus(high_ahead, high_far).astype(jnp.bfloat16), 1)
     low = plus(low_mine, low_back, low_ahead).astype(jnp.bfloat16)
     high = plus(high_mine, high_back, high_ahead).astype(jnp.bfloat16)
-    parts = [*jnp.split(low, 2, axis=0), *jnp.split(high, 2, axis=0)]
-    for phase in (1, 0):
-        moe = plus(parts[0], *(shift(parts[back], phase, -back) for back in range(1, SIDE)))
-        if phase > 0:
-            parts = jnp.split(moe.astype(jnp.bfloat16), SIDE, axis=0)
+    sums = jnp.concatenate([low, high], axis=0).reshape(SIDE * SIDE, tok_count, model_width)
+    moe = jnp.sum(plane_exchange(sums).astype(jnp.float32), axis=0)
     hidden = (resid.astype(jnp.float32) + moe).astype(jnp.bfloat16)
     attn_in = rms_scale(hidden, attn_gain).astype(jnp.bfloat16)
     kv_raw = jnp.dot(attn_in, w_kv, preferred_element_type=jnp.float32)

time: 166 us -> 162 us (0.976)
  the two profiles are of different devices: /device:TPU:2 before, /device:TPU:1 now
where the time goes in v1:
time: 162 us; the launch traced here: 161 us
  waiting for transfers between devices  40.3 us (25%)
  Pallas kernels  39.2 us (24%)
  blocking collectives  33.6 us (21%)
  starting transfers between devices  22.8 us (14%)
  matrix products  11.1 us (7%)
  other arithmetic  7.43 us (5%)
  local copies, waits for them, and re-layouts  5.72 us (4%)
    all_to_all x1, blocking collectives, plane_exchange(): lax.all_to_all(blocks, AXES, split_axis=0, concat_axis=0, axis_index_grou...  33.6 us
    all_to_all x1, waiting for transfers between devices, plane_exchange(): lax.all_to_all(blocks, AXES, split_axis=0, concat_axis=0, axis_index_grou...  23.1 us
    pallas_call x4, Pallas kernels, expert_acts(): pl.pallas_call(act_body, out_shape=jax.ShapeDtypeStruct((tokens, 2 * wide...  21.8 us
    pallas_call x4, Pallas kernels, expert_outs(): pl.pallas_call(down_body, out_shape=[jax.ShapeDtypeStruct((tokens // coun...  17.5 us
    ppermute x12, starting transfers between devices, shift(): return lax.ppermute(values, AXES, pairs)  17.4 us
    ppermute x12, waiting for transfers between devices, shift(): return lax.ppermute(values, AXES, pairs)  17.2 us
    dot_general x1, matrix products, on_device(): kv_raw = jnp.dot(attn_in, w_kv, preferred_element_type=jnp.float32)  5.72 us
    unnamed x24, local copies, waits for them, and re-layouts  4.13 us
  transfers between devices with their start and end apart: 16, of which 7 were waited for; matrix products, arithmetic and copies ran while one was open for 5% of the time, Pallas kernels for 24%

profile of v1, /device:TPU:1, one launch (start us, length us, event | category | flops | bytes accessed | tf_op | source)
XLA Modules:
  0.0 161.2 jit_solution(17471926425737285730)
XLA Ops:
  5.4 33.6 %all_to_all.10 = bf16[16,8,7296]{2,1,0:T(8,128)(2,1)S(1)} all-to-all(bf16[16,8,7296]{2,1,0:T(8,128)(2,1)S(1)} %broadcast_in_dim.27), channel_id=1, replica_groups={{0,4,8,12,16,20,24,28,32,36,40,44,48,52,56,60},{1,5,9,13,17,21,25,29,33..., dimensions={0} | all-to-all | bytes 3735552 | tf_op jit(solution)/shard_map/all_to_all | solution.py:65
  43.0 2.7 %collective-permute-start.5 = (bf16[8,8,7296]{2,1,0:T(8,128)(2,1)}, bf16[8,8,7296]{2,1,0:T(8,128)(2,1)S(1)}, u32[]{:S(2)}, u32[]{:S(2)}) collective-permute-start(bf16[8,8,7296]{2,1,0:T(8,128)(2,1)} %get-tuple-element.58), channel_id=1, source_target_pairs={{0,3},{1,0},{2,1},{3,2},{4,7},{5,4},{6,5},{7,6},{8,11},{9,8},{10,9... | collective-permute-start | bytes 2801672 | tf_op jit(solution)/shard_map/ppermute | solution.py:55
  45.8 2.0 %copy-done.1 = bf16[7168,256]{1,0:T(8,128)(2,1)S(1)} copy-done((bf16[7168,256]{1,0:T(8,128)(2,1)S(1)}, bf16[7168,256]{1,0:T(8,128)(2,1)}, u32[]{:S(2)}) %copy-start.1) | copy-done | bytes 3670040
  47.8 2.0 %copy-done.3 = bf16[7168,256]{1,0:T(8,128)(2,1)S(1)} copy-done((bf16[7168,256]{1,0:T(8,128)(2,1)S(1)}, bf16[7168,256]{1,0:T(8,128)(2,1)}, u32[]{:S(2)}) %copy-start.3) | copy-done | bytes 3670040
  49.9 5.3 %expert_acts.4.acts_ref = bf16[128,512]{1,0:T(8,128)(2,1)S(1)} custom-call(s32[2]{0:T(128)S(1)} %pad_add_fusion.info_ref, bf16[128,7296]{1,0:T(8,128)(2,1)S(1)} %bitcast.19, bf16[7168,256]{1,0:T(8,128)(2,1)S(1)} %copy-done.1, bf16[7168,256]{1,0:T(8,128)(2,1)} %collective-permute-done.refs_2_.refs_3_, bf16[7168,256]{1,0:T(8,128)(2,1)S(1)} %copy-done.3, ...), custom_call_target="tpu_custom_call" | custom-call | flops 1879048192 | bytes 1048576 | tf_op jit(solution)/shard_map/expert_acts/pallas_call | solution.py:102
  55.8 2.1 %collective-permute-start.8 = (bf16[8,8,7296]{2,1,0:T(8,128)(2,1)}, bf16[8,8,7296]{2,1,0:T(8,128)(2,1)S(1)}, u32[]{:S(2)}, u32[]{:S(2)}) collective-permute-start(bf16[8,8,7296]{2,1,0:T(8,128)(2,1)} %collective-permute-done.3), channel_id=1, source_target_pairs={{0,3},{1,0},{2,1},{3,2},{4,7},{5,4},{6,5},{7,6},{8,11},{9,8},{10,9... | collective-permute-start | bytes 2801672 | tf_op jit(solution)/shard_map/ppermute | solution.py:55
  57.9 5.8 %expert_acts.5.acts_ref = bf16[128,512]{1,0:T(8,128)(2,1)S(1)} custom-call(s32[2]{0:T(128)S(1)} %pad_add_fusion.info_ref, bf16[64,7296]{1,0:T(8,128)(2,1)} %bitcast.3.refs_0_, bf16[64,7296]{1,0:T(8,128)(2,1)} %bitcast.4.refs_1_, bf16[7168,256]{1,0:T(8,128)(2,1)S(1)} %copy-done.1, bf16[7168,256]{1,0:T(8,128)(2,1)} %collective-permute-done.refs_2_.refs_3_, ...), custom_call_target="tpu_custom_call" | custom-call | flops 1879048192 | bytes 1048576 | tf_op jit(solution)/shard_map/expert_acts/pallas_call | solution.py:102
  64.5 5.3 %expert_acts.6.acts_ref = bf16[128,512]{1,0:T(8,128)(2,1)S(1)} custom-call(s32[2]{0:T(128)S(1)} %pad_add_fusion.info_ref, bf16[64,7296]{1,0:T(8,128)(2,1)S(1)} %bitcast.22, bf16[64,7296]{1,0:T(8,128)(2,1)S(1)} %bitcast.23, bf16[7168,256]{1,0:T(8,128)(2,1)S(1)} %copy-done.1, bf16[7168,256]{1,0:T(8,128)(2,1)} %collective-permute-done.refs_2_.refs_3_, ...), custom_call_target="tpu_custom_call" | custom-call | flops 1879048192 | bytes 1048576 | tf_op jit(solution)/shard_map/expert_acts/pallas_call | solution.py:102
  69.9 4.5 %expert_outs.4 = (bf16[64,7168]{1,0:T(8,128)(2,1)S(1)}, bf16[64,7168]{1,0:T(8,128)(2,1)S(1)}) custom-call(bf16[128,512]{1,0:T(8,128)(2,1)S(1)} %expert_acts.6.acts_ref, bf16[256,7168]{1,0:T(8,128)(2,1)} %mine_ref.7, bf16[256,7168]{1,0:T(8,128)(2,1)} %collective-permute-done.6.other_ref), custom_call_target="tpu_custom_call" | custom-call | flops 939524096 | bytes 1048576 | tf_op jit(solution)/shard_map/expert_outs/pallas_call | solution.py:133
  75.7 1.7 %collective-permute-start.9 = (bf16[64,7168]{1,0:T(8,128)(2,1)S(1)}, bf16[64,7168]{1,0:T(8,128)(2,1)S(1)}, u32[]{:S(2)}, u32[]{:S(2)}) collective-permute-start(bf16[64,7168]{1,0:T(8,128)(2,1)S(1)} %get-tuple-element.41), channel_id=1, source_target_pairs={{0,3},{1,0},{2,1},{3,2},{4,7},{5,4},{6,5},{7,6},{8,11},{9,8},{10,9... | collective-permute-start | bytes 2752520 | tf_op jit(solution)/shard_map/ppermute | solution.py:55
  77.4 5.3 %expert_acts.7.acts_ref = bf16[128,512]{1,0:T(8,128)(2,1)S(1)} custom-call(s32[2]{0:T(128)S(1)} %pad_add_fusion.info_ref, bf16[64,7296]{1,0:T(8,128)(2,1)S(1)} %bitcast.20, bf16[64,7296]{1,0:T(8,128)(2,1)S(1)} %bitcast.21, bf16[7168,256]{1,0:T(8,128)(2,1)S(1)} %copy-done.2, bf16[7168,256]{1,0:T(8,128)(2,1)} %collective-permute-done.refs_2_.refs_3_, ...), custom_call_target="tpu_custom_call" | custom-call | flops 1879048192 | bytes 1048576 | tf_op jit(solution)/shard_map/expert_acts/pallas_call | solution.py:102
  82.7 4.4 %expert_outs.5 = (bf16[64,7168]{1,0:T(8,128)(2,1)S(1)}, bf16[64,7168]{1,0:T(8,128)(2,1)S(1)}) custom-call(bf16[128,512]{1,0:T(8,128)(2,1)S(1)} %expert_acts.7.acts_ref, bf16[256,7168]{1,0:T(8,128)(2,1)} %mine_ref.7, bf16[256,7168]{1,0:T(8,128)(2,1)} %collective-permute-done.6.other_ref), custom_call_target="tpu_custom_call" | custom-call | flops 939524096 | bytes 1048576 | tf_op jit(solution)/shard_map/expert_outs/pallas_call | solution.py:133
  88.3 2.9 %collective-permute-start.11 = (bf16[64,7168]{1,0:T(8,128)(2,1)S(1)}, bf16[64,7168]{1,0:T(8,128)(2,1)S(1)}, u32[]{:S(2)}, u32[]{:S(2)}) collective-permute-start(bf16[64,7168]{1,0:T(8,128)(2,1)S(1)} %get-tuple-element.43), channel_id=1, source_target_pairs={{0,3},{1,0},{2,1},{3,2},{4,7},{5,4},{6,5},{7,6},{8,11},{9,8},{10,9... | collective-permute-start | bytes 2752520 | tf_op jit(solution)/shard_map/ppermute | solution.py:55
  91.1 4.4 %expert_outs.7 = (bf16[64,7168]{1,0:T(8,128)(2,1)S(1)}, bf16[64,7168]{1,0:T(8,128)(2,1)S(1)}) custom-call(bf16[128,512]{1,0:T(8,128)(2,1)S(1)} %expert_acts.5.acts_ref, bf16[256,7168]{1,0:T(8,128)(2,1)} %mine_ref.7, bf16[256,7168]{1,0:T(8,128)(2,1)} %collective-permute-done.6.other_ref), custom_call_target="tpu_custom_call" | custom-call | flops 939524096 | bytes 1048576 | tf_op jit(solution)/shard_map/expert_outs/pallas_call | solution.py:133
  95.5 4.3 %expert_outs.6 = (bf16[64,7168]{1,0:T(8,128)(2,1)S(1)}, bf16[64,7168]{1,0:T(8,128)(2,1)S(1)}) custom-call(bf16[128,512]{1,0:T(8,128)(2,1)S(1)} %expert_acts.4.acts_ref, bf16[256,7168]{1,0:T(8,128)(2,1)} %mine_ref.7, bf16[256,7168]{1,0:T(8,128)(2,1)} %collective-permute-done.6.other_ref), custom_call_target="tpu_custom_call" | custom-call | flops 939524096 | bytes 1048576 | tf_op jit(solution)/shard_map/expert_outs/pallas_call | solution.py:133
  99.8 1.7 %collective-permute-done.11 = bf16[64,7168]{1,0:T(8,128)(2,1)S(1)} collective-permute-done((bf16[64,7168]{1,0:T(8,128)(2,1)S(1)}, bf16[64,7168]{1,0:T(8,128)(2,1)S(1)}, u32[]{:S(2)}, u32[]{:S(2)}) %collective-permute-start.11) | collective-permute-done | bytes 917536 | tf_op jit(solution)/shard_map/ppermute | solution.py:55
  101.7 3.5 %collective-permute-start.12 = (bf16[64,7168]{1,0:T(8,128)(2,1)S(1)}, bf16[64,7168]{1,0:T(8,128)(2,1)S(1)}, u32[]{:S(2)}, u32[]{:S(2)}) collective-permute-start(bf16[64,7168]{1,0:T(8,128)(2,1)S(1)} %add_convert_fusion.4), channel_id=1, source_target_pairs={{0,3},{1,0},{2,1},{3,2},{4,7},{5,4},{6,5},{7,6},{8,11},{9,8},{10,9... | collective-permute-start | bytes 2752520 | tf_op jit(solution)/shard_map/ppermute | solution.py:55
  105.5 10.0 %collective-permute-done.12 = bf16[64,7168]{1,0:T(8,128)(2,1)S(1)} collective-permute-done((bf16[64,7168]{1,0:T(8,128)(2,1)S(1)}, bf16[64,7168]{1,0:T(8,128)(2,1)S(1)}, u32[]{:S(2)}, u32[]{:S(2)}) %collective-permute-start.12) | collective-permute-done | bytes 917536 | tf_op jit(solution)/shard_map/ppermute | solution.py:55
  115.8 3.4 %collective-permute-done.14 = bf16[64,7168]{1,0:T(8,128)(2,1)S(1)} collective-permute-done((bf16[64,7168]{1,0:T(8,128)(2,1)S(1)}, bf16[64,7168]{1,0:T(8,128)(2,1)S(1)}, u32[]{:S(2)}, u32[]{:S(2)}) %collective-permute-start.14) | collective-permute-done | bytes 917536 | tf_op jit(solution)/shard_map/ppermute | solution.py:55
  120.9 3.8 %all-to-all-start.1 = ((bf16[16,8,7168]{2,1,0:T(8,128)(2,1)}), bf16[16,8,7168]{2,1,0:T(8,128)(2,1)S(1)}, u32[]{:S(2)}, u32[]{:S(2)}) async-start(bf16[16,8,7168]{2,1,0:T(8,128)(2,1)} %maximum_bitcast_fusion), calls=%async_computation.1 | async-start | bytes 3670016 | tf_op jit(solution)/shard_map/all_to_all | solution.py:65
  124.9 3.3 %fusion.35 = (f32[8,128]{1,0:T(8,128)S(1)}, f32[8,128,256]{2,1,0:T(8,128)}) fusion(bf16[8,128,576]{1,2,0:T(8,128)(2,1)S(1)} %copy-done, bf16[8,256,576]{1,2,0:T(8,128)(2,1)} %param.23, pred[8,256]{1,0:T(8,128)(4,1)S(1)} %iota_compare_fusion.1), kind=kOutput, calls=%fused_computation.64 | convolution fusion | flops 302775296 | bytes 4593664 | tf_op jit(solution)/shard_map/thc,tpc->thp/dot_general | solution.py:237
  128.2 23.1 %all-to-all-done.1 = bf16[16,8,7168]{2,1,0:T(8,128)(2,1)S(1)} async-done(((bf16[16,8,7168]{2,1,0:T(8,128)(2,1)}), bf16[16,8,7168]{2,1,0:T(8,128)(2,1)S(1)}, u32[]{:S(2)}, u32[]{:S(2)}) %all-to-all-start.1) | async-done | bytes 1835040 | tf_op jit(solution)/shard_map/all_to_all | solution.py:65
  151.8 5.7 %fusion.15 = f32[8,576]{1,0:T(8,128)S(1)} fusion(bf16[7168,576]{0,1:T(8,128)(2,1)} %param.21, bf16[8,7168]{1,0:T(8,128)(2,1)S(1)} %get-tuple-element.56, f32[7168]{0:T(1024)S(1)} %copy-done.9, f32[8]{0:T(128)S(1)} %add_rsqrt_fusion.1), kind=kOutput, calls=%fused_computation.28 | convolution fusion | flops 66289664 | bytes 8419360 | tf_op jit(solution)/shard_map/dot_general | solution.py:232
  159.3 1.9 %add_convert_fusion = bf16[8,128,512]{2,1,0:T(8,128)(2,1)} fusion(bf16[8,256,576]{1,2,0:T(8,128)(2,1)S(1)} %copy-done.6, f32[8,512]{1,0:T(8,128)S(1)} %get-tuple-element.53, f32[8,128]{1,0:T(8,128)S(1)} %get-tuple-element.62, f32[8,128,256]{2,1,0:T(8,128)S(1)} %copy-done.5, f32[8,128]{1,0:T(8,128)S(1)} %get-tuple-element.61, ...), kind=kOutput, calls=%fused_computation.1 | convolution fusion | flops 270794752 | bytes 4222976 | tf_op jit(solution)/shard_map/thp,tpc->thc/dot_general | solution.py:251
  (75 shorter events, 17.6 us)
Async XLA Ops:
  0.6 124.3 %copy-start = (bf16[8,128,576]{1,2,0:T(8,128)(2,1)S(1)}, bf16[8,128,576]{1,2,0:T(8,128)(2,1)}, u32[]{:S(2)}) copy-start(bf16[8,128,576]{1,2,0:T(8,128)(2,1)} %param.25) | copy-start | bytes 3538948
  0.6 38.3 %collective-permute-start = (bf16[7168,256]{1,0:T(8,128)(2,1)}, bf16[7168,256]{1,0:T(8,128)(2,1)}, u32[]{:S(2)}, u32[]{:S(2)}) collective-permute-start(bf16[7168,256]{1,0:T(8,128)(2,1)} %refs_2_.5), channel_id=1, source_target_pairs={{0,64},{1,65},{2,66},{3,67},{4,68},{5,69},{6,70},{7,71},{8,72},{9,... | collective-permute-start | bytes 11010056 | tf_op jit(solution)/shard_map/ppermute | solution.py:71
  2.1 36.8 %collective-permute-start.1 = (bf16[7168,256]{1,0:T(8,128)(2,1)}, bf16[7168,256]{1,0:T(8,128)(2,1)}, u32[]{:S(2)}, u32[]{:S(2)}) collective-permute-start(bf16[7168,256]{1,0:T(8,128)(2,1)} %refs_4_.5), channel_id=1, source_target_pairs={{0,64},{1,65},{2,66},{3,67},{4,68},{5,69},{6,70},{7,71},{8,72},{9,... | collective-permute-start | bytes 11010056 | tf_op jit(solution)/shard_map/ppermute | solution.py:71
  39.0 30.8 %collective-permute-start.6 = (bf16[256,7168]{1,0:T(8,128)(2,1)}, bf16[256,7168]{1,0:T(8,128)(2,1)}, u32[]{:S(2)}, u32[]{:S(2)}) collective-permute-start(bf16[256,7168]{1,0:T(8,128)(2,1)} %mine_ref.7), channel_id=1, source_target_pairs={{0,64},{1,65},{2,66},{3,67},{4,68},{5,69},{6,70},{7,71},{8,72},{9,... | collective-permute-start | bytes 11010056 | tf_op jit(solution)/shard_map/ppermute | solution.py:71
  40.4 14.8 %collective-permute-start.2 = (bf16[8,8,7296]{2,1,0:T(8,128)(2,1)}, bf16[8,8,7296]{2,1,0:T(8,128)(2,1)}, u32[]{:S(2)}, u32[]{:S(2)}) collective-permute-start(bf16[8,8,7296]{2,1,0:T(8,128)(2,1)} %get-tuple-element.58), channel_id=1, source_target_pairs={{0,1},{1,2},{2,3},{3,0},{4,5},{5,6},{6,7},{7,4},{8,9},{9,10},{10,1... | collective-permute-start | bytes 2801672 | tf_op jit(solution)/shard_map/ppermute | solution.py:55
  41.6 13.6 %collective-permute-start.3 = (bf16[8,8,7296]{2,1,0:T(8,128)(2,1)}, bf16[8,8,7296]{2,1,0:T(8,128)(2,1)}, u32[]{:S(2)}, u32[]{:S(2)}) collective-permute-start(bf16[8,8,7296]{2,1,0:T(8,128)(2,1)} %get-tuple-element.57), channel_id=1, source_target_pairs={{0,3},{1,0},{2,1},{3,2},{4,7},{5,4},{6,5},{7,6},{8,11},{9,8},{10,9... | collective-permute-start | bytes 2801672 | tf_op jit(solution)/shard_map/ppermute | solution.py:55
  43.0 21.5 %collective-permute-start.4 = (bf16[8,8,7296]{2,1,0:T(8,128)(2,1)}, bf16[8,8,7296]{2,1,0:T(8,128)(2,1)S(1)}, u32[]{:S(2)}, u32[]{:S(2)}) collective-permute-start(bf16[8,8,7296]{2,1,0:T(8,128)(2,1)} %get-tuple-element.57), channel_id=1, source_target_pairs={{0,1},{1,2},{2,3},{3,0},{4,5},{5,6},{6,7},{7,4},{8,9},{9,10},{10,1... | collective-permute-start | bytes 2801672 | tf_op jit(solution)/shard_map/ppermute | solution.py:55
  43.0 21.5 %collective-permute-start.5 = (bf16[8,8,7296]{2,1,0:T(8,128)(2,1)}, bf16[8,8,7296]{2,1,0:T(8,128)(2,1)S(1)}, u32[]{:S(2)}, u32[]{:S(2)}) collective-permute-start(bf16[8,8,7296]{2,1,0:T(8,128)(2,1)} %get-tuple-element.58), channel_id=1, source_target_pairs={{0,3},{1,0},{2,1},{3,2},{4,7},{5,4},{6,5},{7,6},{8,11},{9,8},{10,9... | collective-permute-start | bytes 2801672 | tf_op jit(solution)/shard_map/ppermute | solution.py:55
  55.2 19.3 %collective-permute-start.7 = (bf16[8,8,7296]{2,1,0:T(8,128)(2,1)}, bf16[8,8,7296]{2,1,0:T(8,128)(2,1)S(1)}, u32[]{:S(2)}, u32[]{:S(2)}) collective-permute-start(bf16[8,8,7296]{2,1,0:T(8,128)(2,1)} %collective-permute-done.2), channel_id=1, source_target_pairs={{0,1},{1,2},{2,3},{3,0},{4,5},{5,6},{6,7},{7,4},{8,9},{9,10},{10,1... | collective-permute-start | bytes 2801672 | tf_op jit(solution)/shard_map/ppermute | solution.py:55
  55.8 18.7 %collective-permute-start.8 = (bf16[8,8,7296]{2,1,0:T(8,128)(2,1)}, bf16[8,8,7296]{2,1,0:T(8,128)(2,1)S(1)}, u32[]{:S(2)}, u32[]{:S(2)}) collective-permute-start(bf16[8,8,7296]{2,1,0:T(8,128)(2,1)} %collective-permute-done.3), channel_id=1, source_target_pairs={{0,3},{1,0},{2,1},{3,2},{4,7},{5,4},{6,5},{7,6},{8,11},{9,8},{10,9... | collective-permute-start | bytes 2801672 | tf_op jit(solution)/shard_map/ppermute | solution.py:55
  69.8 7.6 %copy-start.2 = (bf16[7168,256]{1,0:T(8,128)(2,1)S(1)}, bf16[7168,256]{1,0:T(8,128)(2,1)}, u32[]{:S(2)}) copy-start(bf16[7168,256]{1,0:T(8,128)(2,1)} %refs_2_.5) | copy-start | bytes 11010052
  69.8 7.5 %copy-start.4 = (bf16[7168,256]{1,0:T(8,128)(2,1)S(1)}, bf16[7168,256]{1,0:T(8,128)(2,1)}, u32[]{:S(2)}) copy-start(bf16[7168,256]{1,0:T(8,128)(2,1)} %refs_4_.5) | copy-start | bytes 11010052
  74.5 13.8 %collective-permute-start.10 = (bf16[64,7168]{1,0:T(8,128)(2,1)S(1)}, bf16[64,7168]{1,0:T(8,128)(2,1)S(1)}, u32[]{:S(2)}, u32[]{:S(2)}) collective-permute-start(bf16[64,7168]{1,0:T(8,128)(2,1)S(1)} %get-tuple-element.42), channel_id=1, source_target_pairs={{0,1},{1,2},{2,3},{3,0},{4,5},{5,6},{6,7},{7,4},{8,9},{9,10},{10,1... | collective-permute-start | bytes 2752520 | tf_op jit(solution)/shard_map/ppermute | solution.py:55
  75.7 12.5 %collective-permute-start.9 = (bf16[64,7168]{1,0:T(8,128)(2,1)S(1)}, bf16[64,7168]{1,0:T(8,128)(2,1)S(1)}, u32[]{:S(2)}, u32[]{:S(2)}) collective-permute-start(bf16[64,7168]{1,0:T(8,128)(2,1)S(1)} %get-tuple-element.41), channel_id=1, source_target_pairs={{0,3},{1,0},{2,1},{3,2},{4,7},{5,4},{6,5},{7,6},{8,11},{9,8},{10,9... | collective-permute-start | bytes 2752520 | tf_op jit(solution)/shard_map/ppermute | solution.py:55
  88.3 13.2 %collective-permute-start.11 = (bf16[64,7168]{1,0:T(8,128)(2,1)S(1)}, bf16[64,7168]{1,0:T(8,128)(2,1)S(1)}, u32[]{:S(2)}, u32[]{:S(2)}) collective-permute-start(bf16[64,7168]{1,0:T(8,128)(2,1)S(1)} %get-tuple-element.43), channel_id=1, source_target_pairs={{0,3},{1,0},{2,1},{3,2},{4,7},{5,4},{6,5},{7,6},{8,11},{9,8},{10,9... | collective-permute-start | bytes 2752520 | tf_op jit(solution)/shard_map/ppermute | solution.py:55
  91.1 14.0 %collective-permute-start.13 = (bf16[64,7168]{1,0:T(8,128)(2,1)S(1)}, bf16[64,7168]{1,0:T(8,128)(2,1)S(1)}, u32[]{:S(2)}, u32[]{:S(2)}) collective-permute-start(bf16[64,7168]{1,0:T(8,128)(2,1)S(1)} %get-tuple-element.52), channel_id=1, source_target_pairs={{0,1},{1,2},{2,3},{3,0},{4,5},{5,6},{6,7},{7,4},{8,9},{9,10},{10,1... | collective-permute-start | bytes 2752520 | tf_op jit(solution)/shard_map/ppermute | solution.py:55
  101.7 13.8 %collective-permute-start.12 = (bf16[64,7168]{1,0:T(8,128)(2,1)S(1)}, bf16[64,7168]{1,0:T(8,128)(2,1)S(1)}, u32[]{:S(2)}, u32[]{:S(2)}) collective-permute-start(bf16[64,7168]{1,0:T(8,128)(2,1)S(1)} %add_convert_fusion.4), channel_id=1, source_target_pairs={{0,3},{1,0},{2,1},{3,2},{4,7},{5,4},{6,5},{7,6},{8,11},{9,8},{10,9... | collective-permute-start | bytes 2752520 | tf_op jit(solution)/shard_map/ppermute | solution.py:55
  105.4 13.8 %collective-permute-start.14 = (bf16[64,7168]{1,0:T(8,128)(2,1)S(1)}, bf16[64,7168]{1,0:T(8,128)(2,1)S(1)}, u32[]{:S(2)}, u32[]{:S(2)}) collective-permute-start(bf16[64,7168]{1,0:T(8,128)(2,1)S(1)} %add_convert_fusion.2), channel_id=1, source_target_pairs={{0,1},{1,2},{2,3},{3,0},{4,5},{5,6},{6,7},{7,4},{8,9},{9,10},{10,1... | collective-permute-start | bytes 2752520 | tf_op jit(solution)/shard_map/ppermute | solution.py:55
  120.9 30.4 %all-to-all-start.1 = ((bf16[16,8,7168]{2,1,0:T(8,128)(2,1)}), bf16[16,8,7168]{2,1,0:T(8,128)(2,1)S(1)}, u32[]{:S(2)}, u32[]{:S(2)}) async-start(bf16[16,8,7168]{2,1,0:T(8,128)(2,1)} %maximum_bitcast_fusion), calls=%async_computation.1 | async-start | bytes 3670016 | tf_op jit(solution)/shard_map/all_to_all | solution.py:65
  128.2 23.3 %copy-start.7 = (bf16[8,7168]{1,0:T(8,128)(2,1)S(1)}, bf16[8,7168]{1,0:T(8,128)(2,1)}, u32[]{:S(2)}) copy-start(bf16[8,7168]{1,0:T(8,128)(2,1)} %param.13) | copy-start | bytes 344068
  128.2 23.6 %copy-start.9 = (f32[7168]{0:T(1024)S(1)}, f32[7168]{0:T(1024)}, u32[]{:S(2)}) copy-start(f32[7168]{0:T(1024)} %param.20) | copy-start | bytes 86020
  151.7 5.8 %copy-start.8 = (bf16[8,7168]{1,0:T(8,128)(2,1)}, bf16[8,7168]{1,0:T(8,128)(2,1)S(1)}, u32[]{:S(2)}) copy-start(bf16[8,7168]{1,0:T(8,128)(2,1)S(1)} %get-tuple-element.56) | copy-start | bytes 344068
  151.8 5.9 %copy-start.10 = (f32[512]{0:T(512)S(1)}, f32[512]{0:T(512)}, u32[]{:S(2)}) copy-start(f32[512]{0:T(512)} %param.22) | copy-start | bytes 6148
  151.8 7.5 %copy-start.6 = (bf16[8,256,576]{1,2,0:T(8,128)(2,1)S(1)}, bf16[8,256,576]{1,2,0:T(8,128)(2,1)}, u32[]{:S(2)}) copy-start(bf16[8,256,576]{1,2,0:T(8,128)(2,1)} %param.23) | copy-start | bytes 7077892
  (4 other events, 9.3 us)

commit v2 on v0

--- a/solution.py
+++ b/solution.py
@@ -96,7 +96,7 @@
 
 
 def act_body(info_ref, *refs):
-    rows, weights, out_ref = refs[:SIDE], refs[SIDE : 2 * SIDE], refs[2 * SIDE]
+    rows, weights, out_ref = refs[:-5], refs[-5:-1], refs[-1]
     depth, wide = weights[0].shape
     held = jnp.concatenate([part[:, depth:] for part in rows], axis=0).astype(jnp.float32)
     lane = lax.broadcasted_iota(jnp.int32, (1, LANES), 1)
@@ -116,15 +116,15 @@
 
 
 def expert_acts(info, rows, weights):
-    tokens = SIDE * rows[0].shape[0]
+    tokens = sum(part.shape[0] for part in rows)
     depth, wide = weights[0].shape
     vmem = pl.BlockSpec(memory_space=pltpu.VMEM)
     return pl.pallas_call(
         act_body,
         out_shape=jax.ShapeDtypeStruct((tokens, 2 * wide), jnp.bfloat16),
-        in_specs=[pl.BlockSpec(memory_space=pltpu.SMEM)] + [vmem] * (2 * SIDE),
+        in_specs=[pl.BlockSpec(memory_space=pltpu.SMEM)] + [vmem] * (len(rows) + 4),
         out_specs=vmem,
-        compiler_params=pltpu.CompilerParams(vmem_limit_bytes=30 << 20),
+        compiler_params=pltpu.CompilerParams(vmem_limit_bytes=18 << 20),
         cost_estimate=pl.CostEstimate(
             flops=8 * tokens * depth * wide, bytes_accessed=1 << 20, transcendentals=0
         ),
@@ -134,30 +134,28 @@
 
 def down_body(acts_ref, mine_ref, other_ref, *outs):
     wide = mine_ref.shape[0]
-    group = acts_ref.shape[0] // SIDE
-    step = 2 * LANES
+    group = outs[0].shape[0]
+    step = 4 * LANES
     for low in range(0, mine_ref.shape[1], step):
         high = low + step
         part = jnp.dot(
             acts_ref[:, :wide], mine_ref[:, low:high], preferred_element_type=jnp.float32
         ) + jnp.dot(acts_ref[:, wide:], other_ref[:, low:high], preferred_element_type=jnp.float32)
         part = part.astype(jnp.bfloat16)
-        for back in range(SIDE):
-            outs[back][:, low:high] = part[back * group : (back + 1) * group]
-
-
-def expert_outs(acts, mine, other):
+        for number, out in enumerate(outs):
+            out[:, low:high] = part[number * group : (number + 1) * group]
+
+
+def expert_outs(acts, mine, other, count):
     tokens, both = acts.shape
-    group, width, steps = tokens // SIDE, mine.shape[1], 4
-    block = width // steps
-    spec = pl.BlockSpec((both // 2, block), lambda i: (0, i))
+    width = mine.shape[1]
+    vmem = pl.BlockSpec(memory_space=pltpu.VMEM)
     return pl.pallas_call(
         down_body,
-        grid=(steps,),
-        out_shape=[jax.ShapeDtypeStruct((group, width), jnp.bfloat16)] * SIDE,
-        in_specs=[pl.BlockSpec((tokens, both), lambda i: (0, 0)), spec, spec],
-        out_specs=[pl.BlockSpec((group, block), lambda i: (0, i))] * SIDE,
-        compiler_params=pltpu.CompilerParams(vmem_limit_bytes=12 << 20),
+        out_shape=[jax.ShapeDtypeStruct((tokens // count, width), jnp.bfloat16)] * count,
+        in_specs=[vmem] * 3,
+        out_specs=[vmem] * count,
+        compiler_params=pltpu.CompilerParams(vmem_limit_bytes=18 << 20),
         cost_estimate=pl.CostEstimate(
             flops=2 * tokens * both * width, bytes_accessed=1 << 20, transcendentals=0
         ),
@@ -208,36 +206,53 @@
     weight_cols = jnp.concatenate(
         [high, middle, low, jnp.zeros((tok_count, LANES - 3 * EXPERTS), jnp.bfloat16)], axis=1
     )
-    rows = jnp.concatenate([normed, weight_cols], axis=1)[None]
-    got = [rows] + [shift(rows, 0, back) for back in range(1, SIDE)]
-    (rows,) = join(lax.optimization_barrier((got, gate_other))[0], 1)
-    up_other = swap_cores(after(w_up, rows))
+    rows = jnp.concatenate([normed, weight_cols], axis=1)
+    up_other = swap_cores(w_up)
+    rows = rows[None]
+    (rows,) = join([rows] + [shift(rows, 0, back) for back in range(1, SIDE)], 1)
     got = [rows] + [shift(rows, 1, back) for back in range(1, SIDE)]
-    low, high = join(lax.optimization_barrier((got, up_other))[0], 2)
+    low, high = join(lax.optimization_barrier((got, gate_other, up_other))[0], 2)
     down_other = swap_cores(after(w_down, low))
     low_back, high_ahead = shift(low, 2, 1), shift(high, 2, -1)
     high_back, low_ahead = shift(high, 2, 1), shift(low, 2, -1)
-    low_far, high_far = shift(low_back, 2, 1), shift(high_ahead, 2, -1)
 
     half = EXPERTS // 2
     info = jnp.stack([chip_expert + sec * half, chip_expert + (1 - sec) * half]).astype(jnp.int32)
     weights = (w_gate, gate_other, w_up, up_other)
 
-    def flat(*parts):
-        return [part.reshape(-1, part.shape[-1]) for part in parts]
-
-    acts = expert_acts(info, flat(low, high, low_back, high_ahead), weights)
-    low_mine, high_mine, low_back, high_ahead = expert_outs(acts, w_down, down_other)
-    info = after(info, low_mine)
-    acts = expert_acts(info, flat(high_back, low_ahead, low_far, high_far), weights)
-    high_back, low_ahead, low_far, high_far = expert_outs(acts, w_down, down_other)
-
+    def acts_of(number, *parts):
+        return expert_acts(number, [part.reshape(-1, part.shape[-1]) for part in parts], weights)
+
+    def outs_of(acts):
+        return expert_outs(acts, w_down, down_other, 2)
+
+    mine_acts = acts_of(info, low, high)
+    low_back, high_ahead = lax.optimization_barrier((low_back, high_ahead, mine_acts))[:2]
+    low_far, high_far = shift(low_back, 2, 1), shift(high_ahead, 2, -1)
+    near_rows = (low_back, high_ahead)
+    high_back, low_ahead = outs_of(acts_of(info, high_back, low_ahead))
+    high_back, low_ahead, low_far, high_far = lax.optimization_barrier(
+        (high_back, low_ahead, low_far, high_far)
+    )
+    high_back, low_ahead = shift(high_back, 2, -1), shift(low_ahead, 2, 1)
+    low_far, high_far = outs_of(acts_of(info, low_far, high_far))
+    near_info = after(info, low_far)
+    low_far, high_far, high_back, low_ahead = lax.optimization_barrier(
+        (low_far, high_far, high_back, low_ahead)
+    )
     low_far, high_far = shift(low_far, 2, -1), shift(high_far, 2, 1)
-    high_back, low_ahead = shift(high_back, 2, -1), shift(low_ahead, 2, 1)
-    low_back = shift(plus(low_back, low_far).astype(jnp.bfloat16), 2, -1)
-    high_ahead = shift(plus(high_ahead, high_far).astype(jnp.bfloat16), 2, 1)
+    low_back, high_ahead = outs_of(acts_of(near_info, *near_rows))
+    low_mine, high_mine = outs_of(after(mine_acts, low_back))
+    low_back, high_ahead = lax.optimization_barrier(
+        (
+            plus(low_back, low_far).astype(jnp.bfloat16),
+            plus(high_ahead, high_far).astype(jnp.bfloat16),
+        )
+    )
+    low_back, high_ahead = shift(low_back, 2, -1), shift(high_ahead, 2, 1)
     low = plus(low_mine, low_back, low_ahead).astype(jnp.bfloat16)
     high = plus(high_mine, high_back, high_ahead).astype(jnp.bfloat16)
+    low, high = lax.optimization_barrier((low, high))
     parts = [*jnp.split(low, 2, axis=0), *jnp.split(high, 2, axis=0)]
     for phase in (1, 0):
         moe = plus(parts[0], *(shift(parts[back], phase, -back) for back in range(1, SIDE)))

time: 166 us -> 164 us (0.988)
  waiting for transfers between devices: 76.8 us -> 62.5 us
  Pallas kernels: 25.7 us -> 36.7 us
  starting transfers between devices: 40.3 us -> 44.9 us
  local copies, waits for them, and re-layouts: 8.32 us -> 4.35 us
    ppermute x24, waiting for transfers between devices: 76.8 us -> 62.5 us  [shift(): return lax.ppermute(values, AXES, pairs)]
    pallas_call x2 -> x4, Pallas kernels: 13.9 us -> 22 us  [expert_acts(): pl.pallas_call(act_body, out_shape=jax.ShapeDtypeStruct((tokens, 2 * wide...]
    ppermute x24, starting transfers between devices: 39.8 us -> 44.2 us  [shift(): return lax.ppermute(values, AXES, pairs)]
    unnamed x32 -> x28, local copies, waits for them, and re-layouts: 8.11 us -> 4.14 us
    pallas_call x2 -> x4, Pallas kernels: 10 us -> 12.8 us  [expert_outs(): pl.pallas_call(down_body, out_shape=[jax.ShapeDtypeStruct((tokens // coun...]
  transfers between devices with their start and end apart: 27 -> 27, of which waited for: 15 -> 17; matrix products, arithmetic and copies ran while one was open for 3% -> 3% of each run, Pallas kernels for 7% -> 22%
where the time goes in v2:
time: 164 us; the launch traced here: 161 us
  waiting for transfers between devices  62.5 us (38%)
  starting transfers between devices  44.9 us (27%)
  Pallas kernels  36.7 us (22%)
  other arithmetic  6.06 us (4%)
  matrix products  5.13 us (3%)
  local copies, waits for them, and re-layouts  4.35 us (3%)
    ppermute x24, waiting for transfers between devices, shift(): return lax.ppermute(values, AXES, pairs)  62.5 us
    ppermute x24, starting transfers between devices, shift(): return lax.ppermute(values, AXES, pairs)  44.2 us
    pallas_call x4, Pallas kernels, expert_acts(): pl.pallas_call(act_body, out_shape=jax.ShapeDtypeStruct((tokens, 2 * wide...  22 us
    pallas_call x4, Pallas kernels, expert_outs(): pl.pallas_call(down_body, out_shape=[jax.ShapeDtypeStruct((tokens // coun...  12.8 us
    unnamed x28, local copies, waits for them, and re-layouts  4.14 us
  transfers between devices with their start and end apart: 27, of which 17 were waited for; matrix products, arithmetic and copies ran while one was open for 3% of the time, Pallas kernels for 22%

profile of v2, /device:TPU:2, one launch (start us, length us, event | category | flops | bytes accessed | tf_op | source)
XLA Modules:
  0.0 160.7 jit_solution(14536737860754892752)
XLA Ops:
  9.0 3.1 %collective-permute-done.1.refs_2_ = bf16[1,8,7296]{2,1,0:T(8,128)(2,1)S(1)} collective-permute-done((bf16[1,8,7296]{2,1,0:T(8,128)(2,1)S(1)}, bf16[1,8,7296]{2,1,0:T(8,128)(2,1)S(1)}, u32[]{:S(2)}, u32[]{:S(2)}) %collective-permute-start.1) | collective-permute-done | bytes 116768 | tf_op jit(solution)/shard_map/ppermute | solution.py:54
  15.2 2.9 %collective-permute-start.4 = (bf16[4,8,7296]{2,1,0:T(8,128)(2,1)S(1)}, bf16[4,8,7296]{2,1,0:T(8,128)(2,1)S(1)}, u32[]{:S(2)}, u32[]{:S(2)}) collective-permute-start(bf16[4,8,7296]{2,1,0:T(8,128)(2,1)S(1)} %join.2.refs_0_), channel_id=1, source_target_pairs={{0,8},{1,9},{2,10},{3,11},{4,12},{5,13},{6,14},{7,15},{8,0},{9,1},... | collective-permute-start | bytes 1400840 | tf_op jit(solution)/shard_map/ppermute | solution.py:54
  19.4 3.9 %collective-permute-done.3.refs_1_ = bf16[4,8,7296]{2,1,0:T(8,128)(2,1)S(1)} collective-permute-done((bf16[4,8,7296]{2,1,0:T(8,128)(2,1)S(1)}, bf16[4,8,7296]{2,1,0:T(8,128)(2,1)S(1)}, u32[]{:S(2)}, u32[]{:S(2)}) %collective-permute-start.3) | collective-permute-done | bytes 466976 | tf_op jit(solution)/shard_map/ppermute | solution.py:54
  23.3 6.3 %collective-permute-done.4.refs_2_ = bf16[4,8,7296]{2,1,0:T(8,128)(2,1)S(1)} collective-permute-done((bf16[4,8,7296]{2,1,0:T(8,128)(2,1)S(1)}, bf16[4,8,7296]{2,1,0:T(8,128)(2,1)S(1)}, u32[]{:S(2)}, u32[]{:S(2)}) %collective-permute-start.4) | collective-permute-done | bytes 466976 | tf_op jit(solution)/shard_map/ppermute | solution.py:54
  35.2 3.2 %collective-permute-start.9 = (bf16[8,8,7296]{2,1,0:T(8,128)(2,1)}, bf16[8,8,7296]{2,1,0:T(8,128)(2,1)S(1)}, u32[]{:S(2)}, u32[]{:S(2)}) collective-permute-start(bf16[8,8,7296]{2,1,0:T(8,128)(2,1)} %get-tuple-element.38), channel_id=1, source_target_pairs={{0,3},{1,0},{2,1},{3,2},{4,7},{5,4},{6,5},{7,6},{8,11},{9,8},{10,9... | collective-permute-start | bytes 2801672 | tf_op jit(solution)/shard_map/ppermute | solution.py:54
  42.6 6.0 %expert_acts.4.acts_ref = bf16[128,512]{1,0:T(8,128)(2,1)S(1)} custom-call(s32[2]{0:T(128)S(1)} %pad_add_fusion.info_ref, bf16[64,7296]{1,0:T(8,128)(2,1)} %bitcast.3.refs_0_, bf16[64,7296]{1,0:T(8,128)(2,1)} %bitcast.4.refs_1_, bf16[7168,256]{1,0:T(8,128)(2,1)S(1)} %copy-done.1, bf16[7168,256]{1,0:T(8,128)(2,1)} %collective-permute-done.6.refs_3_, ...), custom_call_target="tpu_custom_call" | custom-call | flops 1879048192 | bytes 1048576 | tf_op jit(solution)/shard_map/expert_acts/pallas_call | solution.py:122
  48.7 3.2 %collective-permute-start.14 = (bf16[8,8,7296]{2,1,0:T(8,128)(2,1)S(1)}, bf16[8,8,7296]{2,1,0:T(8,128)(2,1)S(1)}, u32[]{:S(2)}, u32[]{:S(2)}) collective-permute-start(bf16[8,8,7296]{2,1,0:T(8,128)(2,1)S(1)} %collective-permute-done.12), channel_id=1, source_target_pairs={{0,3},{1,0},{2,1},{3,2},{4,7},{5,4},{6,5},{7,6},{8,11},{9,8},{10,9... | collective-permute-start | bytes 2801672 | tf_op jit(solution)/shard_map/ppermute | solution.py:54
  51.9 5.0 %collective-permute-done.8 = bf16[8,8,7296]{2,1,0:T(8,128)(2,1)S(1)} collective-permute-done((bf16[8,8,7296]{2,1,0:T(8,128)(2,1)}, bf16[8,8,7296]{2,1,0:T(8,128)(2,1)S(1)}, u32[]{:S(2)}, u32[]{:S(2)}) %collective-permute-start.8) | collective-permute-done | bytes 933920 | tf_op jit(solution)/shard_map/ppermute | solution.py:54
  56.9 5.4 %expert_acts.5.acts_ref = bf16[128,512]{1,0:T(8,128)(2,1)S(1)} custom-call(s32[2]{0:T(128)S(1)} %pad_add_fusion.info_ref, bf16[64,7296]{1,0:T(8,128)(2,1)S(1)} %bitcast.23, bf16[64,7296]{1,0:T(8,128)(2,1)S(1)} %bitcast.24, bf16[7168,256]{1,0:T(8,128)(2,1)S(1)} %copy-done.2, bf16[7168,256]{1,0:T(8,128)(2,1)} %collective-permute-done.6.refs_3_, ...), custom_call_target="tpu_custom_call" | custom-call | flops 1879048192 | bytes 1048576 | tf_op jit(solution)/shard_map/expert_acts/pallas_call | solution.py:122
  62.4 3.2 %expert_outs.4 = (bf16[64,7168]{1,0:T(8,128)(2,1)S(1)}, bf16[64,7168]{1,0:T(8,128)(2,1)S(1)}) custom-call(bf16[128,512]{1,0:T(8,128)(2,1)S(1)} %expert_acts.5.acts_ref, bf16[256,7168]{1,0:T(8,128)(2,1)S(1)} %copy-done.5, bf16[256,7168]{1,0:T(8,128)(2,1)} %collective-permute-done.10.other_ref), custom_call_target="tpu_custom_call" | custom-call | flops 939524096 | bytes 1048576 | tf_op jit(solution)/shard_map/expert_outs/pallas_call | solution.py:153
  66.9 3.3 %collective-permute-start.15 = (bf16[64,7168]{1,0:T(8,128)(2,1)S(1)}, bf16[64,7168]{1,0:T(8,128)(2,1)S(1)}, u32[]{:S(2)}, u32[]{:S(2)}) collective-permute-start(bf16[64,7168]{1,0:T(8,128)(2,1)S(1)} %get-tuple-element.53), channel_id=1, source_target_pairs={{0,3},{1,0},{2,1},{3,2},{4,7},{5,4},{6,5},{7,6},{8,11},{9,8},{10,9... | collective-permute-start | bytes 2752520 | tf_op jit(solution)/shard_map/ppermute | solution.py:54
  70.2 5.3 %expert_acts.6.acts_ref = bf16[128,512]{1,0:T(8,128)(2,1)S(1)} custom-call(s32[2]{0:T(128)S(1)} %pad_add_fusion.info_ref, bf16[64,7296]{1,0:T(8,128)(2,1)S(1)} %bitcast.21, bf16[64,7296]{1,0:T(8,128)(2,1)S(1)} %bitcast.22, bf16[7168,256]{1,0:T(8,128)(2,1)S(1)} %copy-done.2, bf16[7168,256]{1,0:T(8,128)(2,1)} %collective-permute-done.6.refs_3_, ...), custom_call_target="tpu_custom_call" | custom-call | flops 1879048192 | bytes 1048576 | tf_op jit(solution)/shard_map/expert_acts/pallas_call | solution.py:122
  75.5 3.2 %expert_outs.5 = (bf16[64,7168]{1,0:T(8,128)(2,1)S(1)}, bf16[64,7168]{1,0:T(8,128)(2,1)S(1)}) custom-call(bf16[128,512]{1,0:T(8,128)(2,1)S(1)} %expert_acts.6.acts_ref, bf16[256,7168]{1,0:T(8,128)(2,1)S(1)} %copy-done.5, bf16[256,7168]{1,0:T(8,128)(2,1)} %collective-permute-done.10.other_ref), custom_call_target="tpu_custom_call" | custom-call | flops 939524096 | bytes 1048576 | tf_op jit(solution)/shard_map/expert_outs/pallas_call | solution.py:153
  81.1 3.7 %collective-permute-done.16 = bf16[64,7168]{1,0:T(8,128)(2,1)S(1)} collective-permute-done((bf16[64,7168]{1,0:T(8,128)(2,1)S(1)}, bf16[64,7168]{1,0:T(8,128)(2,1)S(1)}, u32[]{:S(2)}, u32[]{:S(2)}) %collective-permute-start.16) | collective-permute-done | bytes 917536 | tf_op jit(solution)/shard_map/ppermute | solution.py:54
  84.8 5.3 %expert_acts.7.acts_ref = bf16[128,512]{1,0:T(8,128)(2,1)S(1)} custom-call(s32[2]{0:T(128)S(1)} %pad_add_fusion.info_ref, bf16[64,7296]{1,0:T(8,128)(2,1)S(1)} %bitcast.19, bf16[64,7296]{1,0:T(8,128)(2,1)S(1)} %bitcast.20, bf16[7168,256]{1,0:T(8,128)(2,1)S(1)} %copy-done.2, bf16[7168,256]{1,0:T(8,128)(2,1)} %collective-permute-done.6.refs_3_, ...), custom_call_target="tpu_custom_call" | custom-call | flops 1879048192 | bytes 1048576 | tf_op jit(solution)/shard_map/expert_acts/pallas_call | solution.py:122
  90.1 3.2 %expert_outs.6 = (bf16[64,7168]{1,0:T(8,128)(2,1)S(1)}, bf16[64,7168]{1,0:T(8,128)(2,1)S(1)}) custom-call(bf16[128,512]{1,0:T(8,128)(2,1)S(1)} %expert_acts.7.acts_ref, bf16[256,7168]{1,0:T(8,128)(2,1)S(1)} %copy-done.5, bf16[256,7168]{1,0:T(8,128)(2,1)} %collective-permute-done.10.other_ref), custom_call_target="tpu_custom_call" | custom-call | flops 939524096 | bytes 1048576 | tf_op jit(solution)/shard_map/expert_outs/pallas_call | solution.py:153
  98.4 9.6 %collective-permute-done.18 = bf16[64,7168]{1,0:T(8,128)(2,1)S(1)} collective-permute-done((bf16[64,7168]{1,0:T(8,128)(2,1)S(1)}, bf16[64,7168]{1,0:T(8,128)(2,1)S(1)}, u32[]{:S(2)}, u32[]{:S(2)}) %collective-permute-start.18) | collective-permute-done | bytes 917536 | tf_op jit(solution)/shard_map/ppermute | solution.py:54
  108.3 3.2 %expert_outs.7 = (bf16[64,7168]{1,0:T(8,128)(2,1)S(1)}, bf16[64,7168]{1,0:T(8,128)(2,1)S(1)}) custom-call(bf16[128,512]{1,0:T(8,128)(2,1)S(1)} %expert_acts.4.acts_ref, bf16[256,7168]{1,0:T(8,128)(2,1)S(1)} %copy-done.5, bf16[256,7168]{1,0:T(8,128)(2,1)} %collective-permute-done.10.other_ref), custom_call_target="tpu_custom_call" | custom-call | flops 939524096 | bytes 1048576 | tf_op jit(solution)/shard_map/expert_outs/pallas_call | solution.py:153
  113.6 8.1 %collective-permute-done.19 = bf16[64,7168]{1,0:T(8,128)(2,1)S(1)} collective-permute-done((bf16[64,7168]{1,0:T(8,128)(2,1)S(1)}, bf16[64,7168]{1,0:T(8,128)(2,1)S(1)}, u32[]{:S(2)}, u32[]{:S(2)}) %collective-permute-start.19) | collective-permute-done | bytes 917536 | tf_op jit(solution)/shard_map/ppermute | solution.py:54
  122.0 4.2 %collective-permute-done.20 = bf16[64,7168]{1,0:T(8,128)(2,1)S(1)} collective-permute-done((bf16[64,7168]{1,0:T(8,128)(2,1)S(1)}, bf16[64,7168]{1,0:T(8,128)(2,1)S(1)}, u32[]{:S(2)}, u32[]{:S(2)}) %collective-permute-start.20) | collective-permute-done | bytes 917536 | tf_op jit(solution)/shard_map/ppermute | solution.py:54
  132.3 4.0 %collective-permute-done.23 = bf16[32,7168]{1,0:T(8,128)(2,1)S(1)} collective-permute-done((bf16[32,7168]{1,0:T(8,128)(2,1)S(1)}, bf16[32,7168]{1,0:T(8,128)(2,1)S(1)}, u32[]{:S(2)}, u32[]{:S(2)}) %collective-permute-start.23) | collective-permute-done | bytes 458784 | tf_op jit(solution)/shard_map/ppermute | solution.py:54
  136.4 5.5 %collective-permute-done.22 = bf16[32,7168]{1,0:T(8,128)(2,1)S(1)} collective-permute-done((bf16[32,7168]{1,0:T(8,128)(2,1)S(1)}, bf16[32,7168]{1,0:T(8,128)(2,1)S(1)}, u32[]{:S(2)}, u32[]{:S(2)}) %collective-permute-start.22) | collective-permute-done | bytes 458784 | tf_op jit(solution)/shard_map/ppermute | solution.py:54
  142.5 3.3 %collective-permute-start.26 = (bf16[8,7168]{1,0:T(8,128)(2,1)S(1)}, bf16[8,7168]{1,0:T(8,128)(2,1)S(1)}, u32[]{:S(2)}, u32[]{:S(2)}) collective-permute-start(bf16[8,7168]{1,0:T(8,128)(2,1)S(1)} %get-tuple-element.72), channel_id=1, source_target_pairs={{0,16},{1,17},{2,18},{3,19},{4,20},{5,21},{6,22},{7,23},{8,24},{9,... | collective-permute-start | bytes 344072 | tf_op jit(solution)/shard_map/ppermute | solution.py:54
  145.8 3.9 %collective-permute-start.25 = (bf16[8,7168]{1,0:T(8,128)(2,1)S(1)}, bf16[8,7168]{1,0:T(8,128)(2,1)S(1)}, u32[]{:S(2)}, u32[]{:S(2)}) collective-permute-start(bf16[8,7168]{1,0:T(8,128)(2,1)S(1)} %get-tuple-element.73), channel_id=1, source_target_pairs={{0,32},{1,33},{2,34},{3,35},{4,36},{5,37},{6,38},{7,39},{8,40},{9,... | collective-permute-start | bytes 344072 | tf_op jit(solution)/shard_map/ppermute | solution.py:54
  (103 shorter events, 51.7 us)
Async XLA Ops:
  0.6 29.0 %collective-permute-start.6 = (bf16[7168,256]{1,0:T(8,128)(2,1)}, bf16[7168,256]{1,0:T(8,128)(2,1)}, u32[]{:S(2)}, u32[]{:S(2)}) collective-permute-start(bf16[7168,256]{1,0:T(8,128)(2,1)} %refs_2_.7), channel_id=1, source_target_pairs={{0,64},{1,65},{2,66},{3,67},{4,68},{5,69},{6,70},{7,71},{8,72},{9,... | collective-permute-start | bytes 11010056 | tf_op jit(solution)/shard_map/ppermute | solution.py:58
  0.7 28.9 %collective-permute-start.7 = (bf16[7168,256]{1,0:T(8,128)(2,1)}, bf16[7168,256]{1,0:T(8,128)(2,1)}, u32[]{:S(2)}, u32[]{:S(2)}) collective-permute-start(bf16[7168,256]{1,0:T(8,128)(2,1)} %refs_4_.7), channel_id=1, source_target_pairs={{0,64},{1,65},{2,66},{3,67},{4,68},{5,69},{6,70},{7,71},{8,72},{9,... | collective-permute-start | bytes 11010056 | tf_op jit(solution)/shard_map/ppermute | solution.py:58
  5.7 6.4 %collective-permute-start.1 = (bf16[1,8,7296]{2,1,0:T(8,128)(2,1)S(1)}, bf16[1,8,7296]{2,1,0:T(8,128)(2,1)S(1)}, u32[]{:S(2)}, u32[]{:S(2)}) collective-permute-start(bf16[1,8,7296]{2,1,0:T(8,128)(2,1)S(1)} %bitcast.26), channel_id=1, source_target_pairs={{0,32},{1,33},{2,34},{3,35},{4,36},{5,37},{6,38},{7,39},{8,40},{9,... | collective-permute-start | bytes 350216 | tf_op jit(solution)/shard_map/ppermute | solution.py:54
  13.4 9.8 %collective-permute-start.3 = (bf16[4,8,7296]{2,1,0:T(8,128)(2,1)S(1)}, bf16[4,8,7296]{2,1,0:T(8,128)(2,1)S(1)}, u32[]{:S(2)}, u32[]{:S(2)}) collective-permute-start(bf16[4,8,7296]{2,1,0:T(8,128)(2,1)S(1)} %join.2.refs_0_), channel_id=1, source_target_pairs={{0,4},{1,5},{2,6},{3,7},{4,8},{5,9},{6,10},{7,11},{8,12},{9,13},{1... | collective-permute-start | bytes 1400840 | tf_op jit(solution)/shard_map/ppermute | solution.py:54
  15.2 14.4 %collective-permute-start.4 = (bf16[4,8,7296]{2,1,0:T(8,128)(2,1)S(1)}, bf16[4,8,7296]{2,1,0:T(8,128)(2,1)S(1)}, u32[]{:S(2)}, u32[]{:S(2)}) collective-permute-start(bf16[4,8,7296]{2,1,0:T(8,128)(2,1)S(1)} %join.2.refs_0_), channel_id=1, source_target_pairs={{0,8},{1,9},{2,10},{3,11},{4,12},{5,13},{6,14},{7,15},{8,0},{9,1},... | collective-permute-start | bytes 1400840 | tf_op jit(solution)/shard_map/ppermute | solution.py:54
  18.1 11.5 %collective-permute-start.5 = (bf16[4,8,7296]{2,1,0:T(8,128)(2,1)S(1)}, bf16[4,8,7296]{2,1,0:T(8,128)(2,1)S(1)}, u32[]{:S(2)}, u32[]{:S(2)}) collective-permute-start(bf16[4,8,7296]{2,1,0:T(8,128)(2,1)S(1)} %join.2.refs_0_), channel_id=1, source_target_pairs={{0,12},{1,13},{2,14},{3,15},{4,0},{5,1},{6,2},{7,3},{8,4},{9,5},{1... | collective-permute-start | bytes 1400840 | tf_op jit(solution)/shard_map/ppermute | solution.py:54
  30.9 31.4 %collective-permute-start.10 = (bf16[256,7168]{1,0:T(8,128)(2,1)}, bf16[256,7168]{1,0:T(8,128)(2,1)}, u32[]{:S(2)}, u32[]{:S(2)}) collective-permute-start(bf16[256,7168]{1,0:T(8,128)(2,1)} %mine_ref.7), channel_id=1, source_target_pairs={{0,64},{1,65},{2,66},{3,67},{4,68},{5,69},{6,70},{7,71},{8,72},{9,... | collective-permute-start | bytes 11010056 | tf_op jit(solution)/shard_map/ppermute | solution.py:58
  31.0 17.6 %collective-permute-start.11 = (bf16[8,8,7296]{2,1,0:T(8,128)(2,1)}, bf16[8,8,7296]{2,1,0:T(8,128)(2,1)S(1)}, u32[]{:S(2)}, u32[]{:S(2)}) collective-permute-start(bf16[8,8,7296]{2,1,0:T(8,128)(2,1)} %get-tuple-element.38), channel_id=1, source_target_pairs={{0,1},{1,2},{2,3},{3,0},{4,5},{5,6},{6,7},{7,4},{8,9},{9,10},{10,1... | collective-permute-start | bytes 2801672 | tf_op jit(solution)/shard_map/ppermute | solution.py:54
  33.0 15.6 %collective-permute-start.12 = (bf16[8,8,7296]{2,1,0:T(8,128)(2,1)}, bf16[8,8,7296]{2,1,0:T(8,128)(2,1)S(1)}, u32[]{:S(2)}, u32[]{:S(2)}) collective-permute-start(bf16[8,8,7296]{2,1,0:T(8,128)(2,1)} %get-tuple-element.39), channel_id=1, source_target_pairs={{0,3},{1,0},{2,1},{3,2},{4,7},{5,4},{6,5},{7,6},{8,11},{9,8},{10,9... | collective-permute-start | bytes 2801672 | tf_op jit(solution)/shard_map/ppermute | solution.py:54
  35.2 21.7 %collective-permute-start.8 = (bf16[8,8,7296]{2,1,0:T(8,128)(2,1)}, bf16[8,8,7296]{2,1,0:T(8,128)(2,1)S(1)}, u32[]{:S(2)}, u32[]{:S(2)}) collective-permute-start(bf16[8,8,7296]{2,1,0:T(8,128)(2,1)} %get-tuple-element.39), channel_id=1, source_target_pairs={{0,1},{1,2},{2,3},{3,0},{4,5},{5,6},{6,7},{7,4},{8,9},{9,10},{10,1... | collective-permute-start | bytes 2801672 | tf_op jit(solution)/shard_map/ppermute | solution.py:54
  35.2 21.7 %collective-permute-start.9 = (bf16[8,8,7296]{2,1,0:T(8,128)(2,1)}, bf16[8,8,7296]{2,1,0:T(8,128)(2,1)S(1)}, u32[]{:S(2)}, u32[]{:S(2)}) collective-permute-start(bf16[8,8,7296]{2,1,0:T(8,128)(2,1)} %get-tuple-element.38), channel_id=1, source_target_pairs={{0,3},{1,0},{2,1},{3,2},{4,7},{5,4},{6,5},{7,6},{8,11},{9,8},{10,9... | collective-permute-start | bytes 2801672 | tf_op jit(solution)/shard_map/ppermute | solution.py:54
  48.6 18.3 %collective-permute-start.13 = (bf16[8,8,7296]{2,1,0:T(8,128)(2,1)S(1)}, bf16[8,8,7296]{2,1,0:T(8,128)(2,1)S(1)}, u32[]{:S(2)}, u32[]{:S(2)}) collective-permute-start(bf16[8,8,7296]{2,1,0:T(8,128)(2,1)S(1)} %collective-permute-done.11), channel_id=1, source_target_pairs={{0,1},{1,2},{2,3},{3,0},{4,5},{5,6},{6,7},{7,4},{8,9},{9,10},{10,1... | collective-permute-start | bytes 2801672 | tf_op jit(solution)/shard_map/ppermute | solution.py:54
  48.7 18.2 %collective-permute-start.14 = (bf16[8,8,7296]{2,1,0:T(8,128)(2,1)S(1)}, bf16[8,8,7296]{2,1,0:T(8,128)(2,1)S(1)}, u32[]{:S(2)}, u32[]{:S(2)}) collective-permute-start(bf16[8,8,7296]{2,1,0:T(8,128)(2,1)S(1)} %collective-permute-done.12), channel_id=1, source_target_pairs={{0,3},{1,0},{2,1},{3,2},{4,7},{5,4},{6,5},{7,6},{8,11},{9,8},{10,9... | collective-permute-start | bytes 2801672 | tf_op jit(solution)/shard_map/ppermute | solution.py:54
  66.9 14.2 %collective-permute-start.15 = (bf16[64,7168]{1,0:T(8,128)(2,1)S(1)}, bf16[64,7168]{1,0:T(8,128)(2,1)S(1)}, u32[]{:S(2)}, u32[]{:S(2)}) collective-permute-start(bf16[64,7168]{1,0:T(8,128)(2,1)S(1)} %get-tuple-element.53), channel_id=1, source_target_pairs={{0,3},{1,0},{2,1},{3,2},{4,7},{5,4},{6,5},{7,6},{8,11},{9,8},{10,9... | collective-permute-start | bytes 2752520 | tf_op jit(solution)/shard_map/ppermute | solution.py:54
  70.2 14.6 %collective-permute-start.16 = (bf16[64,7168]{1,0:T(8,128)(2,1)S(1)}, bf16[64,7168]{1,0:T(8,128)(2,1)S(1)}, u32[]{:S(2)}, u32[]{:S(2)}) collective-permute-start(bf16[64,7168]{1,0:T(8,128)(2,1)S(1)} %get-tuple-element.54), channel_id=1, source_target_pairs={{0,1},{1,2},{2,3},{3,0},{4,5},{5,6},{6,7},{7,4},{8,9},{9,10},{10,1... | collective-permute-start | bytes 2752520 | tf_op jit(solution)/shard_map/ppermute | solution.py:54
  84.8 13.4 %collective-permute-start.17 = (bf16[64,7168]{1,0:T(8,128)(2,1)S(1)}, bf16[64,7168]{1,0:T(8,128)(2,1)S(1)}, u32[]{:S(2)}, u32[]{:S(2)}) collective-permute-start(bf16[64,7168]{1,0:T(8,128)(2,1)S(1)} %get-tuple-element.55), channel_id=1, source_target_pairs={{0,3},{1,0},{2,1},{3,2},{4,7},{5,4},{6,5},{7,6},{8,11},{9,8},{10,9... | collective-permute-start | bytes 2752520 | tf_op jit(solution)/shard_map/ppermute | solution.py:54
  93.3 14.7 %collective-permute-start.18 = (bf16[64,7168]{1,0:T(8,128)(2,1)S(1)}, bf16[64,7168]{1,0:T(8,128)(2,1)S(1)}, u32[]{:S(2)}, u32[]{:S(2)}) collective-permute-start(bf16[64,7168]{1,0:T(8,128)(2,1)S(1)} %get-tuple-element.57), channel_id=1, source_target_pairs={{0,1},{1,2},{2,3},{3,0},{4,5},{5,6},{6,7},{7,4},{8,9},{9,10},{10,1... | collective-permute-start | bytes 2752520 | tf_op jit(solution)/shard_map/ppermute | solution.py:54
  108.2 13.5 %collective-permute-start.19 = (bf16[64,7168]{1,0:T(8,128)(2,1)S(1)}, bf16[64,7168]{1,0:T(8,128)(2,1)S(1)}, u32[]{:S(2)}, u32[]{:S(2)}) collective-permute-start(bf16[64,7168]{1,0:T(8,128)(2,1)S(1)} %add_convert_fusion.4), channel_id=1, source_target_pairs={{0,3},{1,0},{2,1},{3,2},{4,7},{5,4},{6,5},{7,6},{8,11},{9,8},{10,9... | collective-permute-start | bytes 2752520 | tf_op jit(solution)/shard_map/ppermute | solution.py:54
  111.5 14.7 %collective-permute-start.20 = (bf16[64,7168]{1,0:T(8,128)(2,1)S(1)}, bf16[64,7168]{1,0:T(8,128)(2,1)S(1)}, u32[]{:S(2)}, u32[]{:S(2)}) collective-permute-start(bf16[64,7168]{1,0:T(8,128)(2,1)S(1)} %add_convert_fusion.3), channel_id=1, source_target_pairs={{0,1},{1,2},{2,3},{3,0},{4,5},{5,6},{6,7},{7,4},{8,9},{9,10},{10,1... | collective-permute-start | bytes 2752520 | tf_op jit(solution)/shard_map/ppermute | solution.py:54
  126.6 9.8 %collective-permute-start.23 = (bf16[32,7168]{1,0:T(8,128)(2,1)S(1)}, bf16[32,7168]{1,0:T(8,128)(2,1)S(1)}, u32[]{:S(2)}, u32[]{:S(2)}) collective-permute-start(bf16[32,7168]{1,0:T(8,128)(2,1)S(1)} %get-tuple-element.70), channel_id=1, source_target_pairs={{0,4},{1,5},{2,6},{3,7},{4,8},{5,9},{6,10},{7,11},{8,12},{9,13},{1... | collective-permute-start | bytes 1376264 | tf_op jit(solution)/shard_map/ppermute | solution.py:54
  128.3 13.5 %collective-permute-start.22 = (bf16[32,7168]{1,0:T(8,128)(2,1)S(1)}, bf16[32,7168]{1,0:T(8,128)(2,1)S(1)}, u32[]{:S(2)}, u32[]{:S(2)}) collective-permute-start(bf16[32,7168]{1,0:T(8,128)(2,1)S(1)} %get-tuple-element.69), channel_id=1, source_target_pairs={{0,8},{1,9},{2,10},{3,11},{4,12},{5,13},{6,14},{7,15},{8,0},{9,1},... | collective-permute-start | bytes 1376264 | tf_op jit(solution)/shard_map/ppermute | solution.py:54
  130.5 11.8 %collective-permute-start.21 = (bf16[32,7168]{1,0:T(8,128)(2,1)S(1)}, bf16[32,7168]{1,0:T(8,128)(2,1)S(1)}, u32[]{:S(2)}, u32[]{:S(2)}) collective-permute-start(bf16[32,7168]{1,0:T(8,128)(2,1)S(1)} %split.25), channel_id=1, source_target_pairs={{0,12},{1,13},{2,14},{3,15},{4,0},{5,1},{6,2},{7,3},{8,4},{9,5},{1... | collective-permute-start | bytes 1376264 | tf_op jit(solution)/shard_map/ppermute | solution.py:54
  142.5 10.3 %collective-permute-start.26 = (bf16[8,7168]{1,0:T(8,128)(2,1)S(1)}, bf16[8,7168]{1,0:T(8,128)(2,1)S(1)}, u32[]{:S(2)}, u32[]{:S(2)}) collective-permute-start(bf16[8,7168]{1,0:T(8,128)(2,1)S(1)} %get-tuple-element.72), channel_id=1, source_target_pairs={{0,16},{1,17},{2,18},{3,19},{4,20},{5,21},{6,22},{7,23},{8,24},{9,... | collective-permute-start | bytes 344072 | tf_op jit(solution)/shard_map/ppermute | solution.py:54
  145.8 7.0 %collective-permute-start.25 = (bf16[8,7168]{1,0:T(8,128)(2,1)S(1)}, bf16[8,7168]{1,0:T(8,128)(2,1)S(1)}, u32[]{:S(2)}, u32[]{:S(2)}) collective-permute-start(bf16[8,7168]{1,0:T(8,128)(2,1)S(1)} %get-tuple-element.73), channel_id=1, source_target_pairs={{0,32},{1,33},{2,34},{3,35},{4,36},{5,37},{6,38},{7,39},{8,40},{9,... | collective-permute-start | bytes 344072 | tf_op jit(solution)/shard_map/ppermute | solution.py:54
  (17 other events, 310.5 us)

commit v3 on v2

--- a/solution.py
+++ b/solution.py
@@ -229,26 +229,19 @@
     mine_acts = acts_of(info, low, high)
     low_back, high_ahead = lax.optimization_barrier((low_back, high_ahead, mine_acts))[:2]
     low_far, high_far = shift(low_back, 2, 1), shift(high_ahead, 2, -1)
-    near_rows = (low_back, high_ahead)
-    high_back, low_ahead = outs_of(acts_of(info, high_back, low_ahead))
-    high_back, low_ahead, low_far, high_far = lax.optimization_barrier(
-        (high_back, low_ahead, low_far, high_far)
-    )
-    high_back, low_ahead = shift(high_back, 2, -1), shift(low_ahead, 2, 1)
+    near_acts = acts_of(info, high_back, low_ahead, low_back, high_ahead)
+    middle = near_acts.shape[0] // 2
+    high_back, low_ahead = outs_of(near_acts[:middle])
+    high_back = shift(after(high_back, high_far), 2, -1)
+    low_ahead = shift(after(low_ahead, low_far), 2, 1)
     low_far, high_far = outs_of(acts_of(info, low_far, high_far))
-    near_info = after(info, low_far)
-    low_far, high_far, high_back, low_ahead = lax.optimization_barrier(
-        (low_far, high_far, high_back, low_ahead)
-    )
-    low_far, high_far = shift(low_far, 2, -1), shift(high_far, 2, 1)
-    low_back, high_ahead = outs_of(acts_of(near_info, *near_rows))
-    low_mine, high_mine = outs_of(after(mine_acts, low_back))
-    low_back, high_ahead = lax.optimization_barrier(
-        (
-            plus(low_back, low_far).astype(jnp.bfloat16),
-            plus(high_ahead, high_far).astype(jnp.bfloat16),
-        )
-    )
+    near_acts, mine_acts = lax.optimization_barrier((near_acts, mine_acts, low_far))[:2]
+    low_far = shift(after(low_far, high_back), 2, -1)
+    high_far = shift(after(high_far, low_ahead), 2, 1)
+    low_back, high_ahead = outs_of(near_acts[middle:])
+    low_mine, high_mine = outs_of(mine_acts)
+    low_back = after(plus(low_back, low_far).astype(jnp.bfloat16), low_mine)
+    high_ahead = after(plus(high_ahead, high_far).astype(jnp.bfloat16), low_mine)
     low_back, high_ahead = shift(low_back, 2, -1), shift(high_ahead, 2, 1)
     low = plus(low_mine, low_back, low_ahead).astype(jnp.bfloat16)
     high = plus(high_mine, high_back, high_ahead).astype(jnp.bfloat16)

time: 164 us -> 158 us (0.963); the launches traced: 161 us -> 156 us
  starting transfers between devices: 44.9 us -> 40.5 us
  waiting for transfers between devices: 62.5 us -> 65.6 us
  Pallas kernels: 36.7 us -> 33.7 us
    ppermute x24, starting transfers between devices: 44.2 us -> 39.4 us  [shift(): return lax.ppermute(values, AXES, pairs)]
    ppermute x24, waiting for transfers between devices: 62.5 us -> 65.6 us  [shift(): return lax.ppermute(values, AXES, pairs)]
    pallas_call x4 -> x3, Pallas kernels: 22 us -> 19.1 us  [expert_acts(): pl.pallas_call(act_body, out_shape=jax.ShapeDtypeStruct((tokens, 2 * wide...]
  transfers between devices with their start and end apart: 27 -> 27, of which waited for: 17 -> 16; matrix products, arithmetic and copies ran while one was open for 3% -> 3% of each run, Pallas kernels for 22% -> 21%
where the time goes in v3:
time: 158 us; the launch traced here: 156 us
  waiting for transfers between devices  65.6 us (42%)
  starting transfers between devices  40.5 us (26%)
  Pallas kernels  33.7 us (21%)
  other arithmetic  6.08 us (4%)
  matrix products  5.13 us (3%)
  local copies, waits for them, and re-layouts  4.38 us (3%)
    ppermute x24, waiting for transfers between devices, shift(): return lax.ppermute(values, AXES, pairs)  65.6 us
    ppermute x24, starting transfers between devices, shift(): return lax.ppermute(values, AXES, pairs)  39.4 us
    pallas_call x3, Pallas kernels, expert_acts(): pl.pallas_call(act_body, out_shape=jax.ShapeDtypeStruct((tokens, 2 * wide...  19.1 us
    pallas_call x4, Pallas kernels, expert_outs(): pl.pallas_call(down_body, out_shape=[jax.ShapeDtypeStruct((tokens // coun...  12.8 us
    unnamed x28, local copies, waits for them, and re-layouts  4.14 us
  transfers between devices with their start and end apart: 27, of which 16 were waited for; matrix products, arithmetic and copies ran while one was open for 3% of the time, Pallas kernels for 21%

profile of v3, /device:TPU:2, one launch (start us, length us, event | category | flops | bytes accessed | tf_op | source)
XLA Modules:
  0.0 156.4 jit_solution(8555891988426698002)
XLA Ops:
  13.0 3.1 %collective-permute-start.5 = (bf16[4,8,7296]{2,1,0:T(8,128)(2,1)S(1)}, bf16[4,8,7296]{2,1,0:T(8,128)(2,1)S(1)}, u32[]{:S(2)}, u32[]{:S(2)}) collective-permute-start(bf16[4,8,7296]{2,1,0:T(8,128)(2,1)S(1)} %join.2.refs_0_), channel_id=1, source_target_pairs={{0,12},{1,13},{2,14},{3,15},{4,0},{5,1},{6,2},{7,3},{8,4},{9,5},{1... | collective-permute-start | bytes 1400840 | tf_op jit(solution)/shard_map/ppermute | solution.py:54
  17.7 9.5 %collective-permute-done.5.refs_3_ = bf16[4,8,7296]{2,1,0:T(8,128)(2,1)S(1)} collective-permute-done((bf16[4,8,7296]{2,1,0:T(8,128)(2,1)S(1)}, bf16[4,8,7296]{2,1,0:T(8,128)(2,1)S(1)}, u32[]{:S(2)}, u32[]{:S(2)}) %collective-permute-start.5) | collective-permute-done | bytes 466976 | tf_op jit(solution)/shard_map/ppermute | solution.py:54
  27.2 4.0 %collective-permute-done.3.refs_1_ = bf16[4,8,7296]{2,1,0:T(8,128)(2,1)S(1)} collective-permute-done((bf16[4,8,7296]{2,1,0:T(8,128)(2,1)S(1)}, bf16[4,8,7296]{2,1,0:T(8,128)(2,1)S(1)}, u32[]{:S(2)}, u32[]{:S(2)}) %collective-permute-start.3) | collective-permute-done | bytes 466976 | tf_op jit(solution)/shard_map/ppermute | solution.py:54
  32.8 3.7 %collective-permute-start.11 = (bf16[8,8,7296]{2,1,0:T(8,128)(2,1)S(1)}, bf16[8,8,7296]{2,1,0:T(8,128)(2,1)}, u32[]{:S(2)}, u32[]{:S(2)}) collective-permute-start(bf16[8,8,7296]{2,1,0:T(8,128)(2,1)S(1)} %get-tuple-element.34), channel_id=1, source_target_pairs={{0,3},{1,0},{2,1},{3,2},{4,7},{5,4},{6,5},{7,6},{8,11},{9,8},{10,9... | collective-permute-start | bytes 2801672 | tf_op jit(solution)/shard_map/ppermute | solution.py:54
  36.5 3.3 %collective-permute-start.9 = (bf16[8,8,7296]{2,1,0:T(8,128)(2,1)S(1)}, bf16[8,8,7296]{2,1,0:T(8,128)(2,1)}, u32[]{:S(2)}, u32[]{:S(2)}) collective-permute-start(bf16[8,8,7296]{2,1,0:T(8,128)(2,1)S(1)} %get-tuple-element.35), channel_id=1, source_target_pairs={{0,3},{1,0},{2,1},{3,2},{4,7},{5,4},{6,5},{7,6},{8,11},{9,8},{10,9... | collective-permute-start | bytes 2801672 | tf_op jit(solution)/shard_map/ppermute | solution.py:54
  43.9 5.4 %expert_acts.3.acts_ref = bf16[128,512]{1,0:T(8,128)(2,1)S(1)} custom-call(s32[2]{0:T(128)S(1)} %pad_add_fusion.info_ref, bf16[64,7296]{1,0:T(8,128)(2,1)S(1)} %bitcast.19, bf16[64,7296]{1,0:T(8,128)(2,1)S(1)} %bitcast.20, bf16[7168,256]{1,0:T(8,128)(2,1)S(1)} %copy-done.2, bf16[7168,256]{1,0:T(8,128)(2,1)} %collective-permute-done.6.refs_3_.refs_5_, ...), custom_call_target="tpu_custom_call" | custom-call | flops 1879048192 | bytes 1048576 | tf_op jit(solution)/shard_map/expert_acts/pallas_call | solution.py:122
  51.4 3.2 %collective-permute-start.13 = (bf16[8,8,7296]{2,1,0:T(8,128)(2,1)}, bf16[8,8,7296]{2,1,0:T(8,128)(2,1)S(1)}, u32[]{:S(2)}, u32[]{:S(2)}) collective-permute-start(bf16[8,8,7296]{2,1,0:T(8,128)(2,1)} %collective-permute-done.11), channel_id=1, source_target_pairs={{0,3},{1,0},{2,1},{3,2},{4,7},{5,4},{6,5},{7,6},{8,11},{9,8},{10,9... | collective-permute-start | bytes 2801672 | tf_op jit(solution)/shard_map/ppermute | solution.py:54
  54.6 6.8 %collective-permute-done.8 = bf16[8,8,7296]{2,1,0:T(8,128)(2,1)} collective-permute-done((bf16[8,8,7296]{2,1,0:T(8,128)(2,1)S(1)}, bf16[8,8,7296]{2,1,0:T(8,128)(2,1)}, u32[]{:S(2)}, u32[]{:S(2)}) %collective-permute-start.8) | collective-permute-done | bytes 933920 | tf_op jit(solution)/shard_map/ppermute | solution.py:54
  61.4 8.4 %expert_acts.4 = bf16[256,512]{1,0:T(8,128)(2,1)S(1)} custom-call(s32[2]{0:T(128)S(1)} %pad_add_fusion.info_ref, bf16[64,7296]{1,0:T(8,128)(2,1)} %bitcast.3.refs_0_, bf16[64,7296]{1,0:T(8,128)(2,1)} %bitcast.4.refs_1_, bf16[64,7296]{1,0:T(8,128)(2,1)} %bitcast.7.refs_2_, bf16[64,7296]{1,0:T(8,128)(2,1)} %bitcast.8.refs_3_, bf16[7168,256]{1,0:T(8,128)(2,1)S(1)} %copy-done.3, ...), custom_call_target="tpu_custom_call" | custom-call | flops 3758096384 | bytes 1048576 | tf_op jit(solution)/shard_map/expert_acts/pallas_call | solution.py:122
  69.8 3.2 %expert_outs.7 = (bf16[64,7168]{1,0:T(8,128)(2,1)S(1)}, bf16[64,7168]{1,0:T(8,128)(2,1)S(1)}) custom-call(bf16[128,512]{1,0:T(8,128)(2,1)S(1)} %slice.31.acts_ref, bf16[256,7168]{1,0:T(8,128)(2,1)S(1)} %copy-done.1, bf16[256,7168]{1,0:T(8,128)(2,1)} %collective-permute-done.14.other_ref), custom_call_target="tpu_custom_call" | custom-call | flops 939524096 | bytes 1048576 | tf_op jit(solution)/shard_map/expert_outs/pallas_call | solution.py:153
  73.1 3.2 %collective-permute-start.15 = (bf16[64,7168]{1,0:T(8,128)(2,1)S(1)}, bf16[64,7168]{1,0:T(8,128)(2,1)S(1)}, u32[]{:S(2)}, u32[]{:S(2)}) collective-permute-start(bf16[64,7168]{1,0:T(8,128)(2,1)S(1)} %get-tuple-element.45), channel_id=1, source_target_pairs={{0,3},{1,0},{2,1},{3,2},{4,7},{5,4},{6,5},{7,6},{8,11},{9,8},{10,9... | collective-permute-start | bytes 2752520 | tf_op jit(solution)/shard_map/ppermute | solution.py:54
  76.4 5.3 %expert_acts.5.acts_ref = bf16[128,512]{1,0:T(8,128)(2,1)S(1)} custom-call(s32[2]{0:T(128)S(1)} %pad_add_fusion.info_ref, bf16[64,7296]{1,0:T(8,128)(2,1)S(1)} %bitcast.21, bf16[64,7296]{1,0:T(8,128)(2,1)S(1)} %bitcast.22, bf16[7168,256]{1,0:T(8,128)(2,1)S(1)} %copy-done.3, bf16[7168,256]{1,0:T(8,128)(2,1)} %collective-permute-done.6.refs_3_.refs_5_, ...), custom_call_target="tpu_custom_call" | custom-call | flops 1879048192 | bytes 1048576 | tf_op jit(solution)/shard_map/expert_acts/pallas_call | solution.py:122
  81.7 3.2 %expert_outs.4 = (bf16[64,7168]{1,0:T(8,128)(2,1)S(1)}, bf16[64,7168]{1,0:T(8,128)(2,1)S(1)}) custom-call(bf16[128,512]{1,0:T(8,128)(2,1)S(1)} %expert_acts.5.acts_ref, bf16[256,7168]{1,0:T(8,128)(2,1)S(1)} %copy-done.1, bf16[256,7168]{1,0:T(8,128)(2,1)} %collective-permute-done.14.other_ref), custom_call_target="tpu_custom_call" | custom-call | flops 939524096 | bytes 1048576 | tf_op jit(solution)/shard_map/expert_outs/pallas_call | solution.py:153
  84.9 2.8 %collective-permute-done.18 = bf16[64,7168]{1,0:T(8,128)(2,1)S(1)} collective-permute-done((bf16[64,7168]{1,0:T(8,128)(2,1)S(1)}, bf16[64,7168]{1,0:T(8,128)(2,1)S(1)}, u32[]{:S(2)}, u32[]{:S(2)}) %collective-permute-start.18) | collective-permute-done | bytes 917536 | tf_op jit(solution)/shard_map/ppermute | solution.py:54
  87.7 3.2 %collective-permute-start.16 = (bf16[64,7168]{1,0:T(8,128)(2,1)S(1)}, bf16[64,7168]{1,0:T(8,128)(2,1)S(1)}, u32[]{:S(2)}, u32[]{:S(2)}) collective-permute-start(bf16[64,7168]{1,0:T(8,128)(2,1)S(1)} %get-tuple-element.46), channel_id=1, source_target_pairs={{0,3},{1,0},{2,1},{3,2},{4,7},{5,4},{6,5},{7,6},{8,11},{9,8},{10,9... | collective-permute-start | bytes 2752520 | tf_op jit(solution)/shard_map/ppermute | solution.py:54
  91.0 3.2 %expert_outs.6 = (bf16[64,7168]{1,0:T(8,128)(2,1)S(1)}, bf16[64,7168]{1,0:T(8,128)(2,1)S(1)}) custom-call(bf16[128,512]{1,0:T(8,128)(2,1)S(1)} %slice.24.acts_ref, bf16[256,7168]{1,0:T(8,128)(2,1)S(1)} %copy-done.1, bf16[256,7168]{1,0:T(8,128)(2,1)} %collective-permute-done.14.other_ref), custom_call_target="tpu_custom_call" | custom-call | flops 939524096 | bytes 1048576 | tf_op jit(solution)/shard_map/expert_outs/pallas_call | solution.py:153
  94.2 3.2 %expert_outs.5 = (bf16[64,7168]{1,0:T(8,128)(2,1)S(1)}, bf16[64,7168]{1,0:T(8,128)(2,1)S(1)}) custom-call(bf16[128,512]{1,0:T(8,128)(2,1)S(1)} %expert_acts.3.acts_ref, bf16[256,7168]{1,0:T(8,128)(2,1)S(1)} %copy-done.1, bf16[256,7168]{1,0:T(8,128)(2,1)} %collective-permute-done.14.other_ref), custom_call_target="tpu_custom_call" | custom-call | flops 939524096 | bytes 1048576 | tf_op jit(solution)/shard_map/expert_outs/pallas_call | solution.py:153
  97.4 4.5 %collective-permute-done.16 = bf16[64,7168]{1,0:T(8,128)(2,1)S(1)} collective-permute-done((bf16[64,7168]{1,0:T(8,128)(2,1)S(1)}, bf16[64,7168]{1,0:T(8,128)(2,1)S(1)}, u32[]{:S(2)}, u32[]{:S(2)}) %collective-permute-start.16) | collective-permute-done | bytes 917536 | tf_op jit(solution)/shard_map/ppermute | solution.py:54
  101.9 3.7 %collective-permute-done.19 = bf16[64,7168]{1,0:T(8,128)(2,1)S(1)} collective-permute-done((bf16[64,7168]{1,0:T(8,128)(2,1)S(1)}, bf16[64,7168]{1,0:T(8,128)(2,1)S(1)}, u32[]{:S(2)}, u32[]{:S(2)}) %collective-permute-start.19) | collective-permute-done | bytes 917536 | tf_op jit(solution)/shard_map/ppermute | solution.py:54
  108.1 13.0 %collective-permute-done.17 = bf16[64,7168]{1,0:T(8,128)(2,1)S(1)} collective-permute-done((bf16[64,7168]{1,0:T(8,128)(2,1)S(1)}, bf16[64,7168]{1,0:T(8,128)(2,1)S(1)}, u32[]{:S(2)}, u32[]{:S(2)}) %collective-permute-start.17) | collective-permute-done | bytes 917536 | tf_op jit(solution)/shard_map/ppermute | solution.py:54
  124.1 6.4 %collective-permute-done.21 = bf16[32,7168]{1,0:T(8,128)(2,1)S(1)} collective-permute-done((bf16[32,7168]{1,0:T(8,128)(2,1)S(1)}, bf16[32,7168]{1,0:T(8,128)(2,1)S(1)}, u32[]{:S(2)}, u32[]{:S(2)}) %collective-permute-start.21) | collective-permute-done | bytes 458784 | tf_op jit(solution)/shard_map/ppermute | solution.py:54
  132.4 4.8 %collective-permute-done.23 = bf16[32,7168]{1,0:T(8,128)(2,1)S(1)} collective-permute-done((bf16[32,7168]{1,0:T(8,128)(2,1)S(1)}, bf16[32,7168]{1,0:T(8,128)(2,1)S(1)}, u32[]{:S(2)}, u32[]{:S(2)}) %collective-permute-start.23) | collective-permute-done | bytes 458784 | tf_op jit(solution)/shard_map/ppermute | solution.py:54
  137.5 6.5 %collective-permute-start.24 = (bf16[8,7168]{1,0:T(8,128)(2,1)S(1)}, bf16[8,7168]{1,0:T(8,128)(2,1)S(1)}, u32[]{:S(2)}, u32[]{:S(2)}) collective-permute-start(bf16[8,7168]{1,0:T(8,128)(2,1)S(1)} %get-tuple-element.63), channel_id=1, source_target_pairs={{0,48},{1,49},{2,50},{3,51},{4,52},{5,53},{6,54},{7,55},{8,56},{9,... | collective-permute-start | bytes 344072 | tf_op jit(solution)/shard_map/ppermute | solution.py:54
  144.0 2.6 %collective-permute-start.25 = (bf16[8,7168]{1,0:T(8,128)(2,1)S(1)}, bf16[8,7168]{1,0:T(8,128)(2,1)S(1)}, u32[]{:S(2)}, u32[]{:S(2)}) collective-permute-start(bf16[8,7168]{1,0:T(8,128)(2,1)S(1)} %get-tuple-element.65), channel_id=1, source_target_pairs={{0,32},{1,33},{2,34},{3,35},{4,36},{5,37},{6,38},{7,39},{8,40},{9,... | collective-permute-start | bytes 344072 | tf_op jit(solution)/shard_map/ppermute | solution.py:54
  (103 shorter events, 39.3 us)
Async XLA Ops:
  0.6 30.5 %collective-permute-start.6 = (bf16[7168,256]{1,0:T(8,128)(2,1)}, bf16[7168,256]{1,0:T(8,128)(2,1)}, u32[]{:S(2)}, u32[]{:S(2)}) collective-permute-start(bf16[7168,256]{1,0:T(8,128)(2,1)} %refs_2_.3), channel_id=1, source_target_pairs={{0,64},{1,65},{2,66},{3,67},{4,68},{5,69},{6,70},{7,71},{8,72},{9,... | collective-permute-start | bytes 11010056 | tf_op jit(solution)/shard_map/ppermute | solution.py:58
  0.7 30.4 %collective-permute-start.7 = (bf16[7168,256]{1,0:T(8,128)(2,1)}, bf16[7168,256]{1,0:T(8,128)(2,1)}, u32[]{:S(2)}, u32[]{:S(2)}) collective-permute-start(bf16[7168,256]{1,0:T(8,128)(2,1)} %refs_4_.5), channel_id=1, source_target_pairs={{0,64},{1,65},{2,66},{3,67},{4,68},{5,69},{6,70},{7,71},{8,72},{9,... | collective-permute-start | bytes 11010056 | tf_op jit(solution)/shard_map/ppermute | solution.py:58
  4.7 6.5 %collective-permute-start.1 = (bf16[1,8,7296]{2,1,0:T(8,128)(2,1)S(1)}, bf16[1,8,7296]{2,1,0:T(8,128)(2,1)S(1)}, u32[]{:S(2)}, u32[]{:S(2)}) collective-permute-start(bf16[1,8,7296]{2,1,0:T(8,128)(2,1)S(1)} %bitcast.24), channel_id=1, source_target_pairs={{0,32},{1,33},{2,34},{3,35},{4,36},{5,37},{6,38},{7,39},{8,40},{9,... | collective-permute-start | bytes 350216 | tf_op jit(solution)/shard_map/ppermute | solution.py:54
  13.0 14.2 %collective-permute-start.5 = (bf16[4,8,7296]{2,1,0:T(8,128)(2,1)S(1)}, bf16[4,8,7296]{2,1,0:T(8,128)(2,1)S(1)}, u32[]{:S(2)}, u32[]{:S(2)}) collective-permute-start(bf16[4,8,7296]{2,1,0:T(8,128)(2,1)S(1)} %join.2.refs_0_), channel_id=1, source_target_pairs={{0,12},{1,13},{2,14},{3,15},{4,0},{5,1},{6,2},{7,3},{8,4},{9,5},{1... | collective-permute-start | bytes 1400840 | tf_op jit(solution)/shard_map/ppermute | solution.py:54
  16.1 11.1 %collective-permute-start.4 = (bf16[4,8,7296]{2,1,0:T(8,128)(2,1)S(1)}, bf16[4,8,7296]{2,1,0:T(8,128)(2,1)S(1)}, u32[]{:S(2)}, u32[]{:S(2)}) collective-permute-start(bf16[4,8,7296]{2,1,0:T(8,128)(2,1)S(1)} %join.2.refs_0_), channel_id=1, source_target_pairs={{0,8},{1,9},{2,10},{3,11},{4,12},{5,13},{6,14},{7,15},{8,0},{9,1},... | collective-permute-start | bytes 1400840 | tf_op jit(solution)/shard_map/ppermute | solution.py:54
  16.7 14.4 %collective-permute-start.3 = (bf16[4,8,7296]{2,1,0:T(8,128)(2,1)S(1)}, bf16[4,8,7296]{2,1,0:T(8,128)(2,1)S(1)}, u32[]{:S(2)}, u32[]{:S(2)}) collective-permute-start(bf16[4,8,7296]{2,1,0:T(8,128)(2,1)S(1)} %join.2.refs_0_), channel_id=1, source_target_pairs={{0,4},{1,5},{2,6},{3,7},{4,8},{5,9},{6,10},{7,11},{8,12},{9,13},{1... | collective-permute-start | bytes 1400840 | tf_op jit(solution)/shard_map/ppermute | solution.py:54
  32.3 37.5 %collective-permute-start.14 = (bf16[256,7168]{1,0:T(8,128)(2,1)}, bf16[256,7168]{1,0:T(8,128)(2,1)}, u32[]{:S(2)}, u32[]{:S(2)}) collective-permute-start(bf16[256,7168]{1,0:T(8,128)(2,1)} %mine_ref.7), channel_id=1, source_target_pairs={{0,64},{1,65},{2,66},{3,67},{4,68},{5,69},{6,70},{7,71},{8,72},{9,... | collective-permute-start | bytes 11010056 | tf_op jit(solution)/shard_map/ppermute | solution.py:58
  32.8 16.6 %collective-permute-start.11 = (bf16[8,8,7296]{2,1,0:T(8,128)(2,1)S(1)}, bf16[8,8,7296]{2,1,0:T(8,128)(2,1)}, u32[]{:S(2)}, u32[]{:S(2)}) collective-permute-start(bf16[8,8,7296]{2,1,0:T(8,128)(2,1)S(1)} %get-tuple-element.34), channel_id=1, source_target_pairs={{0,3},{1,0},{2,1},{3,2},{4,7},{5,4},{6,5},{7,6},{8,11},{9,8},{10,9... | collective-permute-start | bytes 2801672 | tf_op jit(solution)/shard_map/ppermute | solution.py:54
  36.5 14.9 %collective-permute-start.10 = (bf16[8,8,7296]{2,1,0:T(8,128)(2,1)S(1)}, bf16[8,8,7296]{2,1,0:T(8,128)(2,1)}, u32[]{:S(2)}, u32[]{:S(2)}) collective-permute-start(bf16[8,8,7296]{2,1,0:T(8,128)(2,1)S(1)} %get-tuple-element.35), channel_id=1, source_target_pairs={{0,1},{1,2},{2,3},{3,0},{4,5},{5,6},{6,7},{7,4},{8,9},{9,10},{10,1... | collective-permute-start | bytes 2801672 | tf_op jit(solution)/shard_map/ppermute | solution.py:54
  36.5 24.9 %collective-permute-start.8 = (bf16[8,8,7296]{2,1,0:T(8,128)(2,1)S(1)}, bf16[8,8,7296]{2,1,0:T(8,128)(2,1)}, u32[]{:S(2)}, u32[]{:S(2)}) collective-permute-start(bf16[8,8,7296]{2,1,0:T(8,128)(2,1)S(1)} %get-tuple-element.34), channel_id=1, source_target_pairs={{0,1},{1,2},{2,3},{3,0},{4,5},{5,6},{6,7},{7,4},{8,9},{9,10},{10,1... | collective-permute-start | bytes 2801672 | tf_op jit(solution)/shard_map/ppermute | solution.py:54
  36.5 24.9 %collective-permute-start.9 = (bf16[8,8,7296]{2,1,0:T(8,128)(2,1)S(1)}, bf16[8,8,7296]{2,1,0:T(8,128)(2,1)}, u32[]{:S(2)}, u32[]{:S(2)}) collective-permute-start(bf16[8,8,7296]{2,1,0:T(8,128)(2,1)S(1)} %get-tuple-element.35), channel_id=1, source_target_pairs={{0,3},{1,0},{2,1},{3,2},{4,7},{5,4},{6,5},{7,6},{8,11},{9,8},{10,9... | collective-permute-start | bytes 2801672 | tf_op jit(solution)/shard_map/ppermute | solution.py:54
  51.4 21.6 %collective-permute-start.12 = (bf16[8,8,7296]{2,1,0:T(8,128)(2,1)}, bf16[8,8,7296]{2,1,0:T(8,128)(2,1)S(1)}, u32[]{:S(2)}, u32[]{:S(2)}) collective-permute-start(bf16[8,8,7296]{2,1,0:T(8,128)(2,1)} %collective-permute-done.10), channel_id=1, source_target_pairs={{0,1},{1,2},{2,3},{3,0},{4,5},{5,6},{6,7},{7,4},{8,9},{9,10},{10,1... | collective-permute-start | bytes 2801672 | tf_op jit(solution)/shard_map/ppermute | solution.py:54
  51.4 21.7 %collective-permute-start.13 = (bf16[8,8,7296]{2,1,0:T(8,128)(2,1)}, bf16[8,8,7296]{2,1,0:T(8,128)(2,1)S(1)}, u32[]{:S(2)}, u32[]{:S(2)}) collective-permute-start(bf16[8,8,7296]{2,1,0:T(8,128)(2,1)} %collective-permute-done.11), channel_id=1, source_target_pairs={{0,3},{1,0},{2,1},{3,2},{4,7},{5,4},{6,5},{7,6},{8,11},{9,8},{10,9... | collective-permute-start | bytes 2801672 | tf_op jit(solution)/shard_map/ppermute | solution.py:54
  73.0 14.7 %collective-permute-start.18 = (bf16[64,7168]{1,0:T(8,128)(2,1)S(1)}, bf16[64,7168]{1,0:T(8,128)(2,1)S(1)}, u32[]{:S(2)}, u32[]{:S(2)}) collective-permute-start(bf16[64,7168]{1,0:T(8,128)(2,1)S(1)} %get-tuple-element.49), channel_id=1, source_target_pairs={{0,1},{1,2},{2,3},{3,0},{4,5},{5,6},{6,7},{7,4},{8,9},{9,10},{10,1... | collective-permute-start | bytes 2752520 | tf_op jit(solution)/shard_map/ppermute | solution.py:54
  73.1 14.6 %collective-permute-start.15 = (bf16[64,7168]{1,0:T(8,128)(2,1)S(1)}, bf16[64,7168]{1,0:T(8,128)(2,1)S(1)}, u32[]{:S(2)}, u32[]{:S(2)}) collective-permute-start(bf16[64,7168]{1,0:T(8,128)(2,1)S(1)} %get-tuple-element.45), channel_id=1, source_target_pairs={{0,3},{1,0},{2,1},{3,2},{4,7},{5,4},{6,5},{7,6},{8,11},{9,8},{10,9... | collective-permute-start | bytes 2752520 | tf_op jit(solution)/shard_map/ppermute | solution.py:54
  87.7 14.2 %collective-permute-start.16 = (bf16[64,7168]{1,0:T(8,128)(2,1)S(1)}, bf16[64,7168]{1,0:T(8,128)(2,1)S(1)}, u32[]{:S(2)}, u32[]{:S(2)}) collective-permute-start(bf16[64,7168]{1,0:T(8,128)(2,1)S(1)} %get-tuple-element.46), channel_id=1, source_target_pairs={{0,3},{1,0},{2,1},{3,2},{4,7},{5,4},{6,5},{7,6},{8,11},{9,8},{10,9... | collective-permute-start | bytes 2752520 | tf_op jit(solution)/shard_map/ppermute | solution.py:54
  91.0 14.6 %collective-permute-start.19 = (bf16[64,7168]{1,0:T(8,128)(2,1)S(1)}, bf16[64,7168]{1,0:T(8,128)(2,1)S(1)}, u32[]{:S(2)}, u32[]{:S(2)}) collective-permute-start(bf16[64,7168]{1,0:T(8,128)(2,1)S(1)} %get-tuple-element.53), channel_id=1, source_target_pairs={{0,1},{1,2},{2,3},{3,0},{4,5},{5,6},{6,7},{7,4},{8,9},{9,10},{10,1... | collective-permute-start | bytes 2752520 | tf_op jit(solution)/shard_map/ppermute | solution.py:54
  106.0 15.1 %collective-permute-start.17 = (bf16[64,7168]{1,0:T(8,128)(2,1)S(1)}, bf16[64,7168]{1,0:T(8,128)(2,1)S(1)}, u32[]{:S(2)}, u32[]{:S(2)}) collective-permute-start(bf16[64,7168]{1,0:T(8,128)(2,1)S(1)} %get-tuple-element.47), channel_id=1, source_target_pairs={{0,3},{1,0},{2,1},{3,2},{4,7},{5,4},{6,5},{7,6},{8,11},{9,8},{10,9... | collective-permute-start | bytes 2752520 | tf_op jit(solution)/shard_map/ppermute | solution.py:54
  106.1 15.3 %collective-permute-start.20 = (bf16[64,7168]{1,0:T(8,128)(2,1)S(1)}, bf16[64,7168]{1,0:T(8,128)(2,1)S(1)}, u32[]{:S(2)}, u32[]{:S(2)}) collective-permute-start(bf16[64,7168]{1,0:T(8,128)(2,1)S(1)} %get-tuple-element.54), channel_id=1, source_target_pairs={{0,1},{1,2},{2,3},{3,0},{4,5},{5,6},{6,7},{7,4},{8,9},{9,10},{10,1... | collective-permute-start | bytes 2752520 | tf_op jit(solution)/shard_map/ppermute | solution.py:54
  121.9 8.5 %collective-permute-start.21 = (bf16[32,7168]{1,0:T(8,128)(2,1)S(1)}, bf16[32,7168]{1,0:T(8,128)(2,1)S(1)}, u32[]{:S(2)}, u32[]{:S(2)}) collective-permute-start(bf16[32,7168]{1,0:T(8,128)(2,1)S(1)} %split.25), channel_id=1, source_target_pairs={{0,12},{1,13},{2,14},{3,15},{4,0},{5,1},{6,2},{7,3},{8,4},{9,5},{1... | collective-permute-start | bytes 1376264 | tf_op jit(solution)/shard_map/ppermute | solution.py:54
  122.3 10.1 %collective-permute-start.22 = (bf16[32,7168]{1,0:T(8,128)(2,1)S(1)}, bf16[32,7168]{1,0:T(8,128)(2,1)S(1)}, u32[]{:S(2)}, u32[]{:S(2)}) collective-permute-start(bf16[32,7168]{1,0:T(8,128)(2,1)S(1)} %get-tuple-element.61), channel_id=1, source_target_pairs={{0,8},{1,9},{2,10},{3,11},{4,12},{5,13},{6,14},{7,15},{8,0},{9,1},... | collective-permute-start | bytes 1376264 | tf_op jit(solution)/shard_map/ppermute | solution.py:54
  123.0 14.2 %collective-permute-start.23 = (bf16[32,7168]{1,0:T(8,128)(2,1)S(1)}, bf16[32,7168]{1,0:T(8,128)(2,1)S(1)}, u32[]{:S(2)}, u32[]{:S(2)}) collective-permute-start(bf16[32,7168]{1,0:T(8,128)(2,1)S(1)} %get-tuple-element.62), channel_id=1, source_target_pairs={{0,4},{1,5},{2,6},{3,7},{4,8},{5,9},{6,10},{7,11},{8,12},{9,13},{1... | collective-permute-start | bytes 1376264 | tf_op jit(solution)/shard_map/ppermute | solution.py:54
  137.5 9.9 %collective-permute-start.24 = (bf16[8,7168]{1,0:T(8,128)(2,1)S(1)}, bf16[8,7168]{1,0:T(8,128)(2,1)S(1)}, u32[]{:S(2)}, u32[]{:S(2)}) collective-permute-start(bf16[8,7168]{1,0:T(8,128)(2,1)S(1)} %get-tuple-element.63), channel_id=1, source_target_pairs={{0,48},{1,49},{2,50},{3,51},{4,52},{5,53},{6,54},{7,55},{8,56},{9,... | collective-permute-start | bytes 344072 | tf_op jit(solution)/shard_map/ppermute | solution.py:54
  144.0 6.3 %collective-permute-start.25 = (bf16[8,7168]{1,0:T(8,128)(2,1)S(1)}, bf16[8,7168]{1,0:T(8,128)(2,1)S(1)}, u32[]{:S(2)}, u32[]{:S(2)}) collective-permute-start(bf16[8,7168]{1,0:T(8,128)(2,1)S(1)} %get-tuple-element.65), channel_id=1, source_target_pairs={{0,32},{1,33},{2,34},{3,35},{4,36},{5,37},{6,38},{7,39},{8,40},{9,... | collective-permute-start | bytes 344072 | tf_op jit(solution)/shard_map/ppermute | solution.py:54
  (17 other events, 310.9 us)

commit v4 on v3

--- a/solution.py
+++ b/solution.py
@@ -229,20 +229,22 @@
     mine_acts = acts_of(info, low, high)
     low_back, high_ahead = lax.optimization_barrier((low_back, high_ahead, mine_acts))[:2]
     low_far, high_far = shift(low_back, 2, 1), shift(high_ahead, 2, -1)
-    near_acts = acts_of(info, high_back, low_ahead, low_back, high_ahead)
-    middle = near_acts.shape[0] // 2
-    high_back, low_ahead = outs_of(near_acts[:middle])
-    high_back = shift(after(high_back, high_far), 2, -1)
-    low_ahead = shift(after(low_ahead, low_far), 2, 1)
-    low_far, high_far = outs_of(acts_of(info, low_far, high_far))
-    near_acts, mine_acts = lax.optimization_barrier((near_acts, mine_acts, low_far))[:2]
-    low_far = shift(after(low_far, high_back), 2, -1)
-    high_far = shift(after(high_far, low_ahead), 2, 1)
-    low_back, high_ahead = outs_of(near_acts[middle:])
+    near_acts = acts_of(info, low_back, high_ahead)
+    near_acts, high_back, low_ahead = lax.optimization_barrier((near_acts, high_back, low_ahead))
+    low_back, high_ahead = outs_of(near_acts)
+    low_back = shift(after(low_back, high_far), 2, -1)
+    high_ahead = shift(after(high_ahead, low_far), 2, 1)
+    late_acts = acts_of(info, low_far, high_far, high_back, low_ahead)
+    middle = late_acts.shape[0] // 2
+    low_far, high_far = outs_of(late_acts[:middle])
+    late_acts, mine_acts = lax.optimization_barrier((late_acts, mine_acts, low_far))[:2]
+    high_far = shift(after(high_far, low_back), 2, -1)
+    low_far = shift(after(low_far, high_ahead), 2, 1)
+    high_back, low_ahead = outs_of(late_acts[middle:])
     low_mine, high_mine = outs_of(mine_acts)
-    low_back = after(plus(low_back, low_far).astype(jnp.bfloat16), low_mine)
-    high_ahead = after(plus(high_ahead, high_far).astype(jnp.bfloat16), low_mine)
-    low_back, high_ahead = shift(low_back, 2, -1), shift(high_ahead, 2, 1)
+    high_back = after(plus(high_back, high_far).astype(jnp.bfloat16), low_mine)
+    low_ahead = after(plus(low_ahead, low_far).astype(jnp.bfloat16), low_mine)
+    high_back, low_ahead = shift(high_back, 2, -1), shift(low_ahead, 2, 1)
     low = plus(low_mine, low_back, low_ahead).astype(jnp.bfloat16)
     high = plus(high_mine, high_back, high_ahead).astype(jnp.bfloat16)
     low, high = lax.optimization_barrier((low, high))

time: 158 us -> 154 us (0.975)
  waiting for transfers between devices: 65.6 us -> 63 us
    ppermute x24, waiting for transfers between devices: 65.6 us -> 63 us  [shift(): return lax.ppermute(values, AXES, pairs)]
  transfers between devices with their start and end apart: 27 -> 27, of which waited for: 16 -> 19; matrix products, arithmetic and copies ran while one was open for 3% -> 3% of each run, Pallas kernels for 21% -> 21%
where the time goes in v4:
time: 154 us; the launch traced here: 152 us
  waiting for transfers between devices  63 us (41%)
  starting transfers between devices  39 us (25%)
  Pallas kernels  33.8 us (22%)
  other arithmetic  6.11 us (4%)
  matrix products  5.12 us (3%)
  local copies, waits for them, and re-layouts  4.38 us (3%)
    ppermute x24, waiting for transfers between devices, shift(): return lax.ppermute(values, AXES, pairs)  63 us
    ppermute x24, starting transfers between devices, shift(): return lax.ppermute(values, AXES, pairs)  38.3 us
    pallas_call x3, Pallas kernels, expert_acts(): pl.pallas_call(act_body, out_shape=jax.ShapeDtypeStruct((tokens, 2 * wide...  18.5 us
    pallas_call x4, Pallas kernels, expert_outs(): pl.pallas_call(down_body, out_shape=[jax.ShapeDtypeStruct((tokens // coun...  13.2 us
    unnamed x28, local copies, waits for them, and re-layouts  4.14 us
  transfers between devices with their start and end apart: 27, of which 19 were waited for; matrix products, arithmetic and copies ran while one was open for 3% of the time, Pallas kernels for 21%

profile of v4, /device:TPU:2, one launch (start us, length us, event | category | flops | bytes accessed | tf_op | source)
XLA Modules:
  0.0 152.4 jit_solution(44058270668728252)
XLA Ops:
  6.8 2.2 %collective-permute-start.2 = (bf16[1,8,7296]{2,1,0:T(8,128)(2,1)S(1)}, bf16[1,8,7296]{2,1,0:T(8,128)(2,1)S(1)}, u32[]{:S(2)}, u32[]{:S(2)}) collective-permute-start(bf16[1,8,7296]{2,1,0:T(8,128)(2,1)S(1)} %bitcast.27), channel_id=1, source_target_pairs={{0,48},{1,49},{2,50},{3,51},{4,52},{5,53},{6,54},{7,55},{8,56},{9,... | collective-permute-start | bytes 350216 | tf_op jit(solution)/shard_map/ppermute | solution.py:54
  9.0 3.1 %collective-permute-done.1.refs_2_ = bf16[1,8,7296]{2,1,0:T(8,128)(2,1)S(1)} collective-permute-done((bf16[1,8,7296]{2,1,0:T(8,128)(2,1)S(1)}, bf16[1,8,7296]{2,1,0:T(8,128)(2,1)S(1)}, u32[]{:S(2)}, u32[]{:S(2)}) %collective-permute-start.1) | collective-permute-done | bytes 116768 | tf_op jit(solution)/shard_map/ppermute | solution.py:54
  15.2 2.9 %collective-permute-start.4 = (bf16[4,8,7296]{2,1,0:T(8,128)(2,1)S(1)}, bf16[4,8,7296]{2,1,0:T(8,128)(2,1)S(1)}, u32[]{:S(2)}, u32[]{:S(2)}) collective-permute-start(bf16[4,8,7296]{2,1,0:T(8,128)(2,1)S(1)} %join.2.refs_0_), channel_id=1, source_target_pairs={{0,8},{1,9},{2,10},{3,11},{4,12},{5,13},{6,14},{7,15},{8,0},{9,1},... | collective-permute-start | bytes 1400840 | tf_op jit(solution)/shard_map/ppermute | solution.py:54
  19.4 3.9 %collective-permute-done.3.refs_1_ = bf16[4,8,7296]{2,1,0:T(8,128)(2,1)S(1)} collective-permute-done((bf16[4,8,7296]{2,1,0:T(8,128)(2,1)S(1)}, bf16[4,8,7296]{2,1,0:T(8,128)(2,1)S(1)}, u32[]{:S(2)}, u32[]{:S(2)}) %collective-permute-start.3) | collective-permute-done | bytes 466976 | tf_op jit(solution)/shard_map/ppermute | solution.py:54
  23.3 6.3 %collective-permute-done.4.refs_2_ = bf16[4,8,7296]{2,1,0:T(8,128)(2,1)S(1)} collective-permute-done((bf16[4,8,7296]{2,1,0:T(8,128)(2,1)S(1)}, bf16[4,8,7296]{2,1,0:T(8,128)(2,1)S(1)}, u32[]{:S(2)}, u32[]{:S(2)}) %collective-permute-start.4) | collective-permute-done | bytes 466976 | tf_op jit(solution)/shard_map/ppermute | solution.py:54
  35.5 3.2 %collective-permute-start.13 = (bf16[8,8,7296]{2,1,0:T(8,128)(2,1)S(1)}, bf16[8,8,7296]{2,1,0:T(8,128)(2,1)S(1)}, u32[]{:S(2)}, u32[]{:S(2)}) collective-permute-start(bf16[8,8,7296]{2,1,0:T(8,128)(2,1)S(1)} %get-tuple-element.37), channel_id=1, source_target_pairs={{0,3},{1,0},{2,1},{3,2},{4,7},{5,4},{6,5},{7,6},{8,11},{9,8},{10,9... | collective-permute-start | bytes 2801672 | tf_op jit(solution)/shard_map/ppermute | solution.py:54
  42.8 5.6 %expert_acts.3.acts_ref = bf16[128,512]{1,0:T(8,128)(2,1)S(1)} custom-call(s32[2]{0:T(128)S(1)} %pad_add_fusion.info_ref, bf16[64,7296]{1,0:T(8,128)(2,1)S(1)} %bitcast.20, bf16[64,7296]{1,0:T(8,128)(2,1)} %bitcast.4.refs_1_, bf16[7168,256]{1,0:T(8,128)(2,1)S(1)} %copy-done.2, bf16[7168,256]{1,0:T(8,128)(2,1)} %collective-permute-done.6.refs_3_.refs_5_, ...), custom_call_target="tpu_custom_call" | custom-call | flops 1879048192 | bytes 1048576 | tf_op jit(solution)/shard_map/expert_acts/pallas_call | solution.py:122
  50.5 5.7 %expert_acts.4.acts_ref = bf16[128,512]{1,0:T(8,128)(2,1)S(1)} custom-call(s32[2]{0:T(128)S(1)} %pad_add_fusion.info_ref, bf16[64,7296]{1,0:T(8,128)(2,1)S(1)} %bitcast.19, bf16[64,7296]{1,0:T(8,128)(2,1)} %bitcast.8.refs_1_, bf16[7168,256]{1,0:T(8,128)(2,1)S(1)} %copy-done.2, bf16[7168,256]{1,0:T(8,128)(2,1)} %collective-permute-done.6.refs_3_.refs_5_, ...), custom_call_target="tpu_custom_call" | custom-call | flops 1879048192 | bytes 1048576 | tf_op jit(solution)/shard_map/expert_acts/pallas_call | solution.py:122
  57.0 3.6 %expert_outs.6 = (bf16[64,7168]{1,0:T(8,128)(2,1)S(1)}, bf16[64,7168]{1,0:T(8,128)(2,1)S(1)}) custom-call(bf16[128,512]{1,0:T(8,128)(2,1)S(1)} %expert_acts.4.acts_ref, bf16[256,7168]{1,0:T(8,128)(2,1)S(1)} %copy-done.1, bf16[256,7168]{1,0:T(8,128)(2,1)} %collective-permute-done.14.other_ref), custom_call_target="tpu_custom_call" | custom-call | flops 939524096 | bytes 1048576 | tf_op jit(solution)/shard_map/expert_outs/pallas_call | solution.py:153
  60.6 6.4 %collective-permute-done.11 = bf16[8,8,7296]{2,1,0:T(8,128)(2,1)S(1)} collective-permute-done((bf16[8,8,7296]{2,1,0:T(8,128)(2,1)}, bf16[8,8,7296]{2,1,0:T(8,128)(2,1)S(1)}, u32[]{:S(2)}, u32[]{:S(2)}) %collective-permute-start.11) | collective-permute-done | bytes 933920 | tf_op jit(solution)/shard_map/ppermute | solution.py:54
  67.0 3.4 %collective-permute-start.15 = (bf16[64,7168]{1,0:T(8,128)(2,1)S(1)}, bf16[64,7168]{1,0:T(8,128)(2,1)S(1)}, u32[]{:S(2)}, u32[]{:S(2)}) collective-permute-start(bf16[64,7168]{1,0:T(8,128)(2,1)S(1)} %get-tuple-element.49), channel_id=1, source_target_pairs={{0,3},{1,0},{2,1},{3,2},{4,7},{5,4},{6,5},{7,6},{8,11},{9,8},{10,9... | collective-permute-start | bytes 2752520 | tf_op jit(solution)/shard_map/ppermute | solution.py:54
  70.5 7.2 %expert_acts.5 = bf16[256,512]{1,0:T(8,128)(2,1)S(1)} custom-call(s32[2]{0:T(128)S(1)} %pad_add_fusion.info_ref, bf16[64,7296]{1,0:T(8,128)(2,1)S(1)} %bitcast.24, bf16[64,7296]{1,0:T(8,128)(2,1)S(1)} %bitcast.23, bf16[64,7296]{1,0:T(8,128)(2,1)S(1)} %bitcast.21, bf16[64,7296]{1,0:T(8,128)(2,1)S(1)} %bitcast.22, bf16[7168,256]{1,0:T(8,128)(2,1)S(1)} %copy-done.3, ...), custom_call_target="tpu_custom_call" | custom-call | flops 3758096384 | bytes 1048576 | tf_op jit(solution)/shard_map/expert_acts/pallas_call | solution.py:122
  77.6 3.2 %expert_outs.4 = (bf16[64,7168]{1,0:T(8,128)(2,1)S(1)}, bf16[64,7168]{1,0:T(8,128)(2,1)S(1)}) custom-call(bf16[128,512]{1,0:T(8,128)(2,1)S(1)} %slice.31.acts_ref, bf16[256,7168]{1,0:T(8,128)(2,1)S(1)} %copy-done.1, bf16[256,7168]{1,0:T(8,128)(2,1)} %collective-permute-done.14.other_ref), custom_call_target="tpu_custom_call" | custom-call | flops 939524096 | bytes 1048576 | tf_op jit(solution)/shard_map/expert_outs/pallas_call | solution.py:153
  81.3 3.7 %collective-permute-start.19 = (bf16[64,7168]{1,0:T(8,128)(2,1)S(1)}, bf16[64,7168]{1,0:T(8,128)(2,1)S(1)}, u32[]{:S(2)}, u32[]{:S(2)}) collective-permute-start(bf16[64,7168]{1,0:T(8,128)(2,1)S(1)} %get-tuple-element.59), channel_id=1, source_target_pairs={{0,3},{1,0},{2,1},{3,2},{4,7},{5,4},{6,5},{7,6},{8,11},{9,8},{10,9... | collective-permute-start | bytes 2752520 | tf_op jit(solution)/shard_map/ppermute | solution.py:54
  85.1 3.2 %expert_outs.7 = (bf16[64,7168]{1,0:T(8,128)(2,1)S(1)}, bf16[64,7168]{1,0:T(8,128)(2,1)S(1)}) custom-call(bf16[128,512]{1,0:T(8,128)(2,1)S(1)} %slice.25.acts_ref, bf16[256,7168]{1,0:T(8,128)(2,1)S(1)} %copy-done.1, bf16[256,7168]{1,0:T(8,128)(2,1)} %collective-permute-done.14.other_ref), custom_call_target="tpu_custom_call" | custom-call | flops 939524096 | bytes 1048576 | tf_op jit(solution)/shard_map/expert_outs/pallas_call | solution.py:153
  88.3 3.2 %expert_outs.5 = (bf16[64,7168]{1,0:T(8,128)(2,1)S(1)}, bf16[64,7168]{1,0:T(8,128)(2,1)S(1)}) custom-call(bf16[128,512]{1,0:T(8,128)(2,1)S(1)} %expert_acts.3.acts_ref, bf16[256,7168]{1,0:T(8,128)(2,1)S(1)} %copy-done.1, bf16[256,7168]{1,0:T(8,128)(2,1)} %collective-permute-done.14.other_ref), custom_call_target="tpu_custom_call" | custom-call | flops 939524096 | bytes 1048576 | tf_op jit(solution)/shard_map/expert_outs/pallas_call | solution.py:153
  91.5 4.5 %collective-permute-done.19 = bf16[64,7168]{1,0:T(8,128)(2,1)S(1)} collective-permute-done((bf16[64,7168]{1,0:T(8,128)(2,1)S(1)}, bf16[64,7168]{1,0:T(8,128)(2,1)S(1)}, u32[]{:S(2)}, u32[]{:S(2)}) %collective-permute-start.19) | collective-permute-done | bytes 917536 | tf_op jit(solution)/shard_map/ppermute | solution.py:54
  96.0 3.7 %collective-permute-done.17 = bf16[64,7168]{1,0:T(8,128)(2,1)S(1)} collective-permute-done((bf16[64,7168]{1,0:T(8,128)(2,1)S(1)}, bf16[64,7168]{1,0:T(8,128)(2,1)S(1)}, u32[]{:S(2)}, u32[]{:S(2)}) %collective-permute-start.17) | collective-permute-done | bytes 917536 | tf_op jit(solution)/shard_map/ppermute | solution.py:54
  100.2 3.2 %collective-permute-start.20 = (bf16[64,7168]{1,0:T(8,128)(2,1)S(1)}, bf16[64,7168]{1,0:T(8,128)(2,1)S(1)}, u32[]{:S(2)}, u32[]{:S(2)}) collective-permute-start(bf16[64,7168]{1,0:T(8,128)(2,1)S(1)} %get-tuple-element.60), channel_id=1, source_target_pairs={{0,3},{1,0},{2,1},{3,2},{4,7},{5,4},{6,5},{7,6},{8,11},{9,8},{10,9... | collective-permute-start | bytes 2752520 | tf_op jit(solution)/shard_map/ppermute | solution.py:54
  103.4 12.3 %collective-permute-done.18 = bf16[64,7168]{1,0:T(8,128)(2,1)S(1)} collective-permute-done((bf16[64,7168]{1,0:T(8,128)(2,1)S(1)}, bf16[64,7168]{1,0:T(8,128)(2,1)S(1)}, u32[]{:S(2)}, u32[]{:S(2)}) %collective-permute-start.18) | collective-permute-done | bytes 917536 | tf_op jit(solution)/shard_map/ppermute | solution.py:54
  116.1 3.9 %collective-permute-done.20 = bf16[64,7168]{1,0:T(8,128)(2,1)S(1)} collective-permute-done((bf16[64,7168]{1,0:T(8,128)(2,1)S(1)}, bf16[64,7168]{1,0:T(8,128)(2,1)S(1)}, u32[]{:S(2)}, u32[]{:S(2)}) %collective-permute-start.20) | collective-permute-done | bytes 917536 | tf_op jit(solution)/shard_map/ppermute | solution.py:54
  126.2 5.3 %collective-permute-done.23 = bf16[32,7168]{1,0:T(8,128)(2,1)S(1)} collective-permute-done((bf16[32,7168]{1,0:T(8,128)(2,1)S(1)}, bf16[32,7168]{1,0:T(8,128)(2,1)S(1)}, u32[]{:S(2)}, u32[]{:S(2)}) %collective-permute-start.23) | collective-permute-done | bytes 458784 | tf_op jit(solution)/shard_map/ppermute | solution.py:54
  131.4 6.6 %collective-permute-done.22 = bf16[32,7168]{1,0:T(8,128)(2,1)S(1)} collective-permute-done((bf16[32,7168]{1,0:T(8,128)(2,1)S(1)}, bf16[32,7168]{1,0:T(8,128)(2,1)S(1)}, u32[]{:S(2)}, u32[]{:S(2)}) %collective-permute-start.22) | collective-permute-done | bytes 458784 | tf_op jit(solution)/shard_map/ppermute | solution.py:54
  146.6 2.2 %fusion.15 = f32[8,576]{1,0:T(8,128)S(1)} fusion(bf16[7168,576]{0,1:T(8,128)(2,1)S(1)} %bitcast.30, bf16[8,7168]{1,0:T(8,128)(2,1)S(1)} %get-tuple-element.66, f32[7168]{0:T(1024)S(1)} %copy-done.9, f32[8]{0:T(128)S(1)} %add_rsqrt_fusion.1), kind=kOutput, calls=%fused_computation.27 | convolution fusion | flops 66289664 | bytes 8419360 | tf_op jit(solution)/shard_map/dot_general | solution.py:258
  (103 shorter events, 42.9 us)
Async XLA Ops:
  0.6 29.0 %collective-permute-start.6 = (bf16[7168,256]{1,0:T(8,128)(2,1)}, bf16[7168,256]{1,0:T(8,128)(2,1)}, u32[]{:S(2)}, u32[]{:S(2)}) collective-permute-start(bf16[7168,256]{1,0:T(8,128)(2,1)} %refs_4_.5), channel_id=1, source_target_pairs={{0,64},{1,65},{2,66},{3,67},{4,68},{5,69},{6,70},{7,71},{8,72},{9,... | collective-permute-start | bytes 11010056 | tf_op jit(solution)/shard_map/ppermute | solution.py:58
  0.7 28.9 %collective-permute-start.7 = (bf16[7168,256]{1,0:T(8,128)(2,1)}, bf16[7168,256]{1,0:T(8,128)(2,1)}, u32[]{:S(2)}, u32[]{:S(2)}) collective-permute-start(bf16[7168,256]{1,0:T(8,128)(2,1)} %refs_6_.1), channel_id=1, source_target_pairs={{0,64},{1,65},{2,66},{3,67},{4,68},{5,69},{6,70},{7,71},{8,72},{9,... | collective-permute-start | bytes 11010056 | tf_op jit(solution)/shard_map/ppermute | solution.py:58
  5.7 6.4 %collective-permute-start.1 = (bf16[1,8,7296]{2,1,0:T(8,128)(2,1)S(1)}, bf16[1,8,7296]{2,1,0:T(8,128)(2,1)S(1)}, u32[]{:S(2)}, u32[]{:S(2)}) collective-permute-start(bf16[1,8,7296]{2,1,0:T(8,128)(2,1)S(1)} %bitcast.26), channel_id=1, source_target_pairs={{0,32},{1,33},{2,34},{3,35},{4,36},{5,37},{6,38},{7,39},{8,40},{9,... | collective-permute-start | bytes 350216 | tf_op jit(solution)/shard_map/ppermute | solution.py:54
  13.4 9.8 %collective-permute-start.3 = (bf16[4,8,7296]{2,1,0:T(8,128)(2,1)S(1)}, bf16[4,8,7296]{2,1,0:T(8,128)(2,1)S(1)}, u32[]{:S(2)}, u32[]{:S(2)}) collective-permute-start(bf16[4,8,7296]{2,1,0:T(8,128)(2,1)S(1)} %join.2.refs_0_), channel_id=1, source_target_pairs={{0,4},{1,5},{2,6},{3,7},{4,8},{5,9},{6,10},{7,11},{8,12},{9,13},{1... | collective-permute-start | bytes 1400840 | tf_op jit(solution)/shard_map/ppermute | solution.py:54
  15.2 14.4 %collective-permute-start.4 = (bf16[4,8,7296]{2,1,0:T(8,128)(2,1)S(1)}, bf16[4,8,7296]{2,1,0:T(8,128)(2,1)S(1)}, u32[]{:S(2)}, u32[]{:S(2)}) collective-permute-start(bf16[4,8,7296]{2,1,0:T(8,128)(2,1)S(1)} %join.2.refs_0_), channel_id=1, source_target_pairs={{0,8},{1,9},{2,10},{3,11},{4,12},{5,13},{6,14},{7,15},{8,0},{9,1},... | collective-permute-start | bytes 1400840 | tf_op jit(solution)/shard_map/ppermute | solution.py:54
  18.1 11.5 %collective-permute-start.5 = (bf16[4,8,7296]{2,1,0:T(8,128)(2,1)S(1)}, bf16[4,8,7296]{2,1,0:T(8,128)(2,1)S(1)}, u32[]{:S(2)}, u32[]{:S(2)}) collective-permute-start(bf16[4,8,7296]{2,1,0:T(8,128)(2,1)S(1)} %join.2.refs_0_), channel_id=1, source_target_pairs={{0,12},{1,13},{2,14},{3,15},{4,0},{5,1},{6,2},{7,3},{8,4},{9,5},{1... | collective-permute-start | bytes 1400840 | tf_op jit(solution)/shard_map/ppermute | solution.py:54
  31.1 25.9 %collective-permute-start.14 = (bf16[256,7168]{1,0:T(8,128)(2,1)}, bf16[256,7168]{1,0:T(8,128)(2,1)}, u32[]{:S(2)}, u32[]{:S(2)}) collective-permute-start(bf16[256,7168]{1,0:T(8,128)(2,1)} %mine_ref.7), channel_id=1, source_target_pairs={{0,64},{1,65},{2,66},{3,67},{4,68},{5,69},{6,70},{7,71},{8,72},{9,... | collective-permute-start | bytes 11010056 | tf_op jit(solution)/shard_map/ppermute | solution.py:58
  31.2 17.2 %collective-permute-start.8 = (bf16[8,8,7296]{2,1,0:T(8,128)(2,1)S(1)}, bf16[8,8,7296]{2,1,0:T(8,128)(2,1)S(1)}, u32[]{:S(2)}, u32[]{:S(2)}) collective-permute-start(bf16[8,8,7296]{2,1,0:T(8,128)(2,1)S(1)} %get-tuple-element.37), channel_id=1, source_target_pairs={{0,1},{1,2},{2,3},{3,0},{4,5},{5,6},{6,7},{7,4},{8,9},{9,10},{10,1... | collective-permute-start | bytes 2801672 | tf_op jit(solution)/shard_map/ppermute | solution.py:54
  33.2 15.2 %collective-permute-start.9 = (bf16[8,8,7296]{2,1,0:T(8,128)(2,1)}, bf16[8,8,7296]{2,1,0:T(8,128)(2,1)}, u32[]{:S(2)}, u32[]{:S(2)}) collective-permute-start(bf16[8,8,7296]{2,1,0:T(8,128)(2,1)} %get-tuple-element.38), channel_id=1, source_target_pairs={{0,3},{1,0},{2,1},{3,2},{4,7},{5,4},{6,5},{7,6},{8,11},{9,8},{10,9... | collective-permute-start | bytes 2801672 | tf_op jit(solution)/shard_map/ppermute | solution.py:54
  35.5 21.4 %collective-permute-start.12 = (bf16[8,8,7296]{2,1,0:T(8,128)(2,1)}, bf16[8,8,7296]{2,1,0:T(8,128)(2,1)S(1)}, u32[]{:S(2)}, u32[]{:S(2)}) collective-permute-start(bf16[8,8,7296]{2,1,0:T(8,128)(2,1)} %get-tuple-element.38), channel_id=1, source_target_pairs={{0,1},{1,2},{2,3},{3,0},{4,5},{5,6},{6,7},{7,4},{8,9},{9,10},{10,1... | collective-permute-start | bytes 2801672 | tf_op jit(solution)/shard_map/ppermute | solution.py:54
  35.5 21.5 %collective-permute-start.13 = (bf16[8,8,7296]{2,1,0:T(8,128)(2,1)S(1)}, bf16[8,8,7296]{2,1,0:T(8,128)(2,1)S(1)}, u32[]{:S(2)}, u32[]{:S(2)}) collective-permute-start(bf16[8,8,7296]{2,1,0:T(8,128)(2,1)S(1)} %get-tuple-element.37), channel_id=1, source_target_pairs={{0,3},{1,0},{2,1},{3,2},{4,7},{5,4},{6,5},{7,6},{8,11},{9,8},{10,9... | collective-permute-start | bytes 2801672 | tf_op jit(solution)/shard_map/ppermute | solution.py:54
  48.4 18.6 %collective-permute-start.11 = (bf16[8,8,7296]{2,1,0:T(8,128)(2,1)}, bf16[8,8,7296]{2,1,0:T(8,128)(2,1)S(1)}, u32[]{:S(2)}, u32[]{:S(2)}) collective-permute-start(bf16[8,8,7296]{2,1,0:T(8,128)(2,1)} %collective-permute-done.9), channel_id=1, source_target_pairs={{0,3},{1,0},{2,1},{3,2},{4,7},{5,4},{6,5},{7,6},{8,11},{9,8},{10,9... | collective-permute-start | bytes 2801672 | tf_op jit(solution)/shard_map/ppermute | solution.py:54
  50.5 19.9 %collective-permute-start.10 = (bf16[8,8,7296]{2,1,0:T(8,128)(2,1)S(1)}, bf16[8,8,7296]{2,1,0:T(8,128)(2,1)S(1)}, u32[]{:S(2)}, u32[]{:S(2)}) collective-permute-start(bf16[8,8,7296]{2,1,0:T(8,128)(2,1)S(1)} %collective-permute-done.8), channel_id=1, source_target_pairs={{0,1},{1,2},{2,3},{3,0},{4,5},{5,6},{6,7},{7,4},{8,9},{9,10},{10,1... | collective-permute-start | bytes 2801672 | tf_op jit(solution)/shard_map/ppermute | solution.py:54
  67.0 14.3 %collective-permute-start.15 = (bf16[64,7168]{1,0:T(8,128)(2,1)S(1)}, bf16[64,7168]{1,0:T(8,128)(2,1)S(1)}, u32[]{:S(2)}, u32[]{:S(2)}) collective-permute-start(bf16[64,7168]{1,0:T(8,128)(2,1)S(1)} %get-tuple-element.49), channel_id=1, source_target_pairs={{0,3},{1,0},{2,1},{3,2},{4,7},{5,4},{6,5},{7,6},{8,11},{9,8},{10,9... | collective-permute-start | bytes 2752520 | tf_op jit(solution)/shard_map/ppermute | solution.py:54
  70.4 14.6 %collective-permute-start.16 = (bf16[64,7168]{1,0:T(8,128)(2,1)S(1)}, bf16[64,7168]{1,0:T(8,128)(2,1)S(1)}, u32[]{:S(2)}, u32[]{:S(2)}) collective-permute-start(bf16[64,7168]{1,0:T(8,128)(2,1)S(1)} %get-tuple-element.53), channel_id=1, source_target_pairs={{0,1},{1,2},{2,3},{3,0},{4,5},{5,6},{6,7},{7,4},{8,9},{9,10},{10,1... | collective-permute-start | bytes 2752520 | tf_op jit(solution)/shard_map/ppermute | solution.py:54
  81.3 14.6 %collective-permute-start.19 = (bf16[64,7168]{1,0:T(8,128)(2,1)S(1)}, bf16[64,7168]{1,0:T(8,128)(2,1)S(1)}, u32[]{:S(2)}, u32[]{:S(2)}) collective-permute-start(bf16[64,7168]{1,0:T(8,128)(2,1)S(1)} %get-tuple-element.59), channel_id=1, source_target_pairs={{0,3},{1,0},{2,1},{3,2},{4,7},{5,4},{6,5},{7,6},{8,11},{9,8},{10,9... | collective-permute-start | bytes 2752520 | tf_op jit(solution)/shard_map/ppermute | solution.py:54
  85.0 14.6 %collective-permute-start.17 = (bf16[64,7168]{1,0:T(8,128)(2,1)S(1)}, bf16[64,7168]{1,0:T(8,128)(2,1)S(1)}, u32[]{:S(2)}, u32[]{:S(2)}) collective-permute-start(bf16[64,7168]{1,0:T(8,128)(2,1)S(1)} %get-tuple-element.54), channel_id=1, source_target_pairs={{0,1},{1,2},{2,3},{3,0},{4,5},{5,6},{6,7},{7,4},{8,9},{9,10},{10,1... | collective-permute-start | bytes 2752520 | tf_op jit(solution)/shard_map/ppermute | solution.py:54
  100.1 15.6 %collective-permute-start.18 = (bf16[64,7168]{1,0:T(8,128)(2,1)S(1)}, bf16[64,7168]{1,0:T(8,128)(2,1)S(1)}, u32[]{:S(2)}, u32[]{:S(2)}) collective-permute-start(bf16[64,7168]{1,0:T(8,128)(2,1)S(1)} %get-tuple-element.55), channel_id=1, source_target_pairs={{0,1},{1,2},{2,3},{3,0},{4,5},{5,6},{6,7},{7,4},{8,9},{9,10},{10,1... | collective-permute-start | bytes 2752520 | tf_op jit(solution)/shard_map/ppermute | solution.py:54
  100.2 19.8 %collective-permute-start.20 = (bf16[64,7168]{1,0:T(8,128)(2,1)S(1)}, bf16[64,7168]{1,0:T(8,128)(2,1)S(1)}, u32[]{:S(2)}, u32[]{:S(2)}) collective-permute-start(bf16[64,7168]{1,0:T(8,128)(2,1)S(1)} %get-tuple-element.60), channel_id=1, source_target_pairs={{0,3},{1,0},{2,1},{3,2},{4,7},{5,4},{6,5},{7,6},{8,11},{9,8},{10,9... | collective-permute-start | bytes 2752520 | tf_op jit(solution)/shard_map/ppermute | solution.py:54
  120.4 11.0 %collective-permute-start.23 = (bf16[32,7168]{1,0:T(8,128)(2,1)S(1)}, bf16[32,7168]{1,0:T(8,128)(2,1)S(1)}, u32[]{:S(2)}, u32[]{:S(2)}) collective-permute-start(bf16[32,7168]{1,0:T(8,128)(2,1)S(1)} %get-tuple-element.68), channel_id=1, source_target_pairs={{0,4},{1,5},{2,6},{3,7},{4,8},{5,9},{6,10},{7,11},{8,12},{9,13},{1... | collective-permute-start | bytes 1376264 | tf_op jit(solution)/shard_map/ppermute | solution.py:54
  122.1 15.9 %collective-permute-start.22 = (bf16[32,7168]{1,0:T(8,128)(2,1)S(1)}, bf16[32,7168]{1,0:T(8,128)(2,1)S(1)}, u32[]{:S(2)}, u32[]{:S(2)}) collective-permute-start(bf16[32,7168]{1,0:T(8,128)(2,1)S(1)} %get-tuple-element.67), channel_id=1, source_target_pairs={{0,8},{1,9},{2,10},{3,11},{4,12},{5,13},{6,14},{7,15},{8,0},{9,1},... | collective-permute-start | bytes 1376264 | tf_op jit(solution)/shard_map/ppermute | solution.py:54
  124.3 14.2 %collective-permute-start.21 = (bf16[32,7168]{1,0:T(8,128)(2,1)S(1)}, bf16[32,7168]{1,0:T(8,128)(2,1)S(1)}, u32[]{:S(2)}, u32[]{:S(2)}) collective-permute-start(bf16[32,7168]{1,0:T(8,128)(2,1)S(1)} %split.25), channel_id=1, source_target_pairs={{0,12},{1,13},{2,14},{3,15},{4,0},{5,1},{6,2},{7,3},{8,4},{9,5},{1... | collective-permute-start | bytes 1376264 | tf_op jit(solution)/shard_map/ppermute | solution.py:54
  138.8 6.5 %collective-permute-start.25 = (bf16[8,7168]{1,0:T(8,128)(2,1)S(1)}, bf16[8,7168]{1,0:T(8,128)(2,1)S(1)}, u32[]{:S(2)}, u32[]{:S(2)}) collective-permute-start(bf16[8,7168]{1,0:T(8,128)(2,1)S(1)} %get-tuple-element.71), channel_id=1, source_target_pairs={{0,32},{1,33},{2,34},{3,35},{4,36},{5,37},{6,38},{7,39},{8,40},{9,... | collective-permute-start | bytes 344072 | tf_op jit(solution)/shard_map/ppermute | solution.py:54
  138.9 7.4 %collective-permute-start.24 = (bf16[8,7168]{1,0:T(8,128)(2,1)S(1)}, bf16[8,7168]{1,0:T(8,128)(2,1)S(1)}, u32[]{:S(2)}, u32[]{:S(2)}) collective-permute-start(bf16[8,7168]{1,0:T(8,128)(2,1)S(1)} %get-tuple-element.69), channel_id=1, source_target_pairs={{0,48},{1,49},{2,50},{3,51},{4,52},{5,53},{6,54},{7,55},{8,56},{9,... | collective-permute-start | bytes 344072 | tf_op jit(solution)/shard_map/ppermute | solution.py:54
  (17 other events, 296.0 us)

commit v5 on v4

--- a/solution.py
+++ b/solution.py
@@ -93,6 +93,35 @@
         compiler_params=pltpu.CompilerParams(vmem_limit_bytes=1 << 20),
         name="join",
     )(*blocks)
+
+
+def front_body(resid_ref, gain_ref, ids_ref, weights_ref, out_ref):
+    width = resid_ref.shape[1]
+    out_ref[:, :width] = rms_scale(resid_ref[...], gain_ref[...]).astype(jnp.bfloat16)
+    lane = lax.broadcasted_iota(jnp.int32, (resid_ref.shape[0], LANES), 1)
+    expert = jnp.where(lane < 3 * EXPERTS, lane % EXPERTS, -1)
+    dense = jnp.zeros(lane.shape, jnp.float32)
+    for number in range(ids_ref.shape[1]):
+        hit = ids_ref[:, number : number + 1] == expert
+        dense = dense + jnp.where(hit, weights_ref[:, number : number + 1], 0.0)
+    high = dense.astype(jnp.bfloat16).astype(jnp.float32)
+    rest = dense - high
+    middle = rest.astype(jnp.bfloat16).astype(jnp.float32)
+    part = jnp.where(lane < EXPERTS, high, jnp.where(lane < 2 * EXPERTS, middle, rest - middle))
+    out_ref[:, width:] = part.astype(jnp.bfloat16)
+
+
+def front(resid, gain_vec, ids, weights):
+    rows, width = resid.shape
+    vmem = pl.BlockSpec(memory_space=pltpu.VMEM)
+    return pl.pallas_call(
+        front_body,
+        out_shape=jax.ShapeDtypeStruct((rows, width + LANES), jnp.bfloat16),
+        in_specs=[vmem] * 4,
+        out_specs=vmem,
+        compiler_params=pltpu.CompilerParams(vmem_limit_bytes=58 << 20),
+        name="front",
+    )(resid, gain_vec.reshape(1, width), ids, weights)
 
 
 def act_body(info_ref, *refs):
@@ -190,23 +219,7 @@
     sec = lax.axis_index("sec")
     chip_expert = lax.axis_index("dev") // (SIDE**3 // (EXPERTS // 2))
     gate_other = swap_cores(w_gate)
-    normed = rms_scale(resid, ffn_gain).astype(jnp.bfloat16)
-    dense_weights = jnp.sum(
-        jnp.where(
-            expert_ids[:, :, None] == jnp.arange(EXPERTS, dtype=jnp.int32)[None, None, :],
-            gate_weights[:, :, None],
-            0.0,
-        ),
-        axis=1,
-    )
-    high = dense_weights.astype(jnp.bfloat16)
-    rest = dense_weights - high.astype(jnp.float32)
-    middle = rest.astype(jnp.bfloat16)
-    low = (rest - middle.astype(jnp.float32)).astype(jnp.bfloat16)
-    weight_cols = jnp.concatenate(
-        [high, middle, low, jnp.zeros((tok_count, LANES - 3 * EXPERTS), jnp.bfloat16)], axis=1
-    )
-    rows = jnp.concatenate([normed, weight_cols], axis=1)
+    rows = front(resid, ffn_gain, expert_ids, gate_weights)
     up_other = swap_cores(w_up)
     rows = rows[None]
     (rows,) = join([rows] + [shift(rows, 0, back) for back in range(1, SIDE)], 1)

time: 154 us -> 153 us (level)
  other arithmetic: 6.11 us -> 3.23 us
  Pallas kernels: 33.8 us -> 35.5 us
    pallas_call x0 -> x1, Pallas kernels: none -> 1.75 us  [front(): pl.pallas_call(front_body, out_shape=jax.ShapeDtypeStruct((rows, width +...]
    unnamed x28 -> x30, local copies, waits for them, and re-layouts: 4.14 us -> 5.04 us
  transfers between devices with their start and end apart: 27 -> 27, of which waited for: 19 -> 19; matrix products, arithmetic and copies ran while one was open for 3% -> 1% of each run, Pallas kernels for 21% -> 22%
where the time goes in v5:
time: 153 us; the launch traced here: 152 us
  waiting for transfers between devices  63.3 us (41%)
  starting transfers between devices  39 us (25%)
  Pallas kernels  35.5 us (23%)
  local copies, waits for them, and re-layouts  5.18 us (3%)
  matrix products  5.13 us (3%)
  other arithmetic  3.23 us (2%)
    ppermute x24, waiting for transfers between devices, shift(): return lax.ppermute(values, AXES, pairs)  63.3 us
    ppermute x24, starting transfers between devices, shift(): return lax.ppermute(values, AXES, pairs)  38.3 us
    pallas_call x3, Pallas kernels, expert_acts(): pl.pallas_call(act_body, out_shape=jax.ShapeDtypeStruct((tokens, 2 * wide...  18.5 us
    pallas_call x4, Pallas kernels, expert_outs(): pl.pallas_call(down_body, out_shape=[jax.ShapeDtypeStruct((tokens // coun...  13.2 us
    unnamed x30, local copies, waits for them, and re-layouts  5.04 us
  transfers between devices with their start and end apart: 27, of which 19 were waited for; matrix products, arithmetic and copies ran while one was open for 1% of the time, Pallas kernels for 22%

profile of v5, /device:TPU:2, one launch (start us, length us, event | category | flops | bytes accessed | tf_op | source)
XLA Modules:
  0.0 152.3 jit_solution(6228095177868090042)
XLA Ops:
  5.5 2.2 %collective-permute-start.2 = (bf16[1,8,7296]{2,1,0:T(8,128)(2,1)}, bf16[1,8,7296]{2,1,0:T(8,128)(2,1)S(1)}, u32[]{:S(2)}, u32[]{:S(2)}) collective-permute-start(bf16[1,8,7296]{2,1,0:T(8,128)(2,1)} %bitcast.28), channel_id=1, source_target_pairs={{0,48},{1,49},{2,50},{3,51},{4,52},{5,53},{6,54},{7,55},{8,56},{9,... | collective-permute-start | bytes 350216 | tf_op jit(solution)/shard_map/ppermute | solution.py:54
  8.0 3.1 %collective-permute-done.1.refs_2_ = bf16[1,8,7296]{2,1,0:T(8,128)(2,1)S(1)} collective-permute-done((bf16[1,8,7296]{2,1,0:T(8,128)(2,1)}, bf16[1,8,7296]{2,1,0:T(8,128)(2,1)S(1)}, u32[]{:S(2)}, u32[]{:S(2)}) %collective-permute-start.1) | collective-permute-done | bytes 116768 | tf_op jit(solution)/shard_map/ppermute | solution.py:54
  15.0 2.9 %collective-permute-start.4 = (bf16[4,8,7296]{2,1,0:T(8,128)(2,1)S(1)}, bf16[4,8,7296]{2,1,0:T(8,128)(2,1)S(1)}, u32[]{:S(2)}, u32[]{:S(2)}) collective-permute-start(bf16[4,8,7296]{2,1,0:T(8,128)(2,1)S(1)} %join.2.refs_0_), channel_id=1, source_target_pairs={{0,8},{1,9},{2,10},{3,11},{4,12},{5,13},{6,14},{7,15},{8,0},{9,1},... | collective-permute-start | bytes 1400840 | tf_op jit(solution)/shard_map/ppermute | solution.py:54
  19.3 3.9 %collective-permute-done.3.refs_1_ = bf16[4,8,7296]{2,1,0:T(8,128)(2,1)S(1)} collective-permute-done((bf16[4,8,7296]{2,1,0:T(8,128)(2,1)S(1)}, bf16[4,8,7296]{2,1,0:T(8,128)(2,1)S(1)}, u32[]{:S(2)}, u32[]{:S(2)}) %collective-permute-start.3) | collective-permute-done | bytes 466976 | tf_op jit(solution)/shard_map/ppermute | solution.py:54
  23.1 6.3 %collective-permute-done.4.refs_2_ = bf16[4,8,7296]{2,1,0:T(8,128)(2,1)S(1)} collective-permute-done((bf16[4,8,7296]{2,1,0:T(8,128)(2,1)S(1)}, bf16[4,8,7296]{2,1,0:T(8,128)(2,1)S(1)}, u32[]{:S(2)}, u32[]{:S(2)}) %collective-permute-start.4) | collective-permute-done | bytes 466976 | tf_op jit(solution)/shard_map/ppermute | solution.py:54
  35.4 3.2 %collective-permute-start.13 = (bf16[8,8,7296]{2,1,0:T(8,128)(2,1)S(1)}, bf16[8,8,7296]{2,1,0:T(8,128)(2,1)S(1)}, u32[]{:S(2)}, u32[]{:S(2)}) collective-permute-start(bf16[8,8,7296]{2,1,0:T(8,128)(2,1)S(1)} %get-tuple-element.37), channel_id=1, source_target_pairs={{0,3},{1,0},{2,1},{3,2},{4,7},{5,4},{6,5},{7,6},{8,11},{9,8},{10,9... | collective-permute-start | bytes 2801672 | tf_op jit(solution)/shard_map/ppermute | solution.py:54
  42.7 5.6 %expert_acts.3.acts_ref = bf16[128,512]{1,0:T(8,128)(2,1)S(1)} custom-call(s32[2]{0:T(128)S(1)} %pad_add_fusion.info_ref, bf16[64,7296]{1,0:T(8,128)(2,1)S(1)} %bitcast.21, bf16[64,7296]{1,0:T(8,128)(2,1)} %bitcast.5.refs_1_, bf16[7168,256]{1,0:T(8,128)(2,1)S(1)} %copy-done.2, bf16[7168,256]{1,0:T(8,128)(2,1)} %collective-permute-done.6.refs_3_.refs_5_, ...), custom_call_target="tpu_custom_call" | custom-call | flops 1879048192 | bytes 1048576 | tf_op jit(solution)/shard_map/expert_acts/pallas_call | solution.py:151
  50.4 5.7 %expert_acts.4.acts_ref = bf16[128,512]{1,0:T(8,128)(2,1)S(1)} custom-call(s32[2]{0:T(128)S(1)} %pad_add_fusion.info_ref, bf16[64,7296]{1,0:T(8,128)(2,1)S(1)} %bitcast.20, bf16[64,7296]{1,0:T(8,128)(2,1)} %bitcast.9.refs_1_, bf16[7168,256]{1,0:T(8,128)(2,1)S(1)} %copy-done.2, bf16[7168,256]{1,0:T(8,128)(2,1)} %collective-permute-done.6.refs_3_.refs_5_, ...), custom_call_target="tpu_custom_call" | custom-call | flops 1879048192 | bytes 1048576 | tf_op jit(solution)/shard_map/expert_acts/pallas_call | solution.py:151
  56.9 3.6 %expert_outs.6 = (bf16[64,7168]{1,0:T(8,128)(2,1)S(1)}, bf16[64,7168]{1,0:T(8,128)(2,1)S(1)}) custom-call(bf16[128,512]{1,0:T(8,128)(2,1)S(1)} %expert_acts.4.acts_ref, bf16[256,7168]{1,0:T(8,128)(2,1)S(1)} %copy-done.1, bf16[256,7168]{1,0:T(8,128)(2,1)} %collective-permute-done.14.other_ref), custom_call_target="tpu_custom_call" | custom-call | flops 939524096 | bytes 1048576 | tf_op jit(solution)/shard_map/expert_outs/pallas_call | solution.py:182
  60.5 6.4 %collective-permute-done.11 = bf16[8,8,7296]{2,1,0:T(8,128)(2,1)S(1)} collective-permute-done((bf16[8,8,7296]{2,1,0:T(8,128)(2,1)}, bf16[8,8,7296]{2,1,0:T(8,128)(2,1)S(1)}, u32[]{:S(2)}, u32[]{:S(2)}) %collective-permute-start.11) | collective-permute-done | bytes 933920 | tf_op jit(solution)/shard_map/ppermute | solution.py:54
  66.9 3.4 %collective-permute-start.15 = (bf16[64,7168]{1,0:T(8,128)(2,1)S(1)}, bf16[64,7168]{1,0:T(8,128)(2,1)S(1)}, u32[]{:S(2)}, u32[]{:S(2)}) collective-permute-start(bf16[64,7168]{1,0:T(8,128)(2,1)S(1)} %get-tuple-element.49), channel_id=1, source_target_pairs={{0,3},{1,0},{2,1},{3,2},{4,7},{5,4},{6,5},{7,6},{8,11},{9,8},{10,9... | collective-permute-start | bytes 2752520 | tf_op jit(solution)/shard_map/ppermute | solution.py:54
  70.3 7.2 %expert_acts.5 = bf16[256,512]{1,0:T(8,128)(2,1)S(1)} custom-call(s32[2]{0:T(128)S(1)} %pad_add_fusion.info_ref, bf16[64,7296]{1,0:T(8,128)(2,1)S(1)} %bitcast.25, bf16[64,7296]{1,0:T(8,128)(2,1)S(1)} %bitcast.24, bf16[64,7296]{1,0:T(8,128)(2,1)S(1)} %bitcast.22, bf16[64,7296]{1,0:T(8,128)(2,1)S(1)} %bitcast.23, bf16[7168,256]{1,0:T(8,128)(2,1)S(1)} %copy-done.3, ...), custom_call_target="tpu_custom_call" | custom-call | flops 3758096384 | bytes 1048576 | tf_op jit(solution)/shard_map/expert_acts/pallas_call | solution.py:151
  77.5 3.2 %expert_outs.4 = (bf16[64,7168]{1,0:T(8,128)(2,1)S(1)}, bf16[64,7168]{1,0:T(8,128)(2,1)S(1)}) custom-call(bf16[128,512]{1,0:T(8,128)(2,1)S(1)} %slice.31.acts_ref, bf16[256,7168]{1,0:T(8,128)(2,1)S(1)} %copy-done.1, bf16[256,7168]{1,0:T(8,128)(2,1)} %collective-permute-done.14.other_ref), custom_call_target="tpu_custom_call" | custom-call | flops 939524096 | bytes 1048576 | tf_op jit(solution)/shard_map/expert_outs/pallas_call | solution.py:182
  81.2 3.7 %collective-permute-start.19 = (bf16[64,7168]{1,0:T(8,128)(2,1)S(1)}, bf16[64,7168]{1,0:T(8,128)(2,1)S(1)}, u32[]{:S(2)}, u32[]{:S(2)}) collective-permute-start(bf16[64,7168]{1,0:T(8,128)(2,1)S(1)} %get-tuple-element.59), channel_id=1, source_target_pairs={{0,3},{1,0},{2,1},{3,2},{4,7},{5,4},{6,5},{7,6},{8,11},{9,8},{10,9... | collective-permute-start | bytes 2752520 | tf_op jit(solution)/shard_map/ppermute | solution.py:54
  84.9 3.2 %expert_outs.7 = (bf16[64,7168]{1,0:T(8,128)(2,1)S(1)}, bf16[64,7168]{1,0:T(8,128)(2,1)S(1)}) custom-call(bf16[128,512]{1,0:T(8,128)(2,1)S(1)} %slice.25.acts_ref, bf16[256,7168]{1,0:T(8,128)(2,1)S(1)} %copy-done.1, bf16[256,7168]{1,0:T(8,128)(2,1)} %collective-permute-done.14.other_ref), custom_call_target="tpu_custom_call" | custom-call | flops 939524096 | bytes 1048576 | tf_op jit(solution)/shard_map/expert_outs/pallas_call | solution.py:182
  88.1 3.2 %expert_outs.5 = (bf16[64,7168]{1,0:T(8,128)(2,1)S(1)}, bf16[64,7168]{1,0:T(8,128)(2,1)S(1)}) custom-call(bf16[128,512]{1,0:T(8,128)(2,1)S(1)} %expert_acts.3.acts_ref, bf16[256,7168]{1,0:T(8,128)(2,1)S(1)} %copy-done.1, bf16[256,7168]{1,0:T(8,128)(2,1)} %collective-permute-done.14.other_ref), custom_call_target="tpu_custom_call" | custom-call | flops 939524096 | bytes 1048576 | tf_op jit(solution)/shard_map/expert_outs/pallas_call | solution.py:182
  91.3 4.5 %collective-permute-done.19 = bf16[64,7168]{1,0:T(8,128)(2,1)S(1)} collective-permute-done((bf16[64,7168]{1,0:T(8,128)(2,1)S(1)}, bf16[64,7168]{1,0:T(8,128)(2,1)S(1)}, u32[]{:S(2)}, u32[]{:S(2)}) %collective-permute-start.19) | collective-permute-done | bytes 917536 | tf_op jit(solution)/shard_map/ppermute | solution.py:54
  95.8 3.7 %collective-permute-done.17 = bf16[64,7168]{1,0:T(8,128)(2,1)S(1)} collective-permute-done((bf16[64,7168]{1,0:T(8,128)(2,1)S(1)}, bf16[64,7168]{1,0:T(8,128)(2,1)S(1)}, u32[]{:S(2)}, u32[]{:S(2)}) %collective-permute-start.17) | collective-permute-done | bytes 917536 | tf_op jit(solution)/shard_map/ppermute | solution.py:54
  100.1 3.2 %collective-permute-start.20 = (bf16[64,7168]{1,0:T(8,128)(2,1)S(1)}, bf16[64,7168]{1,0:T(8,128)(2,1)S(1)}, u32[]{:S(2)}, u32[]{:S(2)}) collective-permute-start(bf16[64,7168]{1,0:T(8,128)(2,1)S(1)} %get-tuple-element.60), channel_id=1, source_target_pairs={{0,3},{1,0},{2,1},{3,2},{4,7},{5,4},{6,5},{7,6},{8,11},{9,8},{10,9... | collective-permute-start | bytes 2752520 | tf_op jit(solution)/shard_map/ppermute | solution.py:54
  103.3 12.3 %collective-permute-done.18 = bf16[64,7168]{1,0:T(8,128)(2,1)S(1)} collective-permute-done((bf16[64,7168]{1,0:T(8,128)(2,1)S(1)}, bf16[64,7168]{1,0:T(8,128)(2,1)S(1)}, u32[]{:S(2)}, u32[]{:S(2)}) %collective-permute-start.18) | collective-permute-done | bytes 917536 | tf_op jit(solution)/shard_map/ppermute | solution.py:54
  115.9 3.9 %collective-permute-done.20 = bf16[64,7168]{1,0:T(8,128)(2,1)S(1)} collective-permute-done((bf16[64,7168]{1,0:T(8,128)(2,1)S(1)}, bf16[64,7168]{1,0:T(8,128)(2,1)S(1)}, u32[]{:S(2)}, u32[]{:S(2)}) %collective-permute-start.20) | collective-permute-done | bytes 917536 | tf_op jit(solution)/shard_map/ppermute | solution.py:54
  126.0 5.3 %collective-permute-done.23 = bf16[32,7168]{1,0:T(8,128)(2,1)S(1)} collective-permute-done((bf16[32,7168]{1,0:T(8,128)(2,1)S(1)}, bf16[32,7168]{1,0:T(8,128)(2,1)S(1)}, u32[]{:S(2)}, u32[]{:S(2)}) %collective-permute-start.23) | collective-permute-done | bytes 458784 | tf_op jit(solution)/shard_map/ppermute | solution.py:54
  131.3 6.6 %collective-permute-done.22 = bf16[32,7168]{1,0:T(8,128)(2,1)S(1)} collective-permute-done((bf16[32,7168]{1,0:T(8,128)(2,1)S(1)}, bf16[32,7168]{1,0:T(8,128)(2,1)S(1)}, u32[]{:S(2)}, u32[]{:S(2)}) %collective-permute-start.22) | collective-permute-done | bytes 458784 | tf_op jit(solution)/shard_map/ppermute | solution.py:54
  146.4 2.2 %fusion.11 = f32[8,576]{1,0:T(8,128)S(1)} fusion(bf16[7168,576]{0,1:T(8,128)(2,1)S(1)} %bitcast.31, bf16[8,7168]{1,0:T(8,128)(2,1)S(1)} %get-tuple-element.66, f32[7168]{0:T(1024)S(1)} %copy-done.10, f32[8]{0:T(128)S(1)} %add_rsqrt_fusion.1), kind=kOutput, calls=%fused_computation.21 | convolution fusion | flops 66289664 | bytes 8419360 | tf_op jit(solution)/shard_map/dot_general | solution.py:271
  (99 shorter events, 42.7 us)
Async XLA Ops:
  0.6 28.8 %collective-permute-start.6 = (bf16[7168,256]{1,0:T(8,128)(2,1)}, bf16[7168,256]{1,0:T(8,128)(2,1)}, u32[]{:S(2)}, u32[]{:S(2)}) collective-permute-start(bf16[7168,256]{1,0:T(8,128)(2,1)} %refs_4_.5), channel_id=1, source_target_pairs={{0,64},{1,65},{2,66},{3,67},{4,68},{5,69},{6,70},{7,71},{8,72},{9,... | collective-permute-start | bytes 11010056 | tf_op jit(solution)/shard_map/ppermute | solution.py:58
  0.7 28.7 %collective-permute-start.7 = (bf16[7168,256]{1,0:T(8,128)(2,1)}, bf16[7168,256]{1,0:T(8,128)(2,1)}, u32[]{:S(2)}, u32[]{:S(2)}) collective-permute-start(bf16[7168,256]{1,0:T(8,128)(2,1)} %refs_6_.1), channel_id=1, source_target_pairs={{0,64},{1,65},{2,66},{3,67},{4,68},{5,69},{6,70},{7,71},{8,72},{9,... | collective-permute-start | bytes 11010056 | tf_op jit(solution)/shard_map/ppermute | solution.py:58
  4.5 6.6 %collective-permute-start.1 = (bf16[1,8,7296]{2,1,0:T(8,128)(2,1)}, bf16[1,8,7296]{2,1,0:T(8,128)(2,1)S(1)}, u32[]{:S(2)}, u32[]{:S(2)}) collective-permute-start(bf16[1,8,7296]{2,1,0:T(8,128)(2,1)} %bitcast.27), channel_id=1, source_target_pairs={{0,32},{1,33},{2,34},{3,35},{4,36},{5,37},{6,38},{7,39},{8,40},{9,... | collective-permute-start | bytes 350216 | tf_op jit(solution)/shard_map/ppermute | solution.py:54
  13.3 9.8 %collective-permute-start.3 = (bf16[4,8,7296]{2,1,0:T(8,128)(2,1)S(1)}, bf16[4,8,7296]{2,1,0:T(8,128)(2,1)S(1)}, u32[]{:S(2)}, u32[]{:S(2)}) collective-permute-start(bf16[4,8,7296]{2,1,0:T(8,128)(2,1)S(1)} %join.2.refs_0_), channel_id=1, source_target_pairs={{0,4},{1,5},{2,6},{3,7},{4,8},{5,9},{6,10},{7,11},{8,12},{9,13},{1... | collective-permute-start | bytes 1400840 | tf_op jit(solution)/shard_map/ppermute | solution.py:54
  15.0 14.4 %collective-permute-start.4 = (bf16[4,8,7296]{2,1,0:T(8,128)(2,1)S(1)}, bf16[4,8,7296]{2,1,0:T(8,128)(2,1)S(1)}, u32[]{:S(2)}, u32[]{:S(2)}) collective-permute-start(bf16[4,8,7296]{2,1,0:T(8,128)(2,1)S(1)} %join.2.refs_0_), channel_id=1, source_target_pairs={{0,8},{1,9},{2,10},{3,11},{4,12},{5,13},{6,14},{7,15},{8,0},{9,1},... | collective-permute-start | bytes 1400840 | tf_op jit(solution)/shard_map/ppermute | solution.py:54
  17.9 11.5 %collective-permute-start.5 = (bf16[4,8,7296]{2,1,0:T(8,128)(2,1)S(1)}, bf16[4,8,7296]{2,1,0:T(8,128)(2,1)S(1)}, u32[]{:S(2)}, u32[]{:S(2)}) collective-permute-start(bf16[4,8,7296]{2,1,0:T(8,128)(2,1)S(1)} %join.2.refs_0_), channel_id=1, source_target_pairs={{0,12},{1,13},{2,14},{3,15},{4,0},{5,1},{6,2},{7,3},{8,4},{9,5},{1... | collective-permute-start | bytes 1400840 | tf_op jit(solution)/shard_map/ppermute | solution.py:54
  31.0 25.9 %collective-permute-start.14 = (bf16[256,7168]{1,0:T(8,128)(2,1)}, bf16[256,7168]{1,0:T(8,128)(2,1)}, u32[]{:S(2)}, u32[]{:S(2)}) collective-permute-start(bf16[256,7168]{1,0:T(8,128)(2,1)} %mine_ref.7), channel_id=1, source_target_pairs={{0,64},{1,65},{2,66},{3,67},{4,68},{5,69},{6,70},{7,71},{8,72},{9,... | collective-permute-start | bytes 11010056 | tf_op jit(solution)/shard_map/ppermute | solution.py:58
  31.1 17.2 %collective-permute-start.8 = (bf16[8,8,7296]{2,1,0:T(8,128)(2,1)S(1)}, bf16[8,8,7296]{2,1,0:T(8,128)(2,1)S(1)}, u32[]{:S(2)}, u32[]{:S(2)}) collective-permute-start(bf16[8,8,7296]{2,1,0:T(8,128)(2,1)S(1)} %get-tuple-element.37), channel_id=1, source_target_pairs={{0,1},{1,2},{2,3},{3,0},{4,5},{5,6},{6,7},{7,4},{8,9},{9,10},{10,1... | collective-permute-start | bytes 2801672 | tf_op jit(solution)/shard_map/ppermute | solution.py:54
  33.1 15.2 %collective-permute-start.9 = (bf16[8,8,7296]{2,1,0:T(8,128)(2,1)}, bf16[8,8,7296]{2,1,0:T(8,128)(2,1)}, u32[]{:S(2)}, u32[]{:S(2)}) collective-permute-start(bf16[8,8,7296]{2,1,0:T(8,128)(2,1)} %get-tuple-element.38), channel_id=1, source_target_pairs={{0,3},{1,0},{2,1},{3,2},{4,7},{5,4},{6,5},{7,6},{8,11},{9,8},{10,9... | collective-permute-start | bytes 2801672 | tf_op jit(solution)/shard_map/ppermute | solution.py:54
  35.4 21.4 %collective-permute-start.12 = (bf16[8,8,7296]{2,1,0:T(8,128)(2,1)}, bf16[8,8,7296]{2,1,0:T(8,128)(2,1)S(1)}, u32[]{:S(2)}, u32[]{:S(2)}) collective-permute-start(bf16[8,8,7296]{2,1,0:T(8,128)(2,1)} %get-tuple-element.38), channel_id=1, source_target_pairs={{0,1},{1,2},{2,3},{3,0},{4,5},{5,6},{6,7},{7,4},{8,9},{9,10},{10,1... | collective-permute-start | bytes 2801672 | tf_op jit(solution)/shard_map/ppermute | solution.py:54
  35.4 21.5 %collective-permute-start.13 = (bf16[8,8,7296]{2,1,0:T(8,128)(2,1)S(1)}, bf16[8,8,7296]{2,1,0:T(8,128)(2,1)S(1)}, u32[]{:S(2)}, u32[]{:S(2)}) collective-permute-start(bf16[8,8,7296]{2,1,0:T(8,128)(2,1)S(1)} %get-tuple-element.37), channel_id=1, source_target_pairs={{0,3},{1,0},{2,1},{3,2},{4,7},{5,4},{6,5},{7,6},{8,11},{9,8},{10,9... | collective-permute-start | bytes 2801672 | tf_op jit(solution)/shard_map/ppermute | solution.py:54
  48.3 18.6 %collective-permute-start.11 = (bf16[8,8,7296]{2,1,0:T(8,128)(2,1)}, bf16[8,8,7296]{2,1,0:T(8,128)(2,1)S(1)}, u32[]{:S(2)}, u32[]{:S(2)}) collective-permute-start(bf16[8,8,7296]{2,1,0:T(8,128)(2,1)} %collective-permute-done.9), channel_id=1, source_target_pairs={{0,3},{1,0},{2,1},{3,2},{4,7},{5,4},{6,5},{7,6},{8,11},{9,8},{10,9... | collective-permute-start | bytes 2801672 | tf_op jit(solution)/shard_map/ppermute | solution.py:54
  50.4 19.9 %collective-permute-start.10 = (bf16[8,8,7296]{2,1,0:T(8,128)(2,1)S(1)}, bf16[8,8,7296]{2,1,0:T(8,128)(2,1)S(1)}, u32[]{:S(2)}, u32[]{:S(2)}) collective-permute-start(bf16[8,8,7296]{2,1,0:T(8,128)(2,1)S(1)} %collective-permute-done.8), channel_id=1, source_target_pairs={{0,1},{1,2},{2,3},{3,0},{4,5},{5,6},{6,7},{7,4},{8,9},{9,10},{10,1... | collective-permute-start | bytes 2801672 | tf_op jit(solution)/shard_map/ppermute | solution.py:54
  66.9 14.3 %collective-permute-start.15 = (bf16[64,7168]{1,0:T(8,128)(2,1)S(1)}, bf16[64,7168]{1,0:T(8,128)(2,1)S(1)}, u32[]{:S(2)}, u32[]{:S(2)}) collective-permute-start(bf16[64,7168]{1,0:T(8,128)(2,1)S(1)} %get-tuple-element.49), channel_id=1, source_target_pairs={{0,3},{1,0},{2,1},{3,2},{4,7},{5,4},{6,5},{7,6},{8,11},{9,8},{10,9... | collective-permute-start | bytes 2752520 | tf_op jit(solution)/shard_map/ppermute | solution.py:54
  70.3 14.6 %collective-permute-start.16 = (bf16[64,7168]{1,0:T(8,128)(2,1)S(1)}, bf16[64,7168]{1,0:T(8,128)(2,1)S(1)}, u32[]{:S(2)}, u32[]{:S(2)}) collective-permute-start(bf16[64,7168]{1,0:T(8,128)(2,1)S(1)} %get-tuple-element.53), channel_id=1, source_target_pairs={{0,1},{1,2},{2,3},{3,0},{4,5},{5,6},{6,7},{7,4},{8,9},{9,10},{10,1... | collective-permute-start | bytes 2752520 | tf_op jit(solution)/shard_map/ppermute | solution.py:54
  81.2 14.6 %collective-permute-start.19 = (bf16[64,7168]{1,0:T(8,128)(2,1)S(1)}, bf16[64,7168]{1,0:T(8,128)(2,1)S(1)}, u32[]{:S(2)}, u32[]{:S(2)}) collective-permute-start(bf16[64,7168]{1,0:T(8,128)(2,1)S(1)} %get-tuple-element.59), channel_id=1, source_target_pairs={{0,3},{1,0},{2,1},{3,2},{4,7},{5,4},{6,5},{7,6},{8,11},{9,8},{10,9... | collective-permute-start | bytes 2752520 | tf_op jit(solution)/shard_map/ppermute | solution.py:54
  84.9 14.6 %collective-permute-start.17 = (bf16[64,7168]{1,0:T(8,128)(2,1)S(1)}, bf16[64,7168]{1,0:T(8,128)(2,1)S(1)}, u32[]{:S(2)}, u32[]{:S(2)}) collective-permute-start(bf16[64,7168]{1,0:T(8,128)(2,1)S(1)} %get-tuple-element.54), channel_id=1, source_target_pairs={{0,1},{1,2},{2,3},{3,0},{4,5},{5,6},{6,7},{7,4},{8,9},{9,10},{10,1... | collective-permute-start | bytes 2752520 | tf_op jit(solution)/shard_map/ppermute | solution.py:54
  100.0 15.6 %collective-permute-start.18 = (bf16[64,7168]{1,0:T(8,128)(2,1)S(1)}, bf16[64,7168]{1,0:T(8,128)(2,1)S(1)}, u32[]{:S(2)}, u32[]{:S(2)}) collective-permute-start(bf16[64,7168]{1,0:T(8,128)(2,1)S(1)} %get-tuple-element.55), channel_id=1, source_target_pairs={{0,1},{1,2},{2,3},{3,0},{4,5},{5,6},{6,7},{7,4},{8,9},{9,10},{10,1... | collective-permute-start | bytes 2752520 | tf_op jit(solution)/shard_map/ppermute | solution.py:54
  100.1 19.8 %collective-permute-start.20 = (bf16[64,7168]{1,0:T(8,128)(2,1)S(1)}, bf16[64,7168]{1,0:T(8,128)(2,1)S(1)}, u32[]{:S(2)}, u32[]{:S(2)}) collective-permute-start(bf16[64,7168]{1,0:T(8,128)(2,1)S(1)} %get-tuple-element.60), channel_id=1, source_target_pairs={{0,3},{1,0},{2,1},{3,2},{4,7},{5,4},{6,5},{7,6},{8,11},{9,8},{10,9... | collective-permute-start | bytes 2752520 | tf_op jit(solution)/shard_map/ppermute | solution.py:54
  120.3 11.0 %collective-permute-start.23 = (bf16[32,7168]{1,0:T(8,128)(2,1)S(1)}, bf16[32,7168]{1,0:T(8,128)(2,1)S(1)}, u32[]{:S(2)}, u32[]{:S(2)}) collective-permute-start(bf16[32,7168]{1,0:T(8,128)(2,1)S(1)} %get-tuple-element.68), channel_id=1, source_target_pairs={{0,4},{1,5},{2,6},{3,7},{4,8},{5,9},{6,10},{7,11},{8,12},{9,13},{1... | collective-permute-start | bytes 1376264 | tf_op jit(solution)/shard_map/ppermute | solution.py:54
  122.0 15.9 %collective-permute-start.22 = (bf16[32,7168]{1,0:T(8,128)(2,1)S(1)}, bf16[32,7168]{1,0:T(8,128)(2,1)S(1)}, u32[]{:S(2)}, u32[]{:S(2)}) collective-permute-start(bf16[32,7168]{1,0:T(8,128)(2,1)S(1)} %get-tuple-element.67), channel_id=1, source_target_pairs={{0,8},{1,9},{2,10},{3,11},{4,12},{5,13},{6,14},{7,15},{8,0},{9,1},... | collective-permute-start | bytes 1376264 | tf_op jit(solution)/shard_map/ppermute | solution.py:54
  124.1 14.2 %collective-permute-start.21 = (bf16[32,7168]{1,0:T(8,128)(2,1)S(1)}, bf16[32,7168]{1,0:T(8,128)(2,1)S(1)}, u32[]{:S(2)}, u32[]{:S(2)}) collective-permute-start(bf16[32,7168]{1,0:T(8,128)(2,1)S(1)} %split.25), channel_id=1, source_target_pairs={{0,12},{1,13},{2,14},{3,15},{4,0},{5,1},{6,2},{7,3},{8,4},{9,5},{1... | collective-permute-start | bytes 1376264 | tf_op jit(solution)/shard_map/ppermute | solution.py:54
  138.7 6.5 %collective-permute-start.25 = (bf16[8,7168]{1,0:T(8,128)(2,1)S(1)}, bf16[8,7168]{1,0:T(8,128)(2,1)S(1)}, u32[]{:S(2)}, u32[]{:S(2)}) collective-permute-start(bf16[8,7168]{1,0:T(8,128)(2,1)S(1)} %get-tuple-element.71), channel_id=1, source_target_pairs={{0,32},{1,33},{2,34},{3,35},{4,36},{5,37},{6,38},{7,39},{8,40},{9,... | collective-permute-start | bytes 344072 | tf_op jit(solution)/shard_map/ppermute | solution.py:54
  138.8 7.4 %collective-permute-start.24 = (bf16[8,7168]{1,0:T(8,128)(2,1)S(1)}, bf16[8,7168]{1,0:T(8,128)(2,1)S(1)}, u32[]{:S(2)}, u32[]{:S(2)}) collective-permute-start(bf16[8,7168]{1,0:T(8,128)(2,1)S(1)} %get-tuple-element.69), channel_id=1, source_target_pairs={{0,48},{1,49},{2,50},{3,51},{4,52},{5,53},{6,54},{7,55},{8,56},{9,... | collective-permute-start | bytes 344072 | tf_op jit(solution)/shard_map/ppermute | solution.py:54
  (18 other events, 297.2 us)

commit v6 on v5

--- a/solution.py
+++ b/solution.py
@@ -12,7 +12,7 @@
 AXES = ("sec", "dev")
 SIDE = 4
 STRIDE = {"x": 16, "y": 4, "z": 1}
-ORDER = (("x", "y", "z"), ("y", "z", "x"))
+ORDER = (("y", "x", "z"), ("z", "y", "x"))
 LANES = 128
 
 

time: 153 us -> 148 us (0.967)
  waiting for transfers between devices: 63.3 us -> 57 us
    ppermute x24, waiting for transfers between devices: 63.3 us -> 57 us  [shift(): return lax.ppermute(values, AXES, pairs)]
  transfers between devices with their start and end apart: 27 -> 27, of which waited for: 19 -> 19; matrix products, arithmetic and copies ran while one was open for 1% -> 1% of each run, Pallas kernels for 22% -> 23%
where the time goes in v6:
time: 148 us; the launch traced here: 147 us
  waiting for transfers between devices  57 us (39%)
  starting transfers between devices  40.3 us (27%)
  Pallas kernels  35.5 us (24%)
  local copies, waits for them, and re-layouts  5.17 us (3%)
  matrix products  5.13 us (3%)
  other arithmetic  3.23 us (2%)
    ppermute x24, waiting for transfers between devices, shift(): return lax.ppermute(values, AXES, pairs)  57 us
    ppermute x24, starting transfers between devices, shift(): return lax.ppermute(values, AXES, pairs)  39.6 us
    pallas_call x3, Pallas kernels, expert_acts(): pl.pallas_call(act_body, out_shape=jax.ShapeDtypeStruct((tokens, 2 * wide...  18.5 us
    pallas_call x4, Pallas kernels, expert_outs(): pl.pallas_call(down_body, out_shape=[jax.ShapeDtypeStruct((tokens // coun...  13.2 us
    unnamed x30, local copies, waits for them, and re-layouts  5.04 us
  transfers between devices with their start and end apart: 27, of which 19 were waited for; matrix products, arithmetic and copies ran while one was open for 1% of the time, Pallas kernels for 23%

profile of v6, /device:TPU:2, one launch (start us, length us, event | category | flops | bytes accessed | tf_op | source)
XLA Modules:
  0.0 147.3 jit_solution(8631495548287215267)
XLA Ops:
  4.6 2.9 %collective-permute-start.1 = (bf16[1,8,7296]{2,1,0:T(8,128)(2,1)}, bf16[1,8,7296]{2,1,0:T(8,128)(2,1)S(1)}, u32[]{:S(2)}, u32[]{:S(2)}) collective-permute-start(bf16[1,8,7296]{2,1,0:T(8,128)(2,1)} %bitcast.27), channel_id=1, source_target_pairs={{0,8},{1,9},{2,10},{3,11},{4,12},{5,13},{6,14},{7,15},{8,0},{9,1},... | collective-permute-start | bytes 350216 | tf_op jit(solution)/shard_map/ppermute | solution.py:54
  9.2 2.5 %collective-permute-done.1.refs_2_ = bf16[1,8,7296]{2,1,0:T(8,128)(2,1)S(1)} collective-permute-done((bf16[1,8,7296]{2,1,0:T(8,128)(2,1)}, bf16[1,8,7296]{2,1,0:T(8,128)(2,1)S(1)}, u32[]{:S(2)}, u32[]{:S(2)}) %collective-permute-start.1) | collective-permute-done | bytes 116768 | tf_op jit(solution)/shard_map/ppermute | solution.py:54
  18.8 3.8 %collective-permute-done.3.refs_1_ = bf16[4,8,7296]{2,1,0:T(8,128)(2,1)S(1)} collective-permute-done((bf16[4,8,7296]{2,1,0:T(8,128)(2,1)S(1)}, bf16[4,8,7296]{2,1,0:T(8,128)(2,1)S(1)}, u32[]{:S(2)}, u32[]{:S(2)}) %collective-permute-start.3) | collective-permute-done | bytes 466976 | tf_op jit(solution)/shard_map/ppermute | solution.py:54
  22.6 3.1 %collective-permute-done.4.refs_2_ = bf16[4,8,7296]{2,1,0:T(8,128)(2,1)S(1)} collective-permute-done((bf16[4,8,7296]{2,1,0:T(8,128)(2,1)S(1)}, bf16[4,8,7296]{2,1,0:T(8,128)(2,1)S(1)}, u32[]{:S(2)}, u32[]{:S(2)}) %collective-permute-start.4) | collective-permute-done | bytes 466976 | tf_op jit(solution)/shard_map/ppermute | solution.py:54
  25.7 4.5 %collective-permute-done.5.refs_3_ = bf16[4,8,7296]{2,1,0:T(8,128)(2,1)S(1)} collective-permute-done((bf16[4,8,7296]{2,1,0:T(8,128)(2,1)S(1)}, bf16[4,8,7296]{2,1,0:T(8,128)(2,1)S(1)}, u32[]{:S(2)}, u32[]{:S(2)}) %collective-permute-start.5) | collective-permute-done | bytes 466976 | tf_op jit(solution)/shard_map/ppermute | solution.py:54
  36.1 3.2 %collective-permute-start.13 = (bf16[8,8,7296]{2,1,0:T(8,128)(2,1)S(1)}, bf16[8,8,7296]{2,1,0:T(8,128)(2,1)S(1)}, u32[]{:S(2)}, u32[]{:S(2)}) collective-permute-start(bf16[8,8,7296]{2,1,0:T(8,128)(2,1)S(1)} %get-tuple-element.37), channel_id=1, source_target_pairs={{0,3},{1,0},{2,1},{3,2},{4,7},{5,4},{6,5},{7,6},{8,11},{9,8},{10,9... | collective-permute-start | bytes 2801672 | tf_op jit(solution)/shard_map/ppermute | solution.py:54
  43.4 5.6 %expert_acts.3.acts_ref = bf16[128,512]{1,0:T(8,128)(2,1)S(1)} custom-call(s32[2]{0:T(128)S(1)} %pad_add_fusion.info_ref, bf16[64,7296]{1,0:T(8,128)(2,1)S(1)} %bitcast.21, bf16[64,7296]{1,0:T(8,128)(2,1)} %bitcast.5.refs_1_, bf16[7168,256]{1,0:T(8,128)(2,1)S(1)} %copy-done.2, bf16[7168,256]{1,0:T(8,128)(2,1)} %collective-permute-done.6.refs_3_.refs_5_, ...), custom_call_target="tpu_custom_call" | custom-call | flops 1879048192 | bytes 1048576 | tf_op jit(solution)/shard_map/expert_acts/pallas_call | solution.py:151
  51.2 5.7 %expert_acts.4.acts_ref = bf16[128,512]{1,0:T(8,128)(2,1)S(1)} custom-call(s32[2]{0:T(128)S(1)} %pad_add_fusion.info_ref, bf16[64,7296]{1,0:T(8,128)(2,1)S(1)} %bitcast.20, bf16[64,7296]{1,0:T(8,128)(2,1)} %bitcast.9.refs_1_, bf16[7168,256]{1,0:T(8,128)(2,1)S(1)} %copy-done.2, bf16[7168,256]{1,0:T(8,128)(2,1)} %collective-permute-done.6.refs_3_.refs_5_, ...), custom_call_target="tpu_custom_call" | custom-call | flops 1879048192 | bytes 1048576 | tf_op jit(solution)/shard_map/expert_acts/pallas_call | solution.py:151
  57.6 3.6 %expert_outs.6 = (bf16[64,7168]{1,0:T(8,128)(2,1)S(1)}, bf16[64,7168]{1,0:T(8,128)(2,1)S(1)}) custom-call(bf16[128,512]{1,0:T(8,128)(2,1)S(1)} %expert_acts.4.acts_ref, bf16[256,7168]{1,0:T(8,128)(2,1)S(1)} %copy-done.1, bf16[256,7168]{1,0:T(8,128)(2,1)} %collective-permute-done.14.other_ref), custom_call_target="tpu_custom_call" | custom-call | flops 939524096 | bytes 1048576 | tf_op jit(solution)/shard_map/expert_outs/pallas_call | solution.py:182
  61.2 6.4 %collective-permute-done.11 = bf16[8,8,7296]{2,1,0:T(8,128)(2,1)S(1)} collective-permute-done((bf16[8,8,7296]{2,1,0:T(8,128)(2,1)}, bf16[8,8,7296]{2,1,0:T(8,128)(2,1)S(1)}, u32[]{:S(2)}, u32[]{:S(2)}) %collective-permute-start.11) | collective-permute-done | bytes 933920 | tf_op jit(solution)/shard_map/ppermute | solution.py:54
  67.6 3.4 %collective-permute-start.15 = (bf16[64,7168]{1,0:T(8,128)(2,1)S(1)}, bf16[64,7168]{1,0:T(8,128)(2,1)S(1)}, u32[]{:S(2)}, u32[]{:S(2)}) collective-permute-start(bf16[64,7168]{1,0:T(8,128)(2,1)S(1)} %get-tuple-element.49), channel_id=1, source_target_pairs={{0,3},{1,0},{2,1},{3,2},{4,7},{5,4},{6,5},{7,6},{8,11},{9,8},{10,9... | collective-permute-start | bytes 2752520 | tf_op jit(solution)/shard_map/ppermute | solution.py:54
  71.1 7.2 %expert_acts.5 = bf16[256,512]{1,0:T(8,128)(2,1)S(1)} custom-call(s32[2]{0:T(128)S(1)} %pad_add_fusion.info_ref, bf16[64,7296]{1,0:T(8,128)(2,1)S(1)} %bitcast.25, bf16[64,7296]{1,0:T(8,128)(2,1)S(1)} %bitcast.24, bf16[64,7296]{1,0:T(8,128)(2,1)S(1)} %bitcast.22, bf16[64,7296]{1,0:T(8,128)(2,1)S(1)} %bitcast.23, bf16[7168,256]{1,0:T(8,128)(2,1)S(1)} %copy-done.3, ...), custom_call_target="tpu_custom_call" | custom-call | flops 3758096384 | bytes 1048576 | tf_op jit(solution)/shard_map/expert_acts/pallas_call | solution.py:151
  78.3 3.2 %expert_outs.4 = (bf16[64,7168]{1,0:T(8,128)(2,1)S(1)}, bf16[64,7168]{1,0:T(8,128)(2,1)S(1)}) custom-call(bf16[128,512]{1,0:T(8,128)(2,1)S(1)} %slice.31.acts_ref, bf16[256,7168]{1,0:T(8,128)(2,1)S(1)} %copy-done.1, bf16[256,7168]{1,0:T(8,128)(2,1)} %collective-permute-done.14.other_ref), custom_call_target="tpu_custom_call" | custom-call | flops 939524096 | bytes 1048576 | tf_op jit(solution)/shard_map/expert_outs/pallas_call | solution.py:182
  82.0 3.7 %collective-permute-start.19 = (bf16[64,7168]{1,0:T(8,128)(2,1)S(1)}, bf16[64,7168]{1,0:T(8,128)(2,1)S(1)}, u32[]{:S(2)}, u32[]{:S(2)}) collective-permute-start(bf16[64,7168]{1,0:T(8,128)(2,1)S(1)} %get-tuple-element.59), channel_id=1, source_target_pairs={{0,3},{1,0},{2,1},{3,2},{4,7},{5,4},{6,5},{7,6},{8,11},{9,8},{10,9... | collective-permute-start | bytes 2752520 | tf_op jit(solution)/shard_map/ppermute | solution.py:54
  85.7 3.2 %expert_outs.7 = (bf16[64,7168]{1,0:T(8,128)(2,1)S(1)}, bf16[64,7168]{1,0:T(8,128)(2,1)S(1)}) custom-call(bf16[128,512]{1,0:T(8,128)(2,1)S(1)} %slice.25.acts_ref, bf16[256,7168]{1,0:T(8,128)(2,1)S(1)} %copy-done.1, bf16[256,7168]{1,0:T(8,128)(2,1)} %collective-permute-done.14.other_ref), custom_call_target="tpu_custom_call" | custom-call | flops 939524096 | bytes 1048576 | tf_op jit(solution)/shard_map/expert_outs/pallas_call | solution.py:182
  88.9 3.2 %expert_outs.5 = (bf16[64,7168]{1,0:T(8,128)(2,1)S(1)}, bf16[64,7168]{1,0:T(8,128)(2,1)S(1)}) custom-call(bf16[128,512]{1,0:T(8,128)(2,1)S(1)} %expert_acts.3.acts_ref, bf16[256,7168]{1,0:T(8,128)(2,1)S(1)} %copy-done.1, bf16[256,7168]{1,0:T(8,128)(2,1)} %collective-permute-done.14.other_ref), custom_call_target="tpu_custom_call" | custom-call | flops 939524096 | bytes 1048576 | tf_op jit(solution)/shard_map/expert_outs/pallas_call | solution.py:182
  92.1 4.5 %collective-permute-done.19 = bf16[64,7168]{1,0:T(8,128)(2,1)S(1)} collective-permute-done((bf16[64,7168]{1,0:T(8,128)(2,1)S(1)}, bf16[64,7168]{1,0:T(8,128)(2,1)S(1)}, u32[]{:S(2)}, u32[]{:S(2)}) %collective-permute-start.19) | collective-permute-done | bytes 917536 | tf_op jit(solution)/shard_map/ppermute | solution.py:54
  96.6 3.7 %collective-permute-done.17 = bf16[64,7168]{1,0:T(8,128)(2,1)S(1)} collective-permute-done((bf16[64,7168]{1,0:T(8,128)(2,1)S(1)}, bf16[64,7168]{1,0:T(8,128)(2,1)S(1)}, u32[]{:S(2)}, u32[]{:S(2)}) %collective-permute-start.17) | collective-permute-done | bytes 917536 | tf_op jit(solution)/shard_map/ppermute | solution.py:54
  100.8 3.2 %collective-permute-start.20 = (bf16[64,7168]{1,0:T(8,128)(2,1)S(1)}, bf16[64,7168]{1,0:T(8,128)(2,1)S(1)}, u32[]{:S(2)}, u32[]{:S(2)}) collective-permute-start(bf16[64,7168]{1,0:T(8,128)(2,1)S(1)} %get-tuple-element.60), channel_id=1, source_target_pairs={{0,3},{1,0},{2,1},{3,2},{4,7},{5,4},{6,5},{7,6},{8,11},{9,8},{10,9... | collective-permute-start | bytes 2752520 | tf_op jit(solution)/shard_map/ppermute | solution.py:54
  104.0 11.4 %collective-permute-done.18 = bf16[64,7168]{1,0:T(8,128)(2,1)S(1)} collective-permute-done((bf16[64,7168]{1,0:T(8,128)(2,1)S(1)}, bf16[64,7168]{1,0:T(8,128)(2,1)S(1)}, u32[]{:S(2)}, u32[]{:S(2)}) %collective-permute-start.18) | collective-permute-done | bytes 917536 | tf_op jit(solution)/shard_map/ppermute | solution.py:54
  120.6 4.2 %collective-permute-done.23 = bf16[32,7168]{1,0:T(8,128)(2,1)S(1)} collective-permute-done((bf16[32,7168]{1,0:T(8,128)(2,1)S(1)}, bf16[32,7168]{1,0:T(8,128)(2,1)S(1)}, u32[]{:S(2)}, u32[]{:S(2)}) %collective-permute-start.23) | collective-permute-done | bytes 458784 | tf_op jit(solution)/shard_map/ppermute | solution.py:54
  124.8 2.6 %collective-permute-done.22 = bf16[32,7168]{1,0:T(8,128)(2,1)S(1)} collective-permute-done((bf16[32,7168]{1,0:T(8,128)(2,1)S(1)}, bf16[32,7168]{1,0:T(8,128)(2,1)S(1)}, u32[]{:S(2)}, u32[]{:S(2)}) %collective-permute-start.22) | collective-permute-done | bytes 458784 | tf_op jit(solution)/shard_map/ppermute | solution.py:54
  127.4 4.6 %collective-permute-done.21 = bf16[32,7168]{1,0:T(8,128)(2,1)S(1)} collective-permute-done((bf16[32,7168]{1,0:T(8,128)(2,1)S(1)}, bf16[32,7168]{1,0:T(8,128)(2,1)S(1)}, u32[]{:S(2)}, u32[]{:S(2)}) %collective-permute-start.21) | collective-permute-done | bytes 458784 | tf_op jit(solution)/shard_map/ppermute | solution.py:54
  133.2 3.2 %collective-permute-start.25 = (bf16[8,7168]{1,0:T(8,128)(2,1)S(1)}, bf16[8,7168]{1,0:T(8,128)(2,1)S(1)}, u32[]{:S(2)}, u32[]{:S(2)}) collective-permute-start(bf16[8,7168]{1,0:T(8,128)(2,1)S(1)} %get-tuple-element.71), channel_id=1, source_target_pairs={{0,8},{1,9},{2,10},{3,11},{4,12},{5,13},{6,14},{7,15},{8,0},{9,1},... | collective-permute-start | bytes 344072 | tf_op jit(solution)/shard_map/ppermute | solution.py:54
  (99 shorter events, 43.8 us)
Async XLA Ops:
  0.6 29.6 %collective-permute-start.6 = (bf16[7168,256]{1,0:T(8,128)(2,1)}, bf16[7168,256]{1,0:T(8,128)(2,1)}, u32[]{:S(2)}, u32[]{:S(2)}) collective-permute-start(bf16[7168,256]{1,0:T(8,128)(2,1)} %refs_4_.5), channel_id=1, source_target_pairs={{0,64},{1,65},{2,66},{3,67},{4,68},{5,69},{6,70},{7,71},{8,72},{9,... | collective-permute-start | bytes 11010056 | tf_op jit(solution)/shard_map/ppermute | solution.py:58
  0.7 29.5 %collective-permute-start.7 = (bf16[7168,256]{1,0:T(8,128)(2,1)}, bf16[7168,256]{1,0:T(8,128)(2,1)}, u32[]{:S(2)}, u32[]{:S(2)}) collective-permute-start(bf16[7168,256]{1,0:T(8,128)(2,1)} %refs_6_.1), channel_id=1, source_target_pairs={{0,64},{1,65},{2,66},{3,67},{4,68},{5,69},{6,70},{7,71},{8,72},{9,... | collective-permute-start | bytes 11010056 | tf_op jit(solution)/shard_map/ppermute | solution.py:58
  3.0 6.2 %collective-permute-start = (bf16[1,8,7296]{2,1,0:T(8,128)(2,1)}, bf16[1,8,7296]{2,1,0:T(8,128)(2,1)S(1)}, u32[]{:S(2)}, u32[]{:S(2)}) collective-permute-start(bf16[1,8,7296]{2,1,0:T(8,128)(2,1)} %bitcast.26), channel_id=1, source_target_pairs={{0,4},{1,5},{2,6},{3,7},{4,8},{5,9},{6,10},{7,11},{8,12},{9,13},{1... | collective-permute-start | bytes 350216 | tf_op jit(solution)/shard_map/ppermute | solution.py:54
  4.6 7.2 %collective-permute-start.1 = (bf16[1,8,7296]{2,1,0:T(8,128)(2,1)}, bf16[1,8,7296]{2,1,0:T(8,128)(2,1)S(1)}, u32[]{:S(2)}, u32[]{:S(2)}) collective-permute-start(bf16[1,8,7296]{2,1,0:T(8,128)(2,1)} %bitcast.27), channel_id=1, source_target_pairs={{0,8},{1,9},{2,10},{3,11},{4,12},{5,13},{6,14},{7,15},{8,0},{9,1},... | collective-permute-start | bytes 350216 | tf_op jit(solution)/shard_map/ppermute | solution.py:54
  14.0 8.6 %collective-permute-start.3 = (bf16[4,8,7296]{2,1,0:T(8,128)(2,1)S(1)}, bf16[4,8,7296]{2,1,0:T(8,128)(2,1)S(1)}, u32[]{:S(2)}, u32[]{:S(2)}) collective-permute-start(bf16[4,8,7296]{2,1,0:T(8,128)(2,1)S(1)} %join.2.refs_0_), channel_id=1, source_target_pairs={{0,16},{1,17},{2,18},{3,19},{4,20},{5,21},{6,22},{7,23},{8,24},{9,... | collective-permute-start | bytes 1400840 | tf_op jit(solution)/shard_map/ppermute | solution.py:54
  15.6 10.2 %collective-permute-start.4 = (bf16[4,8,7296]{2,1,0:T(8,128)(2,1)S(1)}, bf16[4,8,7296]{2,1,0:T(8,128)(2,1)S(1)}, u32[]{:S(2)}, u32[]{:S(2)}) collective-permute-start(bf16[4,8,7296]{2,1,0:T(8,128)(2,1)S(1)} %join.2.refs_0_), channel_id=1, source_target_pairs={{0,32},{1,33},{2,34},{3,35},{4,36},{5,37},{6,38},{7,39},{8,40},{9,... | collective-permute-start | bytes 1400840 | tf_op jit(solution)/shard_map/ppermute | solution.py:54
  16.7 13.6 %collective-permute-start.5 = (bf16[4,8,7296]{2,1,0:T(8,128)(2,1)S(1)}, bf16[4,8,7296]{2,1,0:T(8,128)(2,1)S(1)}, u32[]{:S(2)}, u32[]{:S(2)}) collective-permute-start(bf16[4,8,7296]{2,1,0:T(8,128)(2,1)S(1)} %join.2.refs_0_), channel_id=1, source_target_pairs={{0,48},{1,49},{2,50},{3,51},{4,52},{5,53},{6,54},{7,55},{8,56},{9,... | collective-permute-start | bytes 1400840 | tf_op jit(solution)/shard_map/ppermute | solution.py:54
  31.8 25.9 %collective-permute-start.14 = (bf16[256,7168]{1,0:T(8,128)(2,1)}, bf16[256,7168]{1,0:T(8,128)(2,1)}, u32[]{:S(2)}, u32[]{:S(2)}) collective-permute-start(bf16[256,7168]{1,0:T(8,128)(2,1)} %mine_ref.7), channel_id=1, source_target_pairs={{0,64},{1,65},{2,66},{3,67},{4,68},{5,69},{6,70},{7,71},{8,72},{9,... | collective-permute-start | bytes 11010056 | tf_op jit(solution)/shard_map/ppermute | solution.py:58
  31.9 17.2 %collective-permute-start.8 = (bf16[8,8,7296]{2,1,0:T(8,128)(2,1)S(1)}, bf16[8,8,7296]{2,1,0:T(8,128)(2,1)S(1)}, u32[]{:S(2)}, u32[]{:S(2)}) collective-permute-start(bf16[8,8,7296]{2,1,0:T(8,128)(2,1)S(1)} %get-tuple-element.37), channel_id=1, source_target_pairs={{0,1},{1,2},{2,3},{3,0},{4,5},{5,6},{6,7},{7,4},{8,9},{9,10},{10,1... | collective-permute-start | bytes 2801672 | tf_op jit(solution)/shard_map/ppermute | solution.py:54
  33.9 15.2 %collective-permute-start.9 = (bf16[8,8,7296]{2,1,0:T(8,128)(2,1)}, bf16[8,8,7296]{2,1,0:T(8,128)(2,1)}, u32[]{:S(2)}, u32[]{:S(2)}) collective-permute-start(bf16[8,8,7296]{2,1,0:T(8,128)(2,1)} %get-tuple-element.38), channel_id=1, source_target_pairs={{0,3},{1,0},{2,1},{3,2},{4,7},{5,4},{6,5},{7,6},{8,11},{9,8},{10,9... | collective-permute-start | bytes 2801672 | tf_op jit(solution)/shard_map/ppermute | solution.py:54
  36.1 21.4 %collective-permute-start.12 = (bf16[8,8,7296]{2,1,0:T(8,128)(2,1)}, bf16[8,8,7296]{2,1,0:T(8,128)(2,1)S(1)}, u32[]{:S(2)}, u32[]{:S(2)}) collective-permute-start(bf16[8,8,7296]{2,1,0:T(8,128)(2,1)} %get-tuple-element.38), channel_id=1, source_target_pairs={{0,1},{1,2},{2,3},{3,0},{4,5},{5,6},{6,7},{7,4},{8,9},{9,10},{10,1... | collective-permute-start | bytes 2801672 | tf_op jit(solution)/shard_map/ppermute | solution.py:54
  36.1 21.5 %collective-permute-start.13 = (bf16[8,8,7296]{2,1,0:T(8,128)(2,1)S(1)}, bf16[8,8,7296]{2,1,0:T(8,128)(2,1)S(1)}, u32[]{:S(2)}, u32[]{:S(2)}) collective-permute-start(bf16[8,8,7296]{2,1,0:T(8,128)(2,1)S(1)} %get-tuple-element.37), channel_id=1, source_target_pairs={{0,3},{1,0},{2,1},{3,2},{4,7},{5,4},{6,5},{7,6},{8,11},{9,8},{10,9... | collective-permute-start | bytes 2801672 | tf_op jit(solution)/shard_map/ppermute | solution.py:54
  49.1 18.6 %collective-permute-start.11 = (bf16[8,8,7296]{2,1,0:T(8,128)(2,1)}, bf16[8,8,7296]{2,1,0:T(8,128)(2,1)S(1)}, u32[]{:S(2)}, u32[]{:S(2)}) collective-permute-start(bf16[8,8,7296]{2,1,0:T(8,128)(2,1)} %collective-permute-done.9), channel_id=1, source_target_pairs={{0,3},{1,0},{2,1},{3,2},{4,7},{5,4},{6,5},{7,6},{8,11},{9,8},{10,9... | collective-permute-start | bytes 2801672 | tf_op jit(solution)/shard_map/ppermute | solution.py:54
  51.2 19.9 %collective-permute-start.10 = (bf16[8,8,7296]{2,1,0:T(8,128)(2,1)S(1)}, bf16[8,8,7296]{2,1,0:T(8,128)(2,1)S(1)}, u32[]{:S(2)}, u32[]{:S(2)}) collective-permute-start(bf16[8,8,7296]{2,1,0:T(8,128)(2,1)S(1)} %collective-permute-done.8), channel_id=1, source_target_pairs={{0,1},{1,2},{2,3},{3,0},{4,5},{5,6},{6,7},{7,4},{8,9},{9,10},{10,1... | collective-permute-start | bytes 2801672 | tf_op jit(solution)/shard_map/ppermute | solution.py:54
  67.6 14.3 %collective-permute-start.15 = (bf16[64,7168]{1,0:T(8,128)(2,1)S(1)}, bf16[64,7168]{1,0:T(8,128)(2,1)S(1)}, u32[]{:S(2)}, u32[]{:S(2)}) collective-permute-start(bf16[64,7168]{1,0:T(8,128)(2,1)S(1)} %get-tuple-element.49), channel_id=1, source_target_pairs={{0,3},{1,0},{2,1},{3,2},{4,7},{5,4},{6,5},{7,6},{8,11},{9,8},{10,9... | collective-permute-start | bytes 2752520 | tf_op jit(solution)/shard_map/ppermute | solution.py:54
  71.1 14.6 %collective-permute-start.16 = (bf16[64,7168]{1,0:T(8,128)(2,1)S(1)}, bf16[64,7168]{1,0:T(8,128)(2,1)S(1)}, u32[]{:S(2)}, u32[]{:S(2)}) collective-permute-start(bf16[64,7168]{1,0:T(8,128)(2,1)S(1)} %get-tuple-element.53), channel_id=1, source_target_pairs={{0,1},{1,2},{2,3},{3,0},{4,5},{5,6},{6,7},{7,4},{8,9},{9,10},{10,1... | collective-permute-start | bytes 2752520 | tf_op jit(solution)/shard_map/ppermute | solution.py:54
  82.0 14.6 %collective-permute-start.19 = (bf16[64,7168]{1,0:T(8,128)(2,1)S(1)}, bf16[64,7168]{1,0:T(8,128)(2,1)S(1)}, u32[]{:S(2)}, u32[]{:S(2)}) collective-permute-start(bf16[64,7168]{1,0:T(8,128)(2,1)S(1)} %get-tuple-element.59), channel_id=1, source_target_pairs={{0,3},{1,0},{2,1},{3,2},{4,7},{5,4},{6,5},{7,6},{8,11},{9,8},{10,9... | collective-permute-start | bytes 2752520 | tf_op jit(solution)/shard_map/ppermute | solution.py:54
  85.7 14.6 %collective-permute-start.17 = (bf16[64,7168]{1,0:T(8,128)(2,1)S(1)}, bf16[64,7168]{1,0:T(8,128)(2,1)S(1)}, u32[]{:S(2)}, u32[]{:S(2)}) collective-permute-start(bf16[64,7168]{1,0:T(8,128)(2,1)S(1)} %get-tuple-element.54), channel_id=1, source_target_pairs={{0,1},{1,2},{2,3},{3,0},{4,5},{5,6},{6,7},{7,4},{8,9},{9,10},{10,1... | collective-permute-start | bytes 2752520 | tf_op jit(solution)/shard_map/ppermute | solution.py:54
  100.7 14.7 %collective-permute-start.18 = (bf16[64,7168]{1,0:T(8,128)(2,1)S(1)}, bf16[64,7168]{1,0:T(8,128)(2,1)S(1)}, u32[]{:S(2)}, u32[]{:S(2)}) collective-permute-start(bf16[64,7168]{1,0:T(8,128)(2,1)S(1)} %get-tuple-element.55), channel_id=1, source_target_pairs={{0,1},{1,2},{2,3},{3,0},{4,5},{5,6},{6,7},{7,4},{8,9},{9,10},{10,1... | collective-permute-start | bytes 2752520 | tf_op jit(solution)/shard_map/ppermute | solution.py:54
  100.8 14.9 %collective-permute-start.20 = (bf16[64,7168]{1,0:T(8,128)(2,1)S(1)}, bf16[64,7168]{1,0:T(8,128)(2,1)S(1)}, u32[]{:S(2)}, u32[]{:S(2)}) collective-permute-start(bf16[64,7168]{1,0:T(8,128)(2,1)S(1)} %get-tuple-element.60), channel_id=1, source_target_pairs={{0,3},{1,0},{2,1},{3,2},{4,7},{5,4},{6,5},{7,6},{8,11},{9,8},{10,9... | collective-permute-start | bytes 2752520 | tf_op jit(solution)/shard_map/ppermute | solution.py:54
  116.2 8.5 %collective-permute-start.23 = (bf16[32,7168]{1,0:T(8,128)(2,1)S(1)}, bf16[32,7168]{1,0:T(8,128)(2,1)S(1)}, u32[]{:S(2)}, u32[]{:S(2)}) collective-permute-start(bf16[32,7168]{1,0:T(8,128)(2,1)S(1)} %get-tuple-element.68), channel_id=1, source_target_pairs={{0,16},{1,17},{2,18},{3,19},{4,20},{5,21},{6,22},{7,23},{8,24},{9,... | collective-permute-start | bytes 1376264 | tf_op jit(solution)/shard_map/ppermute | solution.py:54
  117.3 10.1 %collective-permute-start.22 = (bf16[32,7168]{1,0:T(8,128)(2,1)S(1)}, bf16[32,7168]{1,0:T(8,128)(2,1)S(1)}, u32[]{:S(2)}, u32[]{:S(2)}) collective-permute-start(bf16[32,7168]{1,0:T(8,128)(2,1)S(1)} %get-tuple-element.67), channel_id=1, source_target_pairs={{0,32},{1,33},{2,34},{3,35},{4,36},{5,37},{6,38},{7,39},{8,40},{9,... | collective-permute-start | bytes 1376264 | tf_op jit(solution)/shard_map/ppermute | solution.py:54
  118.5 13.5 %collective-permute-start.21 = (bf16[32,7168]{1,0:T(8,128)(2,1)S(1)}, bf16[32,7168]{1,0:T(8,128)(2,1)S(1)}, u32[]{:S(2)}, u32[]{:S(2)}) collective-permute-start(bf16[32,7168]{1,0:T(8,128)(2,1)S(1)} %split.25), channel_id=1, source_target_pairs={{0,48},{1,49},{2,50},{3,51},{4,52},{5,53},{6,54},{7,55},{8,56},{9,... | collective-permute-start | bytes 1376264 | tf_op jit(solution)/shard_map/ppermute | solution.py:54
  133.2 7.1 %collective-permute-start.25 = (bf16[8,7168]{1,0:T(8,128)(2,1)S(1)}, bf16[8,7168]{1,0:T(8,128)(2,1)S(1)}, u32[]{:S(2)}, u32[]{:S(2)}) collective-permute-start(bf16[8,7168]{1,0:T(8,128)(2,1)S(1)} %get-tuple-element.71), channel_id=1, source_target_pairs={{0,8},{1,9},{2,10},{3,11},{4,12},{5,13},{6,14},{7,15},{8,0},{9,1},... | collective-permute-start | bytes 344072 | tf_op jit(solution)/shard_map/ppermute | solution.py:54
  (18 other events, 282.1 us)

commit v7 on v6

--- a/solution.py
+++ b/solution.py
@@ -12,7 +12,7 @@
 AXES = ("sec", "dev")
 SIDE = 4
 STRIDE = {"x": 16, "y": 4, "z": 1}
-ORDER = (("y", "x", "z"), ("z", "y", "x"))
+ORDER = (("z", "x", "y"), ("y", "z", "x"))
 LANES = 128
 
 

time: 148 us -> 147 us (level)
  no operation moved by 1% of the time
where the time goes in v7:
time: 147 us
  waiting for transfers between devices  57.6 us (39%)
  starting transfers between devices  39.2 us (27%)
  Pallas kernels  35.7 us (24%)
  local copies, waits for them, and re-layouts  5.17 us (4%)
  matrix products  5.13 us (3%)
  other arithmetic  3.23 us (2%)
    ppermute x24, waiting for transfers between devices, shift(): return lax.ppermute(values, AXES, pairs)  57.6 us
    ppermute x24, starting transfers between devices, shift(): return lax.ppermute(values, AXES, pairs)  38.6 us
    pallas_call x3, Pallas kernels, expert_acts(): pl.pallas_call(act_body, out_shape=jax.ShapeDtypeStruct((tokens, 2 * wide...  18.5 us
    pallas_call x4, Pallas kernels, expert_outs(): pl.pallas_call(down_body, out_shape=[jax.ShapeDtypeStruct((tokens // coun...  13.4 us
    unnamed x30, local copies, waits for them, and re-layouts  5.04 us
  transfers between devices with their start and end apart: 27, of which 19 were waited for; matrix products, arithmetic and copies ran while one was open for 1% of the time, Pallas kernels for 23%

profile of v7, /device:TPU:2, one launch (start us, length us, event | category | flops | bytes accessed | tf_op | source)
XLA Modules:
  0.0 147.1 jit_solution(10377406266196375677)
XLA Ops:
  4.9 3.6 %collective-permute-start.1 = (bf16[1,8,7296]{2,1,0:T(8,128)(2,1)}, bf16[1,8,7296]{2,1,0:T(8,128)(2,1)S(1)}, u32[]{:S(2)}, u32[]{:S(2)}) collective-permute-start(bf16[1,8,7296]{2,1,0:T(8,128)(2,1)} %bitcast.27), channel_id=1, source_target_pairs={{0,2},{1,3},{2,0},{3,1},{4,6},{5,7},{6,4},{7,5},{8,10},{9,11},{10,... | collective-permute-start | bytes 350216 | tf_op jit(solution)/shard_map/ppermute | solution.py:54
  10.0 2.7 %collective-permute-done.1.refs_2_ = bf16[1,8,7296]{2,1,0:T(8,128)(2,1)S(1)} collective-permute-done((bf16[1,8,7296]{2,1,0:T(8,128)(2,1)}, bf16[1,8,7296]{2,1,0:T(8,128)(2,1)S(1)}, u32[]{:S(2)}, u32[]{:S(2)}) %collective-permute-start.1) | collective-permute-done | bytes 116768 | tf_op jit(solution)/shard_map/ppermute | solution.py:54
  19.8 3.8 %collective-permute-done.3.refs_1_ = bf16[4,8,7296]{2,1,0:T(8,128)(2,1)S(1)} collective-permute-done((bf16[4,8,7296]{2,1,0:T(8,128)(2,1)S(1)}, bf16[4,8,7296]{2,1,0:T(8,128)(2,1)S(1)}, u32[]{:S(2)}, u32[]{:S(2)}) %collective-permute-start.3) | collective-permute-done | bytes 466976 | tf_op jit(solution)/shard_map/ppermute | solution.py:54
  23.7 3.1 %collective-permute-done.4.refs_2_ = bf16[4,8,7296]{2,1,0:T(8,128)(2,1)S(1)} collective-permute-done((bf16[4,8,7296]{2,1,0:T(8,128)(2,1)S(1)}, bf16[4,8,7296]{2,1,0:T(8,128)(2,1)S(1)}, u32[]{:S(2)}, u32[]{:S(2)}) %collective-permute-start.4) | collective-permute-done | bytes 466976 | tf_op jit(solution)/shard_map/ppermute | solution.py:54
  26.8 4.5 %collective-permute-done.5.refs_3_ = bf16[4,8,7296]{2,1,0:T(8,128)(2,1)S(1)} collective-permute-done((bf16[4,8,7296]{2,1,0:T(8,128)(2,1)S(1)}, bf16[4,8,7296]{2,1,0:T(8,128)(2,1)S(1)}, u32[]{:S(2)}, u32[]{:S(2)}) %collective-permute-start.5) | collective-permute-done | bytes 466976 | tf_op jit(solution)/shard_map/ppermute | solution.py:54
  36.6 2.9 %collective-permute-start.13 = (bf16[8,8,7296]{2,1,0:T(8,128)(2,1)S(1)}, bf16[8,8,7296]{2,1,0:T(8,128)(2,1)S(1)}, u32[]{:S(2)}, u32[]{:S(2)}) collective-permute-start(bf16[8,8,7296]{2,1,0:T(8,128)(2,1)S(1)} %get-tuple-element.37), channel_id=1, source_target_pairs={{0,12},{1,13},{2,14},{3,15},{4,0},{5,1},{6,2},{7,3},{8,4},{9,5},{1... | collective-permute-start | bytes 2801672 | tf_op jit(solution)/shard_map/ppermute | solution.py:54
  43.6 5.6 %expert_acts.3.acts_ref = bf16[128,512]{1,0:T(8,128)(2,1)S(1)} custom-call(s32[2]{0:T(128)S(1)} %pad_add_fusion.info_ref, bf16[64,7296]{1,0:T(8,128)(2,1)S(1)} %bitcast.21, bf16[64,7296]{1,0:T(8,128)(2,1)} %bitcast.5.refs_1_, bf16[7168,256]{1,0:T(8,128)(2,1)S(1)} %copy-done.2, bf16[7168,256]{1,0:T(8,128)(2,1)} %collective-permute-done.6.refs_3_.refs_5_, ...), custom_call_target="tpu_custom_call" | custom-call | flops 1879048192 | bytes 1048576 | tf_op jit(solution)/shard_map/expert_acts/pallas_call | solution.py:151
  51.3 5.7 %expert_acts.4.acts_ref = bf16[128,512]{1,0:T(8,128)(2,1)S(1)} custom-call(s32[2]{0:T(128)S(1)} %pad_add_fusion.info_ref, bf16[64,7296]{1,0:T(8,128)(2,1)S(1)} %bitcast.20, bf16[64,7296]{1,0:T(8,128)(2,1)} %bitcast.9.refs_1_, bf16[7168,256]{1,0:T(8,128)(2,1)S(1)} %copy-done.2, bf16[7168,256]{1,0:T(8,128)(2,1)} %collective-permute-done.6.refs_3_.refs_5_, ...), custom_call_target="tpu_custom_call" | custom-call | flops 1879048192 | bytes 1048576 | tf_op jit(solution)/shard_map/expert_acts/pallas_call | solution.py:151
  58.3 3.8 %expert_outs.6 = (bf16[64,7168]{1,0:T(8,128)(2,1)S(1)}, bf16[64,7168]{1,0:T(8,128)(2,1)S(1)}) custom-call(bf16[128,512]{1,0:T(8,128)(2,1)S(1)} %expert_acts.4.acts_ref, bf16[256,7168]{1,0:T(8,128)(2,1)S(1)} %copy-done.1, bf16[256,7168]{1,0:T(8,128)(2,1)} %collective-permute-done.14.other_ref), custom_call_target="tpu_custom_call" | custom-call | flops 939524096 | bytes 1048576 | tf_op jit(solution)/shard_map/expert_outs/pallas_call | solution.py:182
  62.1 6.2 %collective-permute-done.11 = bf16[8,8,7296]{2,1,0:T(8,128)(2,1)S(1)} collective-permute-done((bf16[8,8,7296]{2,1,0:T(8,128)(2,1)}, bf16[8,8,7296]{2,1,0:T(8,128)(2,1)S(1)}, u32[]{:S(2)}, u32[]{:S(2)}) %collective-permute-start.11) | collective-permute-done | bytes 933920 | tf_op jit(solution)/shard_map/ppermute | solution.py:54
  68.3 2.9 %collective-permute-start.15 = (bf16[64,7168]{1,0:T(8,128)(2,1)S(1)}, bf16[64,7168]{1,0:T(8,128)(2,1)S(1)}, u32[]{:S(2)}, u32[]{:S(2)}) collective-permute-start(bf16[64,7168]{1,0:T(8,128)(2,1)S(1)} %get-tuple-element.49), channel_id=1, source_target_pairs={{0,12},{1,13},{2,14},{3,15},{4,0},{5,1},{6,2},{7,3},{8,4},{9,5},{1... | collective-permute-start | bytes 2752520 | tf_op jit(solution)/shard_map/ppermute | solution.py:54
  71.2 7.2 %expert_acts.5 = bf16[256,512]{1,0:T(8,128)(2,1)S(1)} custom-call(s32[2]{0:T(128)S(1)} %pad_add_fusion.info_ref, bf16[64,7296]{1,0:T(8,128)(2,1)S(1)} %bitcast.25, bf16[64,7296]{1,0:T(8,128)(2,1)S(1)} %bitcast.24, bf16[64,7296]{1,0:T(8,128)(2,1)S(1)} %bitcast.22, bf16[64,7296]{1,0:T(8,128)(2,1)S(1)} %bitcast.23, bf16[7168,256]{1,0:T(8,128)(2,1)S(1)} %copy-done.3, ...), custom_call_target="tpu_custom_call" | custom-call | flops 3758096384 | bytes 1048576 | tf_op jit(solution)/shard_map/expert_acts/pallas_call | solution.py:151
  78.4 3.2 %expert_outs.4 = (bf16[64,7168]{1,0:T(8,128)(2,1)S(1)}, bf16[64,7168]{1,0:T(8,128)(2,1)S(1)}) custom-call(bf16[128,512]{1,0:T(8,128)(2,1)S(1)} %slice.31.acts_ref, bf16[256,7168]{1,0:T(8,128)(2,1)S(1)} %copy-done.1, bf16[256,7168]{1,0:T(8,128)(2,1)} %collective-permute-done.14.other_ref), custom_call_target="tpu_custom_call" | custom-call | flops 939524096 | bytes 1048576 | tf_op jit(solution)/shard_map/expert_outs/pallas_call | solution.py:182
  82.1 3.7 %collective-permute-start.19 = (bf16[64,7168]{1,0:T(8,128)(2,1)S(1)}, bf16[64,7168]{1,0:T(8,128)(2,1)S(1)}, u32[]{:S(2)}, u32[]{:S(2)}) collective-permute-start(bf16[64,7168]{1,0:T(8,128)(2,1)S(1)} %get-tuple-element.59), channel_id=1, source_target_pairs={{0,12},{1,13},{2,14},{3,15},{4,0},{5,1},{6,2},{7,3},{8,4},{9,5},{1... | collective-permute-start | bytes 2752520 | tf_op jit(solution)/shard_map/ppermute | solution.py:54
  85.8 3.2 %expert_outs.7 = (bf16[64,7168]{1,0:T(8,128)(2,1)S(1)}, bf16[64,7168]{1,0:T(8,128)(2,1)S(1)}) custom-call(bf16[128,512]{1,0:T(8,128)(2,1)S(1)} %slice.25.acts_ref, bf16[256,7168]{1,0:T(8,128)(2,1)S(1)} %copy-done.1, bf16[256,7168]{1,0:T(8,128)(2,1)} %collective-permute-done.14.other_ref), custom_call_target="tpu_custom_call" | custom-call | flops 939524096 | bytes 1048576 | tf_op jit(solution)/shard_map/expert_outs/pallas_call | solution.py:182
  89.0 3.2 %expert_outs.5 = (bf16[64,7168]{1,0:T(8,128)(2,1)S(1)}, bf16[64,7168]{1,0:T(8,128)(2,1)S(1)}) custom-call(bf16[128,512]{1,0:T(8,128)(2,1)S(1)} %expert_acts.3.acts_ref, bf16[256,7168]{1,0:T(8,128)(2,1)S(1)} %copy-done.1, bf16[256,7168]{1,0:T(8,128)(2,1)} %collective-permute-done.14.other_ref), custom_call_target="tpu_custom_call" | custom-call | flops 939524096 | bytes 1048576 | tf_op jit(solution)/shard_map/expert_outs/pallas_call | solution.py:182
  92.2 4.5 %collective-permute-done.19 = bf16[64,7168]{1,0:T(8,128)(2,1)S(1)} collective-permute-done((bf16[64,7168]{1,0:T(8,128)(2,1)S(1)}, bf16[64,7168]{1,0:T(8,128)(2,1)S(1)}, u32[]{:S(2)}, u32[]{:S(2)}) %collective-permute-start.19) | collective-permute-done | bytes 917536 | tf_op jit(solution)/shard_map/ppermute | solution.py:54
  96.7 3.7 %collective-permute-done.17 = bf16[64,7168]{1,0:T(8,128)(2,1)S(1)} collective-permute-done((bf16[64,7168]{1,0:T(8,128)(2,1)S(1)}, bf16[64,7168]{1,0:T(8,128)(2,1)S(1)}, u32[]{:S(2)}, u32[]{:S(2)}) %collective-permute-start.17) | collective-permute-done | bytes 917536 | tf_op jit(solution)/shard_map/ppermute | solution.py:54
  101.0 3.2 %collective-permute-start.20 = (bf16[64,7168]{1,0:T(8,128)(2,1)S(1)}, bf16[64,7168]{1,0:T(8,128)(2,1)S(1)}, u32[]{:S(2)}, u32[]{:S(2)}) collective-permute-start(bf16[64,7168]{1,0:T(8,128)(2,1)S(1)} %get-tuple-element.60), channel_id=1, source_target_pairs={{0,12},{1,13},{2,14},{3,15},{4,0},{5,1},{6,2},{7,3},{8,4},{9,5},{1... | collective-permute-start | bytes 2752520 | tf_op jit(solution)/shard_map/ppermute | solution.py:54
  104.2 11.4 %collective-permute-done.18 = bf16[64,7168]{1,0:T(8,128)(2,1)S(1)} collective-permute-done((bf16[64,7168]{1,0:T(8,128)(2,1)S(1)}, bf16[64,7168]{1,0:T(8,128)(2,1)S(1)}, u32[]{:S(2)}, u32[]{:S(2)}) %collective-permute-start.18) | collective-permute-done | bytes 917536 | tf_op jit(solution)/shard_map/ppermute | solution.py:54
  120.7 4.2 %collective-permute-done.23 = bf16[32,7168]{1,0:T(8,128)(2,1)S(1)} collective-permute-done((bf16[32,7168]{1,0:T(8,128)(2,1)S(1)}, bf16[32,7168]{1,0:T(8,128)(2,1)S(1)}, u32[]{:S(2)}, u32[]{:S(2)}) %collective-permute-start.23) | collective-permute-done | bytes 458784 | tf_op jit(solution)/shard_map/ppermute | solution.py:54
  124.9 2.6 %collective-permute-done.22 = bf16[32,7168]{1,0:T(8,128)(2,1)S(1)} collective-permute-done((bf16[32,7168]{1,0:T(8,128)(2,1)S(1)}, bf16[32,7168]{1,0:T(8,128)(2,1)S(1)}, u32[]{:S(2)}, u32[]{:S(2)}) %collective-permute-start.22) | collective-permute-done | bytes 458784 | tf_op jit(solution)/shard_map/ppermute | solution.py:54
  127.5 4.6 %collective-permute-done.21 = bf16[32,7168]{1,0:T(8,128)(2,1)S(1)} collective-permute-done((bf16[32,7168]{1,0:T(8,128)(2,1)S(1)}, bf16[32,7168]{1,0:T(8,128)(2,1)S(1)}, u32[]{:S(2)}, u32[]{:S(2)}) %collective-permute-start.21) | collective-permute-done | bytes 458784 | tf_op jit(solution)/shard_map/ppermute | solution.py:54
  133.1 3.0 %collective-permute-start.25 = (bf16[8,7168]{1,0:T(8,128)(2,1)S(1)}, bf16[8,7168]{1,0:T(8,128)(2,1)S(1)}, u32[]{:S(2)}, u32[]{:S(2)}) collective-permute-start(bf16[8,7168]{1,0:T(8,128)(2,1)S(1)} %get-tuple-element.71), channel_id=1, source_target_pairs={{0,2},{1,3},{2,0},{3,1},{4,6},{5,7},{6,4},{7,5},{8,10},{9,11},{10,... | collective-permute-start | bytes 344072 | tf_op jit(solution)/shard_map/ppermute | solution.py:54
  (99 shorter events, 43.7 us)
Async XLA Ops:
  0.6 30.6 %collective-permute-start.6 = (bf16[7168,256]{1,0:T(8,128)(2,1)}, bf16[7168,256]{1,0:T(8,128)(2,1)}, u32[]{:S(2)}, u32[]{:S(2)}) collective-permute-start(bf16[7168,256]{1,0:T(8,128)(2,1)} %refs_4_.5), channel_id=1, source_target_pairs={{0,64},{1,65},{2,66},{3,67},{4,68},{5,69},{6,70},{7,71},{8,72},{9,... | collective-permute-start | bytes 11010056 | tf_op jit(solution)/shard_map/ppermute | solution.py:58
  0.7 30.5 %collective-permute-start.7 = (bf16[7168,256]{1,0:T(8,128)(2,1)}, bf16[7168,256]{1,0:T(8,128)(2,1)}, u32[]{:S(2)}, u32[]{:S(2)}) collective-permute-start(bf16[7168,256]{1,0:T(8,128)(2,1)} %refs_6_.1), channel_id=1, source_target_pairs={{0,64},{1,65},{2,66},{3,67},{4,68},{5,69},{6,70},{7,71},{8,72},{9,... | collective-permute-start | bytes 11010056 | tf_op jit(solution)/shard_map/ppermute | solution.py:58
  3.0 7.0 %collective-permute-start = (bf16[1,8,7296]{2,1,0:T(8,128)(2,1)}, bf16[1,8,7296]{2,1,0:T(8,128)(2,1)S(1)}, u32[]{:S(2)}, u32[]{:S(2)}) collective-permute-start(bf16[1,8,7296]{2,1,0:T(8,128)(2,1)} %bitcast.26), channel_id=1, source_target_pairs={{0,1},{1,2},{2,3},{3,0},{4,5},{5,6},{6,7},{7,4},{8,9},{9,10},{10,1... | collective-permute-start | bytes 350216 | tf_op jit(solution)/shard_map/ppermute | solution.py:54
  4.9 7.8 %collective-permute-start.1 = (bf16[1,8,7296]{2,1,0:T(8,128)(2,1)}, bf16[1,8,7296]{2,1,0:T(8,128)(2,1)S(1)}, u32[]{:S(2)}, u32[]{:S(2)}) collective-permute-start(bf16[1,8,7296]{2,1,0:T(8,128)(2,1)} %bitcast.27), channel_id=1, source_target_pairs={{0,2},{1,3},{2,0},{3,1},{4,6},{5,7},{6,4},{7,5},{8,10},{9,11},{10,... | collective-permute-start | bytes 350216 | tf_op jit(solution)/shard_map/ppermute | solution.py:54
  15.0 8.6 %collective-permute-start.3 = (bf16[4,8,7296]{2,1,0:T(8,128)(2,1)S(1)}, bf16[4,8,7296]{2,1,0:T(8,128)(2,1)S(1)}, u32[]{:S(2)}, u32[]{:S(2)}) collective-permute-start(bf16[4,8,7296]{2,1,0:T(8,128)(2,1)S(1)} %join.2.refs_0_), channel_id=1, source_target_pairs={{0,16},{1,17},{2,18},{3,19},{4,20},{5,21},{6,22},{7,23},{8,24},{9,... | collective-permute-start | bytes 1400840 | tf_op jit(solution)/shard_map/ppermute | solution.py:54
  16.6 10.2 %collective-permute-start.4 = (bf16[4,8,7296]{2,1,0:T(8,128)(2,1)S(1)}, bf16[4,8,7296]{2,1,0:T(8,128)(2,1)S(1)}, u32[]{:S(2)}, u32[]{:S(2)}) collective-permute-start(bf16[4,8,7296]{2,1,0:T(8,128)(2,1)S(1)} %join.2.refs_0_), channel_id=1, source_target_pairs={{0,32},{1,33},{2,34},{3,35},{4,36},{5,37},{6,38},{7,39},{8,40},{9,... | collective-permute-start | bytes 1400840 | tf_op jit(solution)/shard_map/ppermute | solution.py:54
  17.7 13.6 %collective-permute-start.5 = (bf16[4,8,7296]{2,1,0:T(8,128)(2,1)S(1)}, bf16[4,8,7296]{2,1,0:T(8,128)(2,1)S(1)}, u32[]{:S(2)}, u32[]{:S(2)}) collective-permute-start(bf16[4,8,7296]{2,1,0:T(8,128)(2,1)S(1)} %join.2.refs_0_), channel_id=1, source_target_pairs={{0,48},{1,49},{2,50},{3,51},{4,52},{5,53},{6,54},{7,55},{8,56},{9,... | collective-permute-start | bytes 1400840 | tf_op jit(solution)/shard_map/ppermute | solution.py:54
  32.8 25.5 %collective-permute-start.14 = (bf16[256,7168]{1,0:T(8,128)(2,1)}, bf16[256,7168]{1,0:T(8,128)(2,1)}, u32[]{:S(2)}, u32[]{:S(2)}) collective-permute-start(bf16[256,7168]{1,0:T(8,128)(2,1)} %mine_ref.7), channel_id=1, source_target_pairs={{0,64},{1,65},{2,66},{3,67},{4,68},{5,69},{6,70},{7,71},{8,72},{9,... | collective-permute-start | bytes 11010056 | tf_op jit(solution)/shard_map/ppermute | solution.py:58
  32.9 16.3 %collective-permute-start.8 = (bf16[8,8,7296]{2,1,0:T(8,128)(2,1)S(1)}, bf16[8,8,7296]{2,1,0:T(8,128)(2,1)S(1)}, u32[]{:S(2)}, u32[]{:S(2)}) collective-permute-start(bf16[8,8,7296]{2,1,0:T(8,128)(2,1)S(1)} %get-tuple-element.37), channel_id=1, source_target_pairs={{0,4},{1,5},{2,6},{3,7},{4,8},{5,9},{6,10},{7,11},{8,12},{9,13},{1... | collective-permute-start | bytes 2801672 | tf_op jit(solution)/shard_map/ppermute | solution.py:54
  34.5 14.7 %collective-permute-start.9 = (bf16[8,8,7296]{2,1,0:T(8,128)(2,1)}, bf16[8,8,7296]{2,1,0:T(8,128)(2,1)}, u32[]{:S(2)}, u32[]{:S(2)}) collective-permute-start(bf16[8,8,7296]{2,1,0:T(8,128)(2,1)} %get-tuple-element.38), channel_id=1, source_target_pairs={{0,12},{1,13},{2,14},{3,15},{4,0},{5,1},{6,2},{7,3},{8,4},{9,5},{1... | collective-permute-start | bytes 2801672 | tf_op jit(solution)/shard_map/ppermute | solution.py:54
  36.3 21.5 %collective-permute-start.12 = (bf16[8,8,7296]{2,1,0:T(8,128)(2,1)}, bf16[8,8,7296]{2,1,0:T(8,128)(2,1)S(1)}, u32[]{:S(2)}, u32[]{:S(2)}) collective-permute-start(bf16[8,8,7296]{2,1,0:T(8,128)(2,1)} %get-tuple-element.38), channel_id=1, source_target_pairs={{0,4},{1,5},{2,6},{3,7},{4,8},{5,9},{6,10},{7,11},{8,12},{9,13},{1... | collective-permute-start | bytes 2801672 | tf_op jit(solution)/shard_map/ppermute | solution.py:54
  36.6 21.7 %collective-permute-start.13 = (bf16[8,8,7296]{2,1,0:T(8,128)(2,1)S(1)}, bf16[8,8,7296]{2,1,0:T(8,128)(2,1)S(1)}, u32[]{:S(2)}, u32[]{:S(2)}) collective-permute-start(bf16[8,8,7296]{2,1,0:T(8,128)(2,1)S(1)} %get-tuple-element.37), channel_id=1, source_target_pairs={{0,12},{1,13},{2,14},{3,15},{4,0},{5,1},{6,2},{7,3},{8,4},{9,5},{1... | collective-permute-start | bytes 2801672 | tf_op jit(solution)/shard_map/ppermute | solution.py:54
  49.2 19.1 %collective-permute-start.11 = (bf16[8,8,7296]{2,1,0:T(8,128)(2,1)}, bf16[8,8,7296]{2,1,0:T(8,128)(2,1)S(1)}, u32[]{:S(2)}, u32[]{:S(2)}) collective-permute-start(bf16[8,8,7296]{2,1,0:T(8,128)(2,1)} %collective-permute-done.9), channel_id=1, source_target_pairs={{0,12},{1,13},{2,14},{3,15},{4,0},{5,1},{6,2},{7,3},{8,4},{9,5},{1... | collective-permute-start | bytes 2801672 | tf_op jit(solution)/shard_map/ppermute | solution.py:54
  51.3 19.9 %collective-permute-start.10 = (bf16[8,8,7296]{2,1,0:T(8,128)(2,1)S(1)}, bf16[8,8,7296]{2,1,0:T(8,128)(2,1)S(1)}, u32[]{:S(2)}, u32[]{:S(2)}) collective-permute-start(bf16[8,8,7296]{2,1,0:T(8,128)(2,1)S(1)} %collective-permute-done.8), channel_id=1, source_target_pairs={{0,4},{1,5},{2,6},{3,7},{4,8},{5,9},{6,10},{7,11},{8,12},{9,13},{1... | collective-permute-start | bytes 2801672 | tf_op jit(solution)/shard_map/ppermute | solution.py:54
  68.3 13.8 %collective-permute-start.15 = (bf16[64,7168]{1,0:T(8,128)(2,1)S(1)}, bf16[64,7168]{1,0:T(8,128)(2,1)S(1)}, u32[]{:S(2)}, u32[]{:S(2)}) collective-permute-start(bf16[64,7168]{1,0:T(8,128)(2,1)S(1)} %get-tuple-element.49), channel_id=1, source_target_pairs={{0,12},{1,13},{2,14},{3,15},{4,0},{5,1},{6,2},{7,3},{8,4},{9,5},{1... | collective-permute-start | bytes 2752520 | tf_op jit(solution)/shard_map/ppermute | solution.py:54
  71.2 14.6 %collective-permute-start.16 = (bf16[64,7168]{1,0:T(8,128)(2,1)S(1)}, bf16[64,7168]{1,0:T(8,128)(2,1)S(1)}, u32[]{:S(2)}, u32[]{:S(2)}) collective-permute-start(bf16[64,7168]{1,0:T(8,128)(2,1)S(1)} %get-tuple-element.53), channel_id=1, source_target_pairs={{0,4},{1,5},{2,6},{3,7},{4,8},{5,9},{6,10},{7,11},{8,12},{9,13},{1... | collective-permute-start | bytes 2752520 | tf_op jit(solution)/shard_map/ppermute | solution.py:54
  82.1 14.6 %collective-permute-start.19 = (bf16[64,7168]{1,0:T(8,128)(2,1)S(1)}, bf16[64,7168]{1,0:T(8,128)(2,1)S(1)}, u32[]{:S(2)}, u32[]{:S(2)}) collective-permute-start(bf16[64,7168]{1,0:T(8,128)(2,1)S(1)} %get-tuple-element.59), channel_id=1, source_target_pairs={{0,12},{1,13},{2,14},{3,15},{4,0},{5,1},{6,2},{7,3},{8,4},{9,5},{1... | collective-permute-start | bytes 2752520 | tf_op jit(solution)/shard_map/ppermute | solution.py:54
  85.8 14.6 %collective-permute-start.17 = (bf16[64,7168]{1,0:T(8,128)(2,1)S(1)}, bf16[64,7168]{1,0:T(8,128)(2,1)S(1)}, u32[]{:S(2)}, u32[]{:S(2)}) collective-permute-start(bf16[64,7168]{1,0:T(8,128)(2,1)S(1)} %get-tuple-element.54), channel_id=1, source_target_pairs={{0,4},{1,5},{2,6},{3,7},{4,8},{5,9},{6,10},{7,11},{8,12},{9,13},{1... | collective-permute-start | bytes 2752520 | tf_op jit(solution)/shard_map/ppermute | solution.py:54
  100.9 14.7 %collective-permute-start.18 = (bf16[64,7168]{1,0:T(8,128)(2,1)S(1)}, bf16[64,7168]{1,0:T(8,128)(2,1)S(1)}, u32[]{:S(2)}, u32[]{:S(2)}) collective-permute-start(bf16[64,7168]{1,0:T(8,128)(2,1)S(1)} %get-tuple-element.55), channel_id=1, source_target_pairs={{0,4},{1,5},{2,6},{3,7},{4,8},{5,9},{6,10},{7,11},{8,12},{9,13},{1... | collective-permute-start | bytes 2752520 | tf_op jit(solution)/shard_map/ppermute | solution.py:54
  101.0 14.9 %collective-permute-start.20 = (bf16[64,7168]{1,0:T(8,128)(2,1)S(1)}, bf16[64,7168]{1,0:T(8,128)(2,1)S(1)}, u32[]{:S(2)}, u32[]{:S(2)}) collective-permute-start(bf16[64,7168]{1,0:T(8,128)(2,1)S(1)} %get-tuple-element.60), channel_id=1, source_target_pairs={{0,12},{1,13},{2,14},{3,15},{4,0},{5,1},{6,2},{7,3},{8,4},{9,5},{1... | collective-permute-start | bytes 2752520 | tf_op jit(solution)/shard_map/ppermute | solution.py:54
  116.4 8.5 %collective-permute-start.23 = (bf16[32,7168]{1,0:T(8,128)(2,1)S(1)}, bf16[32,7168]{1,0:T(8,128)(2,1)S(1)}, u32[]{:S(2)}, u32[]{:S(2)}) collective-permute-start(bf16[32,7168]{1,0:T(8,128)(2,1)S(1)} %get-tuple-element.68), channel_id=1, source_target_pairs={{0,16},{1,17},{2,18},{3,19},{4,20},{5,21},{6,22},{7,23},{8,24},{9,... | collective-permute-start | bytes 1376264 | tf_op jit(solution)/shard_map/ppermute | solution.py:54
  117.4 10.1 %collective-permute-start.22 = (bf16[32,7168]{1,0:T(8,128)(2,1)S(1)}, bf16[32,7168]{1,0:T(8,128)(2,1)S(1)}, u32[]{:S(2)}, u32[]{:S(2)}) collective-permute-start(bf16[32,7168]{1,0:T(8,128)(2,1)S(1)} %get-tuple-element.67), channel_id=1, source_target_pairs={{0,32},{1,33},{2,34},{3,35},{4,36},{5,37},{6,38},{7,39},{8,40},{9,... | collective-permute-start | bytes 1376264 | tf_op jit(solution)/shard_map/ppermute | solution.py:54
  118.7 13.5 %collective-permute-start.21 = (bf16[32,7168]{1,0:T(8,128)(2,1)S(1)}, bf16[32,7168]{1,0:T(8,128)(2,1)S(1)}, u32[]{:S(2)}, u32[]{:S(2)}) collective-permute-start(bf16[32,7168]{1,0:T(8,128)(2,1)S(1)} %split.25), channel_id=1, source_target_pairs={{0,48},{1,49},{2,50},{3,51},{4,52},{5,53},{6,54},{7,55},{8,56},{9,... | collective-permute-start | bytes 1376264 | tf_op jit(solution)/shard_map/ppermute | solution.py:54
  133.1 7.0 %collective-permute-start.25 = (bf16[8,7168]{1,0:T(8,128)(2,1)S(1)}, bf16[8,7168]{1,0:T(8,128)(2,1)S(1)}, u32[]{:S(2)}, u32[]{:S(2)}) collective-permute-start(bf16[8,7168]{1,0:T(8,128)(2,1)S(1)} %get-tuple-element.71), channel_id=1, source_target_pairs={{0,2},{1,3},{2,0},{3,1},{4,6},{5,7},{6,4},{7,5},{8,10},{9,11},{10,... | collective-permute-start | bytes 344072 | tf_op jit(solution)/shard_map/ppermute | solution.py:54
  (18 other events, 281.4 us)

commit v8 on v7

--- a/solution.py
+++ b/solution.py
@@ -222,8 +222,10 @@
     rows = front(resid, ffn_gain, expert_ids, gate_weights)
     up_other = swap_cores(w_up)
     rows = rows[None]
-    (rows,) = join([rows] + [shift(rows, 0, back) for back in range(1, SIDE)], 1)
-    got = [rows] + [shift(rows, 1, back) for back in range(1, SIDE)]
+    one, three, two = (shift(rows, 0, back) for back in (1, 3, 2))
+    (rows,) = join([rows, one, two, three], 1)
+    one, three, two = (shift(rows, 1, back) for back in (1, 3, 2))
+    got = [rows, one, two, three]
     low, high = join(lax.optimization_barrier((got, gate_other, up_other))[0], 2)
     down_other = swap_cores(after(w_down, low))
     low_back, high_ahead = shift(low, 2, 1), shift(high, 2, -1)
@@ -263,7 +265,7 @@
     low, high = lax.optimization_barrier((low, high))
     parts = [*jnp.split(low, 2, axis=0), *jnp.split(high, 2, axis=0)]
     for phase in (1, 0):
-        moe = plus(parts[0], *(shift(parts[back], phase, -back) for back in range(1, SIDE)))
+        moe = plus(parts[0], *(shift(parts[back], phase, -back) for back in (1, 3, 2)))
         if phase > 0:
             parts = jnp.split(moe.astype(jnp.bfloat16), SIDE, axis=0)
     hidden = (resid.astype(jnp.float32) + moe).astype(jnp.bfloat16)

time: 147 us -> 146 us (level)
  no operation moved by 1% of the time
where the time goes in v8:
time: 146 us
  waiting for transfers between devices  56.2 us (38%)
  starting transfers between devices  39.2 us (27%)
  Pallas kernels  35.7 us (24%)
  local copies, waits for them, and re-layouts  5.17 us (4%)
  matrix products  5.13 us (4%)
  other arithmetic  3.23 us (2%)
    ppermute x24, waiting for transfers between devices, shift(): return lax.ppermute(values, AXES, pairs)  56.2 us
    ppermute x24, starting transfers between devices, shift(): return lax.ppermute(values, AXES, pairs)  38.6 us
    pallas_call x3, Pallas kernels, expert_acts(): pl.pallas_call(act_body, out_shape=jax.ShapeDtypeStruct((tokens, 2 * wide...  18.5 us
    pallas_call x4, Pallas kernels, expert_outs(): pl.pallas_call(down_body, out_shape=[jax.ShapeDtypeStruct((tokens // coun...  13.4 us
    unnamed x30, local copies, waits for them, and re-layouts  5.04 us
  transfers between devices with their start and end apart: 27, of which 19 were waited for; matrix products, arithmetic and copies ran while one was open for 1% of the time, Pallas kernels for 23%

profile of v8, /device:TPU:2, one launch (start us, length us, event | category | flops | bytes accessed | tf_op | source)
XLA Modules:
  0.0 145.7 jit_solution(12891089160836874016)
XLA Ops:
  4.9 3.6 %collective-permute-start.1 = (bf16[1,8,7296]{2,1,0:T(8,128)(2,1)}, bf16[1,8,7296]{2,1,0:T(8,128)(2,1)S(1)}, u32[]{:S(2)}, u32[]{:S(2)}) collective-permute-start(bf16[1,8,7296]{2,1,0:T(8,128)(2,1)} %bitcast.27), channel_id=1, source_target_pairs={{0,2},{1,3},{2,0},{3,1},{4,6},{5,7},{6,4},{7,5},{8,10},{9,11},{10,... | collective-permute-start | bytes 350216 | tf_op jit(solution)/shard_map/ppermute | solution.py:54
  10.0 2.7 %collective-permute-done.1.refs_2_ = bf16[1,8,7296]{2,1,0:T(8,128)(2,1)S(1)} collective-permute-done((bf16[1,8,7296]{2,1,0:T(8,128)(2,1)}, bf16[1,8,7296]{2,1,0:T(8,128)(2,1)S(1)}, u32[]{:S(2)}, u32[]{:S(2)}) %collective-permute-start.1) | collective-permute-done | bytes 116768 | tf_op jit(solution)/shard_map/ppermute | solution.py:54
  17.7 2.2 %collective-permute-start.5 = (bf16[4,8,7296]{2,1,0:T(8,128)(2,1)S(1)}, bf16[4,8,7296]{2,1,0:T(8,128)(2,1)S(1)}, u32[]{:S(2)}, u32[]{:S(2)}) collective-permute-start(bf16[4,8,7296]{2,1,0:T(8,128)(2,1)S(1)} %join.2.refs_0_), channel_id=1, source_target_pairs={{0,48},{1,49},{2,50},{3,51},{4,52},{5,53},{6,54},{7,55},{8,56},{9,... | collective-permute-start | bytes 1400840 | tf_op jit(solution)/shard_map/ppermute | solution.py:54
  19.8 3.8 %collective-permute-done.3.refs_1_ = bf16[4,8,7296]{2,1,0:T(8,128)(2,1)S(1)} collective-permute-done((bf16[4,8,7296]{2,1,0:T(8,128)(2,1)S(1)}, bf16[4,8,7296]{2,1,0:T(8,128)(2,1)S(1)}, u32[]{:S(2)}, u32[]{:S(2)}) %collective-permute-start.3) | collective-permute-done | bytes 466976 | tf_op jit(solution)/shard_map/ppermute | solution.py:54
  23.7 3.1 %collective-permute-done.4.refs_2_ = bf16[4,8,7296]{2,1,0:T(8,128)(2,1)S(1)} collective-permute-done((bf16[4,8,7296]{2,1,0:T(8,128)(2,1)S(1)}, bf16[4,8,7296]{2,1,0:T(8,128)(2,1)S(1)}, u32[]{:S(2)}, u32[]{:S(2)}) %collective-permute-start.4) | collective-permute-done | bytes 466976 | tf_op jit(solution)/shard_map/ppermute | solution.py:54
  26.8 4.5 %collective-permute-done.5.refs_3_ = bf16[4,8,7296]{2,1,0:T(8,128)(2,1)S(1)} collective-permute-done((bf16[4,8,7296]{2,1,0:T(8,128)(2,1)S(1)}, bf16[4,8,7296]{2,1,0:T(8,128)(2,1)S(1)}, u32[]{:S(2)}, u32[]{:S(2)}) %collective-permute-start.5) | collective-permute-done | bytes 466976 | tf_op jit(solution)/shard_map/ppermute | solution.py:54
  36.6 2.9 %collective-permute-start.13 = (bf16[8,8,7296]{2,1,0:T(8,128)(2,1)S(1)}, bf16[8,8,7296]{2,1,0:T(8,128)(2,1)S(1)}, u32[]{:S(2)}, u32[]{:S(2)}) collective-permute-start(bf16[8,8,7296]{2,1,0:T(8,128)(2,1)S(1)} %get-tuple-element.37), channel_id=1, source_target_pairs={{0,12},{1,13},{2,14},{3,15},{4,0},{5,1},{6,2},{7,3},{8,4},{9,5},{1... | collective-permute-start | bytes 2801672 | tf_op jit(solution)/shard_map/ppermute | solution.py:54
  43.6 5.6 %expert_acts.3.acts_ref = bf16[128,512]{1,0:T(8,128)(2,1)S(1)} custom-call(s32[2]{0:T(128)S(1)} %pad_add_fusion.info_ref, bf16[64,7296]{1,0:T(8,128)(2,1)S(1)} %bitcast.21, bf16[64,7296]{1,0:T(8,128)(2,1)} %bitcast.5.refs_1_, bf16[7168,256]{1,0:T(8,128)(2,1)S(1)} %copy-done.2, bf16[7168,256]{1,0:T(8,128)(2,1)} %collective-permute-done.6.refs_3_.refs_5_, ...), custom_call_target="tpu_custom_call" | custom-call | flops 1879048192 | bytes 1048576 | tf_op jit(solution)/shard_map/expert_acts/pallas_call | solution.py:151
  51.3 5.7 %expert_acts.4.acts_ref = bf16[128,512]{1,0:T(8,128)(2,1)S(1)} custom-call(s32[2]{0:T(128)S(1)} %pad_add_fusion.info_ref, bf16[64,7296]{1,0:T(8,128)(2,1)S(1)} %bitcast.20, bf16[64,7296]{1,0:T(8,128)(2,1)} %bitcast.9.refs_1_, bf16[7168,256]{1,0:T(8,128)(2,1)S(1)} %copy-done.2, bf16[7168,256]{1,0:T(8,128)(2,1)} %collective-permute-done.6.refs_3_.refs_5_, ...), custom_call_target="tpu_custom_call" | custom-call | flops 1879048192 | bytes 1048576 | tf_op jit(solution)/shard_map/expert_acts/pallas_call | solution.py:151
  58.3 3.8 %expert_outs.6 = (bf16[64,7168]{1,0:T(8,128)(2,1)S(1)}, bf16[64,7168]{1,0:T(8,128)(2,1)S(1)}) custom-call(bf16[128,512]{1,0:T(8,128)(2,1)S(1)} %expert_acts.4.acts_ref, bf16[256,7168]{1,0:T(8,128)(2,1)S(1)} %copy-done.1, bf16[256,7168]{1,0:T(8,128)(2,1)} %collective-permute-done.14.other_ref), custom_call_target="tpu_custom_call" | custom-call | flops 939524096 | bytes 1048576 | tf_op jit(solution)/shard_map/expert_outs/pallas_call | solution.py:182
  62.1 6.2 %collective-permute-done.11 = bf16[8,8,7296]{2,1,0:T(8,128)(2,1)S(1)} collective-permute-done((bf16[8,8,7296]{2,1,0:T(8,128)(2,1)}, bf16[8,8,7296]{2,1,0:T(8,128)(2,1)S(1)}, u32[]{:S(2)}, u32[]{:S(2)}) %collective-permute-start.11) | collective-permute-done | bytes 933920 | tf_op jit(solution)/shard_map/ppermute | solution.py:54
  68.3 2.9 %collective-permute-start.15 = (bf16[64,7168]{1,0:T(8,128)(2,1)S(1)}, bf16[64,7168]{1,0:T(8,128)(2,1)S(1)}, u32[]{:S(2)}, u32[]{:S(2)}) collective-permute-start(bf16[64,7168]{1,0:T(8,128)(2,1)S(1)} %get-tuple-element.49), channel_id=1, source_target_pairs={{0,12},{1,13},{2,14},{3,15},{4,0},{5,1},{6,2},{7,3},{8,4},{9,5},{1... | collective-permute-start | bytes 2752520 | tf_op jit(solution)/shard_map/ppermute | solution.py:54
  71.2 7.2 %expert_acts.5 = bf16[256,512]{1,0:T(8,128)(2,1)S(1)} custom-call(s32[2]{0:T(128)S(1)} %pad_add_fusion.info_ref, bf16[64,7296]{1,0:T(8,128)(2,1)S(1)} %bitcast.25, bf16[64,7296]{1,0:T(8,128)(2,1)S(1)} %bitcast.24, bf16[64,7296]{1,0:T(8,128)(2,1)S(1)} %bitcast.22, bf16[64,7296]{1,0:T(8,128)(2,1)S(1)} %bitcast.23, bf16[7168,256]{1,0:T(8,128)(2,1)S(1)} %copy-done.3, ...), custom_call_target="tpu_custom_call" | custom-call | flops 3758096384 | bytes 1048576 | tf_op jit(solution)/shard_map/expert_acts/pallas_call | solution.py:151
  78.4 3.2 %expert_outs.4 = (bf16[64,7168]{1,0:T(8,128)(2,1)S(1)}, bf16[64,7168]{1,0:T(8,128)(2,1)S(1)}) custom-call(bf16[128,512]{1,0:T(8,128)(2,1)S(1)} %slice.31.acts_ref, bf16[256,7168]{1,0:T(8,128)(2,1)S(1)} %copy-done.1, bf16[256,7168]{1,0:T(8,128)(2,1)} %collective-permute-done.14.other_ref), custom_call_target="tpu_custom_call" | custom-call | flops 939524096 | bytes 1048576 | tf_op jit(solution)/shard_map/expert_outs/pallas_call | solution.py:182
  82.1 3.7 %collective-permute-start.19 = (bf16[64,7168]{1,0:T(8,128)(2,1)S(1)}, bf16[64,7168]{1,0:T(8,128)(2,1)S(1)}, u32[]{:S(2)}, u32[]{:S(2)}) collective-permute-start(bf16[64,7168]{1,0:T(8,128)(2,1)S(1)} %get-tuple-element.59), channel_id=1, source_target_pairs={{0,12},{1,13},{2,14},{3,15},{4,0},{5,1},{6,2},{7,3},{8,4},{9,5},{1... | collective-permute-start | bytes 2752520 | tf_op jit(solution)/shard_map/ppermute | solution.py:54
  85.8 3.2 %expert_outs.7 = (bf16[64,7168]{1,0:T(8,128)(2,1)S(1)}, bf16[64,7168]{1,0:T(8,128)(2,1)S(1)}) custom-call(bf16[128,512]{1,0:T(8,128)(2,1)S(1)} %slice.25.acts_ref, bf16[256,7168]{1,0:T(8,128)(2,1)S(1)} %copy-done.1, bf16[256,7168]{1,0:T(8,128)(2,1)} %collective-permute-done.14.other_ref), custom_call_target="tpu_custom_call" | custom-call | flops 939524096 | bytes 1048576 | tf_op jit(solution)/shard_map/expert_outs/pallas_call | solution.py:182
  89.0 3.2 %expert_outs.5 = (bf16[64,7168]{1,0:T(8,128)(2,1)S(1)}, bf16[64,7168]{1,0:T(8,128)(2,1)S(1)}) custom-call(bf16[128,512]{1,0:T(8,128)(2,1)S(1)} %expert_acts.3.acts_ref, bf16[256,7168]{1,0:T(8,128)(2,1)S(1)} %copy-done.1, bf16[256,7168]{1,0:T(8,128)(2,1)} %collective-permute-done.14.other_ref), custom_call_target="tpu_custom_call" | custom-call | flops 939524096 | bytes 1048576 | tf_op jit(solution)/shard_map/expert_outs/pallas_call | solution.py:182
  92.2 4.5 %collective-permute-done.19 = bf16[64,7168]{1,0:T(8,128)(2,1)S(1)} collective-permute-done((bf16[64,7168]{1,0:T(8,128)(2,1)S(1)}, bf16[64,7168]{1,0:T(8,128)(2,1)S(1)}, u32[]{:S(2)}, u32[]{:S(2)}) %collective-permute-start.19) | collective-permute-done | bytes 917536 | tf_op jit(solution)/shard_map/ppermute | solution.py:54
  96.7 3.7 %collective-permute-done.17 = bf16[64,7168]{1,0:T(8,128)(2,1)S(1)} collective-permute-done((bf16[64,7168]{1,0:T(8,128)(2,1)S(1)}, bf16[64,7168]{1,0:T(8,128)(2,1)S(1)}, u32[]{:S(2)}, u32[]{:S(2)}) %collective-permute-start.17) | collective-permute-done | bytes 917536 | tf_op jit(solution)/shard_map/ppermute | solution.py:54
  101.0 3.2 %collective-permute-start.20 = (bf16[64,7168]{1,0:T(8,128)(2,1)S(1)}, bf16[64,7168]{1,0:T(8,128)(2,1)S(1)}, u32[]{:S(2)}, u32[]{:S(2)}) collective-permute-start(bf16[64,7168]{1,0:T(8,128)(2,1)S(1)} %get-tuple-element.60), channel_id=1, source_target_pairs={{0,12},{1,13},{2,14},{3,15},{4,0},{5,1},{6,2},{7,3},{8,4},{9,5},{1... | collective-permute-start | bytes 2752520 | tf_op jit(solution)/shard_map/ppermute | solution.py:54
  104.2 11.4 %collective-permute-done.18 = bf16[64,7168]{1,0:T(8,128)(2,1)S(1)} collective-permute-done((bf16[64,7168]{1,0:T(8,128)(2,1)S(1)}, bf16[64,7168]{1,0:T(8,128)(2,1)S(1)}, u32[]{:S(2)}, u32[]{:S(2)}) %collective-permute-start.18) | collective-permute-done | bytes 917536 | tf_op jit(solution)/shard_map/ppermute | solution.py:54
  120.1 6.4 %collective-permute-done.23 = bf16[32,7168]{1,0:T(8,128)(2,1)S(1)} collective-permute-done((bf16[32,7168]{1,0:T(8,128)(2,1)S(1)}, bf16[32,7168]{1,0:T(8,128)(2,1)S(1)}, u32[]{:S(2)}, u32[]{:S(2)}) %collective-permute-start.23) | collective-permute-done | bytes 458784 | tf_op jit(solution)/shard_map/ppermute | solution.py:54
  126.5 4.4 %collective-permute-done.22 = bf16[32,7168]{1,0:T(8,128)(2,1)S(1)} collective-permute-done((bf16[32,7168]{1,0:T(8,128)(2,1)S(1)}, bf16[32,7168]{1,0:T(8,128)(2,1)S(1)}, u32[]{:S(2)}, u32[]{:S(2)}) %collective-permute-start.22) | collective-permute-done | bytes 458784 | tf_op jit(solution)/shard_map/ppermute | solution.py:54
  139.8 2.2 %fusion.11 = f32[8,576]{1,0:T(8,128)S(1)} fusion(bf16[7168,576]{0,1:T(8,128)(2,1)S(1)} %bitcast.31, bf16[8,7168]{1,0:T(8,128)(2,1)S(1)} %get-tuple-element.66, f32[7168]{0:T(1024)S(1)} %copy-done.10, f32[8]{0:T(128)S(1)} %add_rsqrt_fusion.1), kind=kOutput, calls=%fused_computation.21 | convolution fusion | flops 66289664 | bytes 8419360 | tf_op jit(solution)/shard_map/dot_general | solution.py:273
  (99 shorter events, 41.6 us)
Async XLA Ops:
  0.6 30.6 %collective-permute-start.6 = (bf16[7168,256]{1,0:T(8,128)(2,1)}, bf16[7168,256]{1,0:T(8,128)(2,1)}, u32[]{:S(2)}, u32[]{:S(2)}) collective-permute-start(bf16[7168,256]{1,0:T(8,128)(2,1)} %refs_4_.5), channel_id=1, source_target_pairs={{0,64},{1,65},{2,66},{3,67},{4,68},{5,69},{6,70},{7,71},{8,72},{9,... | collective-permute-start | bytes 11010056 | tf_op jit(solution)/shard_map/ppermute | solution.py:58
  0.7 30.5 %collective-permute-start.7 = (bf16[7168,256]{1,0:T(8,128)(2,1)}, bf16[7168,256]{1,0:T(8,128)(2,1)}, u32[]{:S(2)}, u32[]{:S(2)}) collective-permute-start(bf16[7168,256]{1,0:T(8,128)(2,1)} %refs_6_.1), channel_id=1, source_target_pairs={{0,64},{1,65},{2,66},{3,67},{4,68},{5,69},{6,70},{7,71},{8,72},{9,... | collective-permute-start | bytes 11010056 | tf_op jit(solution)/shard_map/ppermute | solution.py:58
  3.0 7.0 %collective-permute-start = (bf16[1,8,7296]{2,1,0:T(8,128)(2,1)}, bf16[1,8,7296]{2,1,0:T(8,128)(2,1)S(1)}, u32[]{:S(2)}, u32[]{:S(2)}) collective-permute-start(bf16[1,8,7296]{2,1,0:T(8,128)(2,1)} %bitcast.26), channel_id=1, source_target_pairs={{0,1},{1,2},{2,3},{3,0},{4,5},{5,6},{6,7},{7,4},{8,9},{9,10},{10,1... | collective-permute-start | bytes 350216 | tf_op jit(solution)/shard_map/ppermute | solution.py:54
  4.9 7.8 %collective-permute-start.1 = (bf16[1,8,7296]{2,1,0:T(8,128)(2,1)}, bf16[1,8,7296]{2,1,0:T(8,128)(2,1)S(1)}, u32[]{:S(2)}, u32[]{:S(2)}) collective-permute-start(bf16[1,8,7296]{2,1,0:T(8,128)(2,1)} %bitcast.27), channel_id=1, source_target_pairs={{0,2},{1,3},{2,0},{3,1},{4,6},{5,7},{6,4},{7,5},{8,10},{9,11},{10,... | collective-permute-start | bytes 350216 | tf_op jit(solution)/shard_map/ppermute | solution.py:54
  15.0 8.6 %collective-permute-start.3 = (bf16[4,8,7296]{2,1,0:T(8,128)(2,1)S(1)}, bf16[4,8,7296]{2,1,0:T(8,128)(2,1)S(1)}, u32[]{:S(2)}, u32[]{:S(2)}) collective-permute-start(bf16[4,8,7296]{2,1,0:T(8,128)(2,1)S(1)} %join.2.refs_0_), channel_id=1, source_target_pairs={{0,16},{1,17},{2,18},{3,19},{4,20},{5,21},{6,22},{7,23},{8,24},{9,... | collective-permute-start | bytes 1400840 | tf_op jit(solution)/shard_map/ppermute | solution.py:54
  16.6 10.2 %collective-permute-start.4 = (bf16[4,8,7296]{2,1,0:T(8,128)(2,1)S(1)}, bf16[4,8,7296]{2,1,0:T(8,128)(2,1)S(1)}, u32[]{:S(2)}, u32[]{:S(2)}) collective-permute-start(bf16[4,8,7296]{2,1,0:T(8,128)(2,1)S(1)} %join.2.refs_0_), channel_id=1, source_target_pairs={{0,32},{1,33},{2,34},{3,35},{4,36},{5,37},{6,38},{7,39},{8,40},{9,... | collective-permute-start | bytes 1400840 | tf_op jit(solution)/shard_map/ppermute | solution.py:54
  17.7 13.6 %collective-permute-start.5 = (bf16[4,8,7296]{2,1,0:T(8,128)(2,1)S(1)}, bf16[4,8,7296]{2,1,0:T(8,128)(2,1)S(1)}, u32[]{:S(2)}, u32[]{:S(2)}) collective-permute-start(bf16[4,8,7296]{2,1,0:T(8,128)(2,1)S(1)} %join.2.refs_0_), channel_id=1, source_target_pairs={{0,48},{1,49},{2,50},{3,51},{4,52},{5,53},{6,54},{7,55},{8,56},{9,... | collective-permute-start | bytes 1400840 | tf_op jit(solution)/shard_map/ppermute | solution.py:54
  32.8 25.5 %collective-permute-start.14 = (bf16[256,7168]{1,0:T(8,128)(2,1)}, bf16[256,7168]{1,0:T(8,128)(2,1)}, u32[]{:S(2)}, u32[]{:S(2)}) collective-permute-start(bf16[256,7168]{1,0:T(8,128)(2,1)} %mine_ref.7), channel_id=1, source_target_pairs={{0,64},{1,65},{2,66},{3,67},{4,68},{5,69},{6,70},{7,71},{8,72},{9,... | collective-permute-start | bytes 11010056 | tf_op jit(solution)/shard_map/ppermute | solution.py:58
  32.9 16.3 %collective-permute-start.8 = (bf16[8,8,7296]{2,1,0:T(8,128)(2,1)S(1)}, bf16[8,8,7296]{2,1,0:T(8,128)(2,1)S(1)}, u32[]{:S(2)}, u32[]{:S(2)}) collective-permute-start(bf16[8,8,7296]{2,1,0:T(8,128)(2,1)S(1)} %get-tuple-element.37), channel_id=1, source_target_pairs={{0,4},{1,5},{2,6},{3,7},{4,8},{5,9},{6,10},{7,11},{8,12},{9,13},{1... | collective-permute-start | bytes 2801672 | tf_op jit(solution)/shard_map/ppermute | solution.py:54
  34.5 14.7 %collective-permute-start.9 = (bf16[8,8,7296]{2,1,0:T(8,128)(2,1)}, bf16[8,8,7296]{2,1,0:T(8,128)(2,1)}, u32[]{:S(2)}, u32[]{:S(2)}) collective-permute-start(bf16[8,8,7296]{2,1,0:T(8,128)(2,1)} %get-tuple-element.38), channel_id=1, source_target_pairs={{0,12},{1,13},{2,14},{3,15},{4,0},{5,1},{6,2},{7,3},{8,4},{9,5},{1... | collective-permute-start | bytes 2801672 | tf_op jit(solution)/shard_map/ppermute | solution.py:54
  36.3 21.5 %collective-permute-start.12 = (bf16[8,8,7296]{2,1,0:T(8,128)(2,1)}, bf16[8,8,7296]{2,1,0:T(8,128)(2,1)S(1)}, u32[]{:S(2)}, u32[]{:S(2)}) collective-permute-start(bf16[8,8,7296]{2,1,0:T(8,128)(2,1)} %get-tuple-element.38), channel_id=1, source_target_pairs={{0,4},{1,5},{2,6},{3,7},{4,8},{5,9},{6,10},{7,11},{8,12},{9,13},{1... | collective-permute-start | bytes 2801672 | tf_op jit(solution)/shard_map/ppermute | solution.py:54
  36.6 21.7 %collective-permute-start.13 = (bf16[8,8,7296]{2,1,0:T(8,128)(2,1)S(1)}, bf16[8,8,7296]{2,1,0:T(8,128)(2,1)S(1)}, u32[]{:S(2)}, u32[]{:S(2)}) collective-permute-start(bf16[8,8,7296]{2,1,0:T(8,128)(2,1)S(1)} %get-tuple-element.37), channel_id=1, source_target_pairs={{0,12},{1,13},{2,14},{3,15},{4,0},{5,1},{6,2},{7,3},{8,4},{9,5},{1... | collective-permute-start | bytes 2801672 | tf_op jit(solution)/shard_map/ppermute | solution.py:54
  49.2 19.1 %collective-permute-start.11 = (bf16[8,8,7296]{2,1,0:T(8,128)(2,1)}, bf16[8,8,7296]{2,1,0:T(8,128)(2,1)S(1)}, u32[]{:S(2)}, u32[]{:S(2)}) collective-permute-start(bf16[8,8,7296]{2,1,0:T(8,128)(2,1)} %collective-permute-done.9), channel_id=1, source_target_pairs={{0,12},{1,13},{2,14},{3,15},{4,0},{5,1},{6,2},{7,3},{8,4},{9,5},{1... | collective-permute-start | bytes 2801672 | tf_op jit(solution)/shard_map/ppermute | solution.py:54
  51.3 19.9 %collective-permute-start.10 = (bf16[8,8,7296]{2,1,0:T(8,128)(2,1)S(1)}, bf16[8,8,7296]{2,1,0:T(8,128)(2,1)S(1)}, u32[]{:S(2)}, u32[]{:S(2)}) collective-permute-start(bf16[8,8,7296]{2,1,0:T(8,128)(2,1)S(1)} %collective-permute-done.8), channel_id=1, source_target_pairs={{0,4},{1,5},{2,6},{3,7},{4,8},{5,9},{6,10},{7,11},{8,12},{9,13},{1... | collective-permute-start | bytes 2801672 | tf_op jit(solution)/shard_map/ppermute | solution.py:54
  68.3 13.8 %collective-permute-start.15 = (bf16[64,7168]{1,0:T(8,128)(2,1)S(1)}, bf16[64,7168]{1,0:T(8,128)(2,1)S(1)}, u32[]{:S(2)}, u32[]{:S(2)}) collective-permute-start(bf16[64,7168]{1,0:T(8,128)(2,1)S(1)} %get-tuple-element.49), channel_id=1, source_target_pairs={{0,12},{1,13},{2,14},{3,15},{4,0},{5,1},{6,2},{7,3},{8,4},{9,5},{1... | collective-permute-start | bytes 2752520 | tf_op jit(solution)/shard_map/ppermute | solution.py:54
  71.2 14.6 %collective-permute-start.16 = (bf16[64,7168]{1,0:T(8,128)(2,1)S(1)}, bf16[64,7168]{1,0:T(8,128)(2,1)S(1)}, u32[]{:S(2)}, u32[]{:S(2)}) collective-permute-start(bf16[64,7168]{1,0:T(8,128)(2,1)S(1)} %get-tuple-element.53), channel_id=1, source_target_pairs={{0,4},{1,5},{2,6},{3,7},{4,8},{5,9},{6,10},{7,11},{8,12},{9,13},{1... | collective-permute-start | bytes 2752520 | tf_op jit(solution)/shard_map/ppermute | solution.py:54
  82.1 14.6 %collective-permute-start.19 = (bf16[64,7168]{1,0:T(8,128)(2,1)S(1)}, bf16[64,7168]{1,0:T(8,128)(2,1)S(1)}, u32[]{:S(2)}, u32[]{:S(2)}) collective-permute-start(bf16[64,7168]{1,0:T(8,128)(2,1)S(1)} %get-tuple-element.59), channel_id=1, source_target_pairs={{0,12},{1,13},{2,14},{3,15},{4,0},{5,1},{6,2},{7,3},{8,4},{9,5},{1... | collective-permute-start | bytes 2752520 | tf_op jit(solution)/shard_map/ppermute | solution.py:54
  85.8 14.6 %collective-permute-start.17 = (bf16[64,7168]{1,0:T(8,128)(2,1)S(1)}, bf16[64,7168]{1,0:T(8,128)(2,1)S(1)}, u32[]{:S(2)}, u32[]{:S(2)}) collective-permute-start(bf16[64,7168]{1,0:T(8,128)(2,1)S(1)} %get-tuple-element.54), channel_id=1, source_target_pairs={{0,4},{1,5},{2,6},{3,7},{4,8},{5,9},{6,10},{7,11},{8,12},{9,13},{1... | collective-permute-start | bytes 2752520 | tf_op jit(solution)/shard_map/ppermute | solution.py:54
  100.9 14.7 %collective-permute-start.18 = (bf16[64,7168]{1,0:T(8,128)(2,1)S(1)}, bf16[64,7168]{1,0:T(8,128)(2,1)S(1)}, u32[]{:S(2)}, u32[]{:S(2)}) collective-permute-start(bf16[64,7168]{1,0:T(8,128)(2,1)S(1)} %get-tuple-element.55), channel_id=1, source_target_pairs={{0,4},{1,5},{2,6},{3,7},{4,8},{5,9},{6,10},{7,11},{8,12},{9,13},{1... | collective-permute-start | bytes 2752520 | tf_op jit(solution)/shard_map/ppermute | solution.py:54
  101.0 14.9 %collective-permute-start.20 = (bf16[64,7168]{1,0:T(8,128)(2,1)S(1)}, bf16[64,7168]{1,0:T(8,128)(2,1)S(1)}, u32[]{:S(2)}, u32[]{:S(2)}) collective-permute-start(bf16[64,7168]{1,0:T(8,128)(2,1)S(1)} %get-tuple-element.60), channel_id=1, source_target_pairs={{0,12},{1,13},{2,14},{3,15},{4,0},{5,1},{6,2},{7,3},{8,4},{9,5},{1... | collective-permute-start | bytes 2752520 | tf_op jit(solution)/shard_map/ppermute | solution.py:54
  116.4 10.2 %collective-permute-start.23 = (bf16[32,7168]{1,0:T(8,128)(2,1)S(1)}, bf16[32,7168]{1,0:T(8,128)(2,1)S(1)}, u32[]{:S(2)}, u32[]{:S(2)}) collective-permute-start(bf16[32,7168]{1,0:T(8,128)(2,1)S(1)} %get-tuple-element.68), channel_id=1, source_target_pairs={{0,32},{1,33},{2,34},{3,35},{4,36},{5,37},{6,38},{7,39},{8,40},{9,... | collective-permute-start | bytes 1376264 | tf_op jit(solution)/shard_map/ppermute | solution.py:54
  117.9 13.0 %collective-permute-start.22 = (bf16[32,7168]{1,0:T(8,128)(2,1)S(1)}, bf16[32,7168]{1,0:T(8,128)(2,1)S(1)}, u32[]{:S(2)}, u32[]{:S(2)}) collective-permute-start(bf16[32,7168]{1,0:T(8,128)(2,1)S(1)} %get-tuple-element.67), channel_id=1, source_target_pairs={{0,16},{1,17},{2,18},{3,19},{4,20},{5,21},{6,22},{7,23},{8,24},{9,... | collective-permute-start | bytes 1376264 | tf_op jit(solution)/shard_map/ppermute | solution.py:54
  118.1 13.3 %collective-permute-start.21 = (bf16[32,7168]{1,0:T(8,128)(2,1)S(1)}, bf16[32,7168]{1,0:T(8,128)(2,1)S(1)}, u32[]{:S(2)}, u32[]{:S(2)}) collective-permute-start(bf16[32,7168]{1,0:T(8,128)(2,1)S(1)} %split.25), channel_id=1, source_target_pairs={{0,48},{1,49},{2,50},{3,51},{4,52},{5,53},{6,54},{7,55},{8,56},{9,... | collective-permute-start | bytes 1376264 | tf_op jit(solution)/shard_map/ppermute | solution.py:54
  131.6 6.4 %collective-permute-start.26 = (bf16[8,7168]{1,0:T(8,128)(2,1)S(1)}, bf16[8,7168]{1,0:T(8,128)(2,1)S(1)}, u32[]{:S(2)}, u32[]{:S(2)}) collective-permute-start(bf16[8,7168]{1,0:T(8,128)(2,1)S(1)} %get-tuple-element.70), channel_id=1, source_target_pairs={{0,2},{1,3},{2,0},{3,1},{4,6},{5,7},{6,4},{7,5},{8,10},{9,11},{10,... | collective-permute-start | bytes 344072 | tf_op jit(solution)/shard_map/ppermute | solution.py:54
  (18 other events, 277.1 us)
